TPU v7x, 32 devices: a whole 2x2x4 slice. The times are simulated.
32 devices in a mesh: section: 2 (over core), dp: 4 (over z), seq: 4 (over y, x).
Axes of the slice: x: 2, y: 2, z: 4, core: 2. Of those that a mesh axis runs over, the one named last changes fastest.
Arguments:
- patches: bfloat16 [8, 96, 12, 768], P('dp', 'seq'), may hold values from -6 to 6
- queries: bfloat16 [8, 128, 768], P('dp'), may hold values from -6 to 6
- page_rows: int32 [8], P('dp'), may hold values from 1 to 8, as said below
- window_mask: int32 [8, 8, 1], P('dp', 'seq'), may hold values from 0 to 1, as said below
- query_lengths: int32 [8], P('dp'), may hold values from 1 to 128, as said below
- plan: int32 [4, 2], P('dp'), may hold values from 0 to 1, each once within a row
- norm_attn: bfloat16 [2, 768], P('section', ('dp', 'seq')), may hold values from 0.099609375 to 1.8984375
- norm_mlp: bfloat16 [2, 768], P('section', ('dp', 'seq')), may hold values from 0.099609375 to 1.8984375
- norm_query: bfloat16 [2, 768], P('section', ('dp', 'seq')), may hold values from 0.099609375 to 1.8984375
- attn_input: bfloat16 [2, 768, 2304], P('section', ('dp', 'seq')), may hold values from -0.21875 to 0.21875
- attn_output: bfloat16 [2, 768, 768], P('section', ('dp', 'seq')), may hold values from -1.5 to 1.5
- mlp_up: bfloat16 [2, 768, 3072], P('section', ('dp', 'seq')), may hold values from -0.21875 to 0.21875
- mlp_down: bfloat16 [2, 3072, 768], P('section', ('dp', 'seq')), may hold values from -0.109375 to 0.109375
- cross_query: bfloat16 [2, 768, 768], P('section', ('dp', 'seq')), may hold values from -0.21875 to 0.21875
- cross_pair: bfloat16 [2, 768, 1536], P('section', ('dp', 'seq')), may hold values from -0.21875 to 0.21875
- cross_output: bfloat16 [2, 768, 768], P('section', ('dp', 'seq')), may hold values from -4 to 4
- patch_cotangent: bfloat16 [8, 96, 12, 768], P('dp', 'seq'), may hold values from -6 to 6
- query_cotangent: bfloat16 [8, 128, 768], P('dp'), may hold values from -6 to 6
Outputs:
- patch_ends: bfloat16 [2, 8, 96, 12, 768], P('section', 'dp', 'seq')
- query_ends: bfloat16 [2, 8, 128, 768], P('section', 'dp')
- grad_norm_attn: float32 [2, 768], P('section', ('dp', 'seq'))
- grad_norm_mlp: float32 [2, 768], P('section', ('dp', 'seq'))
- grad_norm_query: float32 [2, 768], P('section', ('dp', 'seq'))
- grad_attn_input: float32 [2, 768, 2304], P('section', ('dp', 'seq'))
- grad_attn_output: float32 [2, 768, 768], P('section', ('dp', 'seq'))
- grad_mlp_up: float32 [2, 768, 3072], P('section', ('dp', 'seq'))
- grad_mlp_down: float32 [2, 3072, 768], P('section', ('dp', 'seq'))
- grad_cross_query: float32 [2, 768, 768], P('section', ('dp', 'seq'))
- grad_cross_pair: float32 [2, 768, 1536], P('section', ('dp', 'seq'))
- grad_cross_output: float32 [2, 768, 768], P('section', ('dp', 'seq'))
Inputs may be any that keep to these rules, and one draw needn't show every extreme that they name: `page_rows`: among the 2 pages of each dp index one holds content in all 8 window rows. `window_mask`: window 0 of window row 0 of every page is 1. `query_lengths`: among the 2 query sets of each dp index one has all 128 tokens live. `plan`: each row is a permutation of the numbers below 2.
All inputs are finite; a program needn't handle non-finite values.
Results may differ from a plain program's by a relative error of at most 0.025.
Values may be sent and summed in bfloat16 or wider, within the bound.
No kernel may reach another device: no remote copies, remote signals or barrier semaphores. Data moves between devices by JAX's collectives and lax.ppermute only.
A program may use at most 320 MiB of HBM per device.

v0:
```python
from functools import partial
import math

import jax
import jax.numpy as jnp
from jax import lax
from jax.sharding import PartitionSpec as P

D = 768
HEADS = 12
HDIM = 64
WIN = 12
NQ = 128


epsilon = 1e-05
hidden_value = -1e30


def merged(array, axis, combine):
    everything = jax.tree.map(lambda part: lax.all_gather(part, axis), array)
    first = jax.tree.map(lambda part: part[0], everything)

    def lap(k, so_far):
        return combine(so_far, jax.tree.map(lambda part: part[k], everything))

    return lax.fori_loop(1, lax.axis_size(axis), lap, first)


def padded(cells, sides, width):
    for axis, dim in sides:
        count = lax.axis_size(axis)
        ends = count - 1
        head = lax.slice_in_dim(cells, 0, width, axis=dim)
        tail = lax.slice_in_dim(cells, cells.shape[dim] - width, cells.shape[dim], axis=dim)
        cells = jnp.concatenate(
            [
                lax.ppermute(tail, axis, [(i, (i + 1) % count) for i in range(ends)]),
                cells,
                lax.ppermute(head, axis, [((i + 1) % count, i) for i in range(ends)]),
            ],
            axis=dim,
        )
    return cells


def shifted(array, axis, by):
    length = lax.axis_size(axis)
    pairs = [(i, i + by) for i in range(length) if 0 <= i + by < length]
    return lax.ppermute(array, axis, pairs)


def layer_norm(values, gain):
    center = values - jnp.mean(values, axis=-1, keepdims=True)
    spread = jnp.mean(center * center, axis=-1, keepdims=True)
    return center * lax.rsqrt(spread + epsilon) * gain


def heads_view(values):
    return values.reshape(values.shape[:-1] + (HEADS, HDIM))


def outer_product(left_side, right_side):
    return lax.dot_general(
        left_side, right_side, (((0,), (0,)), ((), ())), preferred_element_type=jnp.float32
    )


def times_transpose(left_side, right_side):
    return lax.dot_general(
        left_side, right_side, (((1,), (1,)), ((), ())), preferred_element_type=jnp.float32
    )


def to_windows(grid_view):
    row_count, col_count, features = grid_view.shape
    blocks = grid_view.reshape(row_count // WIN, WIN, col_count // WIN, WIN, features)
    return blocks.transpose(0, 2, 1, 3, 4).reshape(-1, WIN * WIN, features)


def from_windows(blocks, row_count, col_count):
    features = blocks.shape[-1]
    grid_view = blocks.reshape(row_count // WIN, col_count // WIN, WIN, WIN, features)
    return grid_view.transpose(0, 2, 1, 3, 4).reshape(row_count, col_count, features)


def window_probs(packed, present):
    scaling = 1.0 / math.sqrt(HDIM)
    query_heads = heads_view(packed[..., :D])
    key_heads = heads_view(packed[..., D : 2 * D])
    scores = (
        jnp.einsum("nqhe,nkhe->nhqk", query_heads, key_heads, preferred_element_type=jnp.float32)
        * scaling
    )
    scores = jnp.where(present[:, None, None, :], scores, hidden_value)
    return jax.nn.softmax(scores, axis=-1)


def window_forward(packed, present):
    softmaxed = window_probs(packed, present)
    value_heads = heads_view(packed[..., 2 * D :])
    mixed_out = jnp.einsum(
        "nhqk,nkhe->nqhe",
        softmaxed.astype(jnp.bfloat16),
        value_heads,
        preferred_element_type=jnp.float32,
    )
    return mixed_out.reshape(packed.shape[0], packed.shape[1], D).astype(jnp.bfloat16)


def window_backward(packed, present, grad_out):
    scaling = 1.0 / math.sqrt(HDIM)
    softmaxed = window_probs(packed, present)
    query_heads = heads_view(packed[..., :D])
    key_heads = heads_view(packed[..., D : 2 * D])
    value_heads = heads_view(packed[..., 2 * D :])
    grad_heads = heads_view(grad_out)
    grad_probs = jnp.einsum(
        "nqhe,nkhe->nhqk", grad_heads, value_heads, preferred_element_type=jnp.float32
    )
    inner_sum = jnp.sum(softmaxed * grad_probs, axis=-1, keepdims=True)
    grad_scores = (softmaxed * (grad_probs - inner_sum)).astype(jnp.bfloat16)
    grad_query = (
        jnp.einsum("nhqk,nkhe->nqhe", grad_scores, key_heads, preferred_element_type=jnp.float32)
        * scaling
    )
    grad_key = (
        jnp.einsum("nhqk,nqhe->nkhe", grad_scores, query_heads, preferred_element_type=jnp.float32)
        * scaling
    )
    grad_value = jnp.einsum(
        "nhqk,nqhe->nkhe",
        softmaxed.astype(jnp.bfloat16),
        grad_heads,
        preferred_element_type=jnp.float32,
    )
    win_shape = (packed.shape[0], packed.shape[1], D)
    return jnp.concatenate(
        [grad_query.reshape(win_shape), grad_key.reshape(win_shape), grad_value.reshape(win_shape)],
        axis=-1,
    )


def plain_forward(packed, framed, presence):
    row_count, col_count = (packed.shape[0], packed.shape[1])
    present = jnp.ones((row_count * col_count // (WIN * WIN), WIN * WIN), dtype=bool)
    return from_windows(window_forward(to_windows(packed), present), row_count, col_count)


def shifted_forward(packed, framed, presence):
    row_count, col_count = (packed.shape[0], packed.shape[1])
    half_win = WIN // 2
    widened = jnp.pad(framed, ((0, 0), (half_win, half_win), (0, 0)))
    present = to_windows(presence[..., None])[..., 0]
    mixed_out = from_windows(
        window_forward(to_windows(widened), present), row_count + WIN, col_count + WIN
    )
    return mixed_out[half_win : half_win + row_count, half_win : half_win + col_count]


def plain_backward(packed, framed, presence, grad_mixed):
    row_count, col_count = (packed.shape[0], packed.shape[1])
    present = jnp.ones((row_count * col_count // (WIN * WIN), WIN * WIN), dtype=bool)
    blocks = window_backward(to_windows(packed), present, to_windows(grad_mixed))
    return (
        from_windows(blocks, row_count, col_count),
        jnp.zeros((WIN, col_count, 3 * D), jnp.float32),
    )


def shifted_backward(packed, framed, presence, grad_mixed):
    row_count, col_count = (packed.shape[0], packed.shape[1])
    half_win = WIN // 2
    widened = jnp.pad(framed, ((0, 0), (half_win, half_win), (0, 0)))
    grad_wide = jnp.pad(grad_mixed, ((half_win, half_win), (half_win, half_win), (0, 0)))
    present = to_windows(presence[..., None])[..., 0]
    blocks = window_backward(to_windows(widened), present, to_windows(grad_wide))
    grid_view = from_windows(blocks, row_count + WIN, col_count + WIN)[
        :, half_win : half_win + col_count
    ]
    own_grad = grid_view[half_win : half_win + row_count]
    rim_grads = jnp.concatenate([grid_view[:half_win], grid_view[half_win + row_count :]], axis=0)
    return (own_grad, rim_grads)


def combine_stats(first_pair, second_pair):
    peak_score = jnp.maximum(first_pair[0], second_pair[0])
    denom_sum = first_pair[1] * jnp.exp(first_pair[0] - peak_score) + second_pair[1] * jnp.exp(
        second_pair[0] - peak_score
    )
    return (peak_score, denom_sum)


def cross_probs(query_proj, pair_proj, key_valid):
    scaling = 1.0 / math.sqrt(HDIM)
    scores = (
        jnp.einsum(
            "qhe,khe->hqk",
            heads_view(query_proj),
            heads_view(pair_proj[:, :D]),
            preferred_element_type=jnp.float32,
        )
        * scaling
    )
    scores = jnp.where(key_valid[None, None, :], scores, hidden_value)
    peak_score = jnp.max(scores, axis=-1)
    denom_sum = jnp.sum(
        jnp.where(key_valid[None, None, :], jnp.exp(scores - peak_score[..., None]), 0.0), axis=-1
    )
    peak_score, denom_sum = merged((peak_score, denom_sum), "seq", combine_stats)
    weighted = jnp.where(key_valid[None, None, :], jnp.exp(scores - peak_score[..., None]), 0.0)
    return weighted / denom_sum[..., None]


def layer_forward(weights, patch_in, query_in, key_valid, query_live, section_id, presence):
    gain_attn, gain_mlp, gain_query, w_input, w_output, w_up, w_down, w_query, w_pair, w_cross = (
        weights
    )
    row_count, col_count = (patch_in.shape[0], patch_in.shape[1])
    flat_patch = patch_in.reshape(row_count * col_count, D).astype(jnp.float32)
    normed = layer_norm(flat_patch, gain_attn.astype(jnp.float32)).astype(jnp.bfloat16)
    packed = jnp.dot(normed, w_input, preferred_element_type=jnp.float32).astype(jnp.bfloat16)
    packed = packed.reshape(row_count, col_count, 3 * D)
    framed = padded(packed, (("seq", 0),), WIN // 2)
    mixed_out = lax.cond(section_id == 0, plain_forward, shifted_forward, packed, framed, presence)
    mixed_out = mixed_out.reshape(row_count * col_count, D)
    first_sum = flat_patch + jnp.dot(mixed_out, w_output, preferred_element_type=jnp.float32)
    normed_mlp = layer_norm(first_sum, gain_mlp.astype(jnp.float32)).astype(jnp.bfloat16)
    lifted = jnp.dot(normed_mlp, w_up, preferred_element_type=jnp.float32)
    active = jax.nn.gelu(lifted, approximate=False).astype(jnp.bfloat16)
    second_sum = first_sum + jnp.dot(active, w_down, preferred_element_type=jnp.float32)
    query_flat = query_in.astype(jnp.float32)
    normed_query = layer_norm(query_flat, gain_query.astype(jnp.float32)).astype(jnp.bfloat16)
    query_proj = jnp.dot(normed_query, w_query, preferred_element_type=jnp.float32).astype(
        jnp.bfloat16
    )
    pair_proj = jnp.dot(normed_mlp, w_pair, preferred_element_type=jnp.float32).astype(jnp.bfloat16)
    softmaxed = cross_probs(query_proj, pair_proj, key_valid)
    partial_sum = jnp.einsum(
        "hqk,khe->qhe",
        softmaxed.astype(jnp.bfloat16),
        heads_view(pair_proj[:, D:]),
        preferred_element_type=jnp.float32,
    ).reshape(-1, D)
    attended = lax.psum(partial_sum.astype(jnp.bfloat16), "seq")
    query_out = query_flat + query_live[:, None] * jnp.dot(
        attended, w_cross, preferred_element_type=jnp.float32
    )
    kept = (
        patch_in,
        normed,
        packed,
        framed,
        mixed_out,
        first_sum,
        normed_mlp,
        lifted,
        active,
        normed_query,
        query_proj,
        pair_proj,
        softmaxed,
        attended,
        key_valid,
        query_live,
        query_in,
    )
    return (
        second_sum.reshape(row_count, col_count, D).astype(jnp.bfloat16),
        query_out.astype(jnp.bfloat16),
        kept,
    )


def layer_backward(weights, kept, grad_patch, grad_query, section_id, presence):
    gain_attn, gain_mlp, gain_query, w_input, w_output, w_up, w_down, w_query, w_pair, w_cross = (
        weights
    )
    (
        patch_in,
        normed,
        packed,
        framed,
        mixed_out,
        first_sum,
        normed_mlp,
        lifted,
        active,
        normed_query,
        query_proj,
        pair_proj,
        softmaxed,
        attended,
        key_valid,
        query_live,
        query_in,
    ) = kept
    scaling = 1.0 / math.sqrt(HDIM)
    half_win = WIN // 2
    row_count, col_count = (patch_in.shape[0], patch_in.shape[1])
    grad_second = grad_patch.reshape(row_count * col_count, D)
    grad_cross = (query_live[:, None] * grad_query.astype(jnp.float32)).astype(jnp.bfloat16)
    grad_att = times_transpose(grad_cross, w_cross).astype(jnp.bfloat16)
    grad_heads = heads_view(grad_att)
    grad_probs = jnp.einsum(
        "qhe,khe->hqk", grad_heads, heads_view(pair_proj[:, D:]), preferred_element_type=jnp.float32
    )
    inner_sum = lax.psum(jnp.sum(softmaxed * grad_probs, axis=-1), "seq")
    grad_scores = (softmaxed * (grad_probs - inner_sum[..., None])).astype(jnp.bfloat16)
    query_part = (
        jnp.einsum(
            "hqk,khe->qhe",
            grad_scores,
            heads_view(pair_proj[:, :D]),
            preferred_element_type=jnp.float32,
        ).reshape(-1, D)
        * scaling
    )
    grad_proj = lax.psum(query_part.astype(jnp.bfloat16), "seq")
    grad_key = (
        jnp.einsum(
            "hqk,qhe->khe", grad_scores, heads_view(query_proj), preferred_element_type=jnp.float32
        ).reshape(-1, D)
        * scaling
    )
    grad_value = jnp.einsum(
        "hqk,qhe->khe",
        softmaxed.astype(jnp.bfloat16),
        grad_heads,
        preferred_element_type=jnp.float32,
    ).reshape(-1, D)
    grad_pair = jnp.concatenate([grad_key, grad_value], axis=-1).astype(jnp.bfloat16)
    grad_nq = times_transpose(grad_proj, w_query)
    _, query_norm_back = jax.vjp(
        layer_norm, query_in.astype(jnp.float32), gain_query.astype(jnp.float32)
    )
    grad_q_norm, d_gain_query = query_norm_back(grad_nq)
    query_grad = grad_query.astype(jnp.float32) + grad_q_norm
    grad_active = times_transpose(grad_second, w_down)
    _, gelu_back = jax.vjp(partial(jax.nn.gelu, approximate=False), lifted)
    grad_lifted = gelu_back(grad_active)[0].astype(jnp.bfloat16)
    grad_nm = times_transpose(grad_lifted, w_up) + times_transpose(grad_pair, w_pair)
    _, mlp_norm_back = jax.vjp(layer_norm, first_sum, gain_mlp.astype(jnp.float32))
    grad_first_norm, d_gain_mlp = mlp_norm_back(grad_nm)
    grad_first = grad_second.astype(jnp.float32) + grad_first_norm
    grad_first_low = grad_first.astype(jnp.bfloat16)
    grad_mixed = (
        times_transpose(grad_first_low, w_output)
        .astype(jnp.bfloat16)
        .reshape(row_count, col_count, D)
    )
    own_grad, rim_grads = lax.cond(
        section_id == 0, plain_backward, shifted_backward, packed, framed, presence, grad_mixed
    )
    rim_wide = padded(rim_grads.astype(jnp.bfloat16), (("seq", 0),), WIN // 2).astype(
        rim_grads.dtype
    )
    own_grad = own_grad.at[:half_win].add(rim_wide[:half_win])
    own_grad = own_grad.at[row_count - half_win :].add(rim_wide[WIN + half_win :])
    grad_packed = own_grad.astype(jnp.bfloat16).reshape(row_count * col_count, 3 * D)
    grad_normed = times_transpose(grad_packed, w_input)
    flat_patch = patch_in.reshape(row_count * col_count, D).astype(jnp.float32)
    _, attn_norm_back = jax.vjp(layer_norm, flat_patch, gain_attn.astype(jnp.float32))
    grad_x_norm, d_gain_attn = attn_norm_back(grad_normed)
    patch_grad = (grad_first + grad_x_norm).reshape(row_count, col_count, D)
    gain_grads = (d_gain_attn, d_gain_mlp, d_gain_query)
    matrix_pairs = (
        (normed, grad_packed),
        (mixed_out, grad_first_low),
        (normed_mlp, grad_lifted),
        (active, grad_second),
        (normed_query, grad_proj),
        (normed_mlp, grad_pair),
        (attended, grad_cross),
    )
    return (
        patch_grad.astype(jnp.bfloat16),
        query_grad.astype(jnp.bfloat16),
        gain_grads,
        matrix_pairs,
    )


def per_device(
    patches,
    queries,
    page_rows,
    window_mask,
    query_lengths,
    plan,
    norm_attn,
    norm_mlp,
    norm_query,
    attn_input,
    attn_output,
    mlp_up,
    mlp_down,
    cross_query,
    cross_pair,
    cross_output,
    patch_cotangent,
    query_cotangent,
):
    section_id = lax.axis_index("section")
    seq_id = lax.axis_index("seq")
    seq_count = lax.axis_size("seq")
    first_section = section_id == 0
    fetched = (
        lax.all_gather(norm_attn, ("dp", "seq"), axis=1, tiled=True),
        lax.all_gather(norm_mlp, ("dp", "seq"), axis=1, tiled=True),
        lax.all_gather(norm_query, ("dp", "seq"), axis=1, tiled=True),
        lax.all_gather(attn_input, ("dp", "seq"), axis=1, tiled=True),
        lax.all_gather(attn_output, ("dp", "seq"), axis=1, tiled=True),
        lax.all_gather(mlp_up, ("dp", "seq"), axis=1, tiled=True),
        lax.all_gather(mlp_down, ("dp", "seq"), axis=1, tiled=True),
        lax.all_gather(cross_query, ("dp", "seq"), axis=1, tiled=True),
        lax.all_gather(cross_pair, ("dp", "seq"), axis=1, tiled=True),
        lax.all_gather(cross_output, ("dp", "seq"), axis=1, tiled=True),
    )
    weights = tuple((fetched_one[0] for fetched_one in fetched))
    batches = patches.shape[0]
    row_count, col_count = (patches.shape[1], patches.shape[2])
    half_win = WIN // 2
    page_order = plan[0]
    frame_rows = seq_id * row_count + jnp.arange(row_count + WIN) - half_win
    row_inside = (frame_rows >= 0) & (frame_rows < row_count * seq_count)
    frame_cols = jnp.arange(col_count + WIN) - half_win
    col_inside = (frame_cols >= 0) & (frame_cols < col_count)
    presence = row_inside[:, None] & col_inside[None, :]
    window_rows = seq_id * (row_count // WIN) + jnp.arange(row_count) // WIN

    def batch_inputs(batch_id):
        page_id = page_order[batch_id]
        picked = lax.dynamic_index_in_dim(patches, page_id, 0, keepdims=False)
        filled = lax.dynamic_index_in_dim(page_rows, page_id, 0, keepdims=False)
        window_marks = lax.dynamic_index_in_dim(window_mask, page_id, 0, keepdims=False)
        column_marks = jnp.repeat(window_marks, WIN, axis=1) == 1
        cell_marks = jnp.repeat(column_marks, WIN, axis=0)
        key_valid = ((window_rows < filled)[:, None] & cell_marks).reshape(-1)
        query_live = (jnp.arange(NQ) < query_lengths[batch_id]).astype(jnp.float32)
        return (picked, key_valid, query_live)

    incoming = (
        jnp.zeros((row_count, col_count, D), jnp.bfloat16),
        jnp.zeros((NQ, D), jnp.bfloat16),
    )
    kept_list, patch_outs, query_outs = ([], [], [])
    for section_step in range(batches + 1):
        early_in = batch_inputs(min(section_step, batches - 1))
        late_in = batch_inputs(max(section_step - 1, 0))
        key_valid = jnp.where(first_section, early_in[1], late_in[1])
        query_live = jnp.where(first_section, early_in[2], late_in[2])
        patch_in = jnp.where(first_section, early_in[0], incoming[0])
        query_in = jnp.where(first_section, queries[min(section_step, batches - 1)], incoming[1])
        patch_out, query_out, kept = layer_forward(
            weights, patch_in, query_in, key_valid, query_live, section_id, presence
        )
        kept_list.append(kept)
        patch_outs.append(patch_out)
        query_outs.append(query_out)
        if section_step < batches:
            incoming = shifted((patch_out, query_out), "section", 1)
    refetched = (
        lax.all_gather(norm_attn, ("dp", "seq"), axis=1, tiled=True),
        lax.all_gather(norm_mlp, ("dp", "seq"), axis=1, tiled=True),
        lax.all_gather(norm_query, ("dp", "seq"), axis=1, tiled=True),
        lax.all_gather(attn_input, ("dp", "seq"), axis=1, tiled=True),
        lax.all_gather(attn_output, ("dp", "seq"), axis=1, tiled=True),
        lax.all_gather(mlp_up, ("dp", "seq"), axis=1, tiled=True),
        lax.all_gather(mlp_down, ("dp", "seq"), axis=1, tiled=True),
        lax.all_gather(cross_query, ("dp", "seq"), axis=1, tiled=True),
        lax.all_gather(cross_pair, ("dp", "seq"), axis=1, tiled=True),
        lax.all_gather(cross_output, ("dp", "seq"), axis=1, tiled=True),
    )
    weights = tuple((fetched_one[0] for fetched_one in refetched))
    gain_totals = [jnp.zeros(weights[slot].shape, jnp.float32) for slot in range(3)]
    pair_steps = []
    returning = (
        jnp.zeros((row_count, col_count, D), jnp.bfloat16),
        jnp.zeros((NQ, D), jnp.bfloat16),
    )
    patch_backs, query_backs = ([], [])
    for section_step in range(batches + 1):
        late_id = min(section_step, batches - 1)
        given_patch = lax.dynamic_index_in_dim(
            patch_cotangent, page_order[late_id], 0, keepdims=False
        )
        given_query = query_cotangent[late_id]
        active_now = jnp.where(first_section, section_step >= 1, section_step < batches)
        grad_patch = jnp.where(
            active_now,
            jnp.where(first_section, returning[0], given_patch),
            jnp.zeros_like(given_patch),
        )
        grad_query = jnp.where(
            active_now,
            jnp.where(first_section, returning[1], given_query),
            jnp.zeros_like(given_query),
        )
        kept = jax.tree.map(
            lambda early_val, late_val: jnp.where(first_section, early_val, late_val),
            kept_list[max(section_step - 1, 0)],
            kept_list[min(section_step + 1, batches)],
        )
        patch_grad, query_grad, gain_grads, matrix_pairs = layer_backward(
            weights, kept, grad_patch, grad_query, section_id, presence
        )
        gain_totals = [
            total_grad + part_grad for total_grad, part_grad in zip(gain_totals, gain_grads)
        ]
        pair_steps.append(matrix_pairs)
        patch_backs.append(patch_grad)
        query_backs.append(query_grad)
        if section_step < batches:
            returning = shifted((patch_grad, query_grad), "section", -1)
    grad_totals = list(gain_totals)
    for slot in range(7):
        left_rows = jnp.concatenate([step_pairs[slot][0] for step_pairs in pair_steps], axis=0)
        right_rows = jnp.concatenate([step_pairs[slot][1] for step_pairs in pair_steps], axis=0)
        grad_totals.append(outer_product(left_rows, right_rows))
    batch_ends = [
        jnp.where(first_section, patch_backs[batch_id + 1], patch_outs[batch_id + 1])
        for batch_id in range(batches)
    ]
    placed = []
    for page_slot in range(batches):
        page_value = jnp.zeros_like(batch_ends[0])
        for batch_id in range(batches):
            page_value = jnp.where(
                page_order[batch_id] == page_slot, batch_ends[batch_id], page_value
            )
        placed.append(page_value)
    patch_ends = jnp.stack(placed)[None]
    query_ends = jnp.stack(
        [
            jnp.where(first_section, query_backs[batch_id + 1], query_outs[batch_id + 1])
            for batch_id in range(batches)
        ]
    )[None]
    share = 1.0 / seq_count
    grad_totals[2] = grad_totals[2] * share
    grad_totals[7] = grad_totals[7] * share
    grad_totals[9] = grad_totals[9] * share
    summed = (
        lax.psum_scatter(grad_totals[0][None], ("dp", "seq"), scatter_dimension=1, tiled=True),
        lax.psum_scatter(grad_totals[1][None], ("dp", "seq"), scatter_dimension=1, tiled=True),
        lax.psum_scatter(grad_totals[2][None], ("dp", "seq"), scatter_dimension=1, tiled=True),
        lax.psum_scatter(grad_totals[3][None], ("dp", "seq"), scatter_dimension=1, tiled=True),
        lax.psum_scatter(grad_totals[4][None], ("dp", "seq"), scatter_dimension=1, tiled=True),
        lax.psum_scatter(grad_totals[5][None], ("dp", "seq"), scatter_dimension=1, tiled=True),
        lax.psum_scatter(grad_totals[6][None], ("dp", "seq"), scatter_dimension=1, tiled=True),
        lax.psum_scatter(grad_totals[7][None], ("dp", "seq"), scatter_dimension=1, tiled=True),
        lax.psum_scatter(grad_totals[8][None], ("dp", "seq"), scatter_dimension=1, tiled=True),
        lax.psum_scatter(grad_totals[9][None], ("dp", "seq"), scatter_dimension=1, tiled=True),
    )
    return (patch_ends, query_ends) + tuple(summed)


def solution(mesh):
    return jax.shard_map(
        per_device,
        mesh=mesh,
        in_specs=(
            P("dp", "seq", None, None),
            P("dp", None, None),
            P("dp"),
            P("dp", "seq", None),
            P("dp"),
            P("dp", None),
            P("section", ("dp", "seq")),
            P("section", ("dp", "seq")),
            P("section", ("dp", "seq")),
            P("section", ("dp", "seq"), None),
            P("section", ("dp", "seq"), None),
            P("section", ("dp", "seq"), None),
            P("section", ("dp", "seq"), None),
            P("section", ("dp", "seq"), None),
            P("section", ("dp", "seq"), None),
            P("section", ("dp", "seq"), None),
            P("dp", "seq", None, None),
            P("dp", None, None),
        ),
        out_specs=(
            P("section", "dp", "seq", None, None),
            P("section", "dp", None, None),
            P("section", ("dp", "seq")),
            P("section", ("dp", "seq")),
            P("section", ("dp", "seq")),
            P("section", ("dp", "seq"), None),
            P("section", ("dp", "seq"), None),
            P("section", ("dp", "seq"), None),
            P("section", ("dp", "seq"), None),
            P("section", ("dp", "seq"), None),
            P("section", ("dp", "seq"), None),
            P("section", ("dp", "seq"), None),
        ),
        check_vma=False,
    )
```

profile of v0, /device:TPU:0, one launch (start us, length us, event | category | flops | bytes accessed | tf_op | source)
XLA Modules:
  0.0 2962.1 jit_solution(10654315760657649748)
XLA Ops:
  24.5 44.5 %all-reduce.12 = (bf16[768]{0:T(1024)(128)(2,1)S(1)}, bf16[768]{0:T(1024)(128)(2,1)S(1)}, bf16[768]{0:T(1024)(128)(2,1)S(1)}) all-reduce(bf16[768]{0:T(1024)(128)(2,1)S(1)} %dynamic-update-slice.18, bf16[768]{0:T(1024)(128)(2,1)S(1)} %dynamic-update-slice.19, ...), channel_id=1, replica_groups=mesh['section'=2,'dp'=4,'seq'=4] {'dp','seq'}, use_global_device_ids=true, to_apply=%add.9 | all-reduce | flops 2304 | bytes 9216
  76.2 9.0 all-gather.20.cloned.1.call-done
  97.1 45.8 %all-gather.28.cloned.1.call-done = bf16[1,768,768]{2,1,0:T(8,128)(2,1)} async-done(((bf16[1,48,768]{2,1,0:T(8,128)(2,1)}), bf16[1,768,768]{2,1,0:T(8,128)(2,1)}) %all-gather.28.cloned.1.call-update) | async-done | bytes 1179664 | tf_op jit(solution)/shard_map/all_gather | solution.py:416
  151.8 8.6 collective-permute-done.1
  161.2 15.3 conditional.6
  176.5 24.3 all-gather.22.cloned.1.call-done
  203.2 61.4 %all-gather.30.cloned.1.call-done = bf16[1,768,1536]{2,1,0:T(8,128)(2,1)} async-done(((bf16[1,48,1536]{2,1,0:T(8,128)(2,1)}), bf16[1,768,1536]{2,1,0:T(8,128)(2,1)}) %all-gather.30.cloned.1.call-update) | async-done | bytes 2359312 | tf_op jit(solution)/shard_map/all_gather | solution.py:417
  270.4 8.1 all-gather.7
  278.5 7.3 all-gather.6
  299.9 22.3 all-gather.32.cloned.1.call-done
  322.2 44.7 %all-reduce.20.cloned.1.call-done = bf16[128,768]{1,0:T(8,128)(2,1)} async-done(((bf16[128,768]{1,0:T(8,128)(2,1)}), bf16[128,768]{1,0:T(8,128)(2,1)}) %all-reduce.20.cloned.1.call-update) | async-done | bytes 196624 | tf_op jit(solution)/shard_map/psum | solution.py:245
  373.9 76.7 %all-gather.24.cloned.1.call-done = bf16[1,768,3072]{2,1,0:T(8,128)(2,1)} async-done(((bf16[1,48,3072]{2,1,0:T(8,128)(2,1)}), bf16[1,768,3072]{2,1,0:T(8,128)(2,1)}) %all-gather.24.cloned.1.call-update) | async-done | bytes 4718608 | tf_op jit(solution)/shard_map/all_gather | solution.py:414
  450.6 12.0 fusion.200
  462.6 70.3 %all-gather.26.cloned.1.call-done = bf16[1,3072,768]{2,1,0:T(8,128)(2,1)} async-done(((bf16[1,192,768]{2,1,0:T(8,128)(2,1)}), bf16[1,3072,768]{2,1,0:T(8,128)(2,1)}) %all-gather.26.cloned.1.call-update) | async-done | bytes 4718608 | tf_op jit(solution)/shard_map/all_gather | solution.py:415
  532.9 4.5 fusion.340
  579.2 7.6 collective-permute-done.4
  588.7 28.8 conditional.7
  604.6 4.6 fusion.561
  620.9 12.5 broadcast_select_fusion.5
  636.4 52.7 %collective-permute-start.9 = (bf16[24,12,768]{2,0,1:T(8,128)(2,1)S(1)}, bf16[24,12,768]{2,0,1:T(8,128)(2,1)S(1)}, u32[]{:S(2)}, u32[]{:S(2)}) collective-permute-start(bf16[24,12,768]{2,0,1:T(8,128)(2,1)S(1)} %copy.744), channel_id=1, source_target_pairs={{0,16},{1,17},{2,18},{3,19},{4,20},{5,21},{6,22},{7,23},{8,24},{9,... | collective-permute-start | bytes 1327112 | tf_op jit(solution)/shard_map/ppermute | solution.py:50
  689.2 11.4 fusion.205
  700.6 5.5 fusion.187
  748.3 9.0 collective-permute-done.11
  758.1 23.5 conditional.9
  770.9 4.5 fusion.570
  798.8 7.1 all-gather.9
  805.9 8.2 all-gather.8
  822.9 9.1 psum.64
  836.3 12.5 broadcast_select_fusion.4
  860.8 59.8 %all-reduce.26.cloned.1.call-done = (bf16[128,768]{0,1:T(8,128)(2,1)}, bf16[128,768]{1,0:T(8,128)(2,1)}) async-done(((bf16[128,768]{0,1:T(8,128)(2,1)}, bf16[128,768]{1,0:T(8,128)(2,1)}), (bf16[128,768]{0,1:T(8,128)(2,1)}, bf16[128,768]{1,0:T(8,128)(2,1)})) %all-reduce.26.cloned.1.call-update) | async-done | bytes 393232 | tf_op jit(solution)/shard_map/psum | solution.py:319
  955.1 8.1 all-gather.11
  963.2 7.2 all-gather.10
  975.4 4.5 multiply_reduce_fusion.10
  979.9 9.8 psum.67
  996.4 69.8 %conditional.8 = (f32[24,12,2304]{2,1,0:T(8,128)}, bf16[12,12,2304]{2,1,0:T(8,128)(2,1)S(1)}, f32[6,12,2304]{2,1,0:T(8,128)S(1)}) conditional(s32[]{:T(128)} %convert_element_type.662, (pred[36,12,2304]{2,1,0:T(8,128)(4,1)}, bf16[36,12,2304]{2,1,0:T(8,128)(2,1)}, bf16[36,12,2304]{2,1,0:T(8,128)(2,1)}, pred[36,24]{0,1:T(8,128)(4,1)S(1)}, ...), branch_computations={%region_39.43_spmd, %region_43.47_spmd} | conditional | flops 981549056 | bytes 235815968 | solution.py:352
  1023.7 4.5 fusion.566
  1095.4 4.5 multiply_reduce_fusion.17
  1104.7 83.4 %collective-permute-done.17 = bf16[128,768]{1,0:T(8,128)(2,1)} collective-permute-done((bf16[128,768]{1,0:T(8,128)(2,1)}, bf16[128,768]{1,0:T(8,128)(2,1)}, u32[]{:S(2)}, u32[]{:S(2)}) %collective-permute-start.17) | collective-permute-done | bytes 196640 | tf_op jit(solution)/shard_map/ppermute | solution.py:50
  1190.7 5.0 multiply_reduce_fusion.9
  1195.7 10.9 psum.69
  1215.9 11.6 fusion.213
  1227.6 4.6 fusion.183
  1236.3 56.4 %conditional.10 = (f32[24,12,2304]{2,1,0:T(8,128)}, bf16[12,12,2304]{2,1,0:T(8,128)(2,1)S(1)}, f32[6,12,2304]{2,1,0:T(8,128)S(1)}) conditional(s32[]{:T(128)} %convert_element_type.662, (pred[36,12,2304]{2,1,0:T(8,128)(4,1)S(1)}, bf16[36,12,2304]{2,1,0:T(8,128)(2,1)}, bf16[36,12,2304]{2,1,0:T(8,128)(2,1)}, pred[36,24]{0,1:T(8,128)(4,1)S(1)}, ...), branch_computations={%region_79.83_spmd, %region_83.87_spmd} | conditional | flops 981549056 | bytes 241290336 | solution.py:352
  1303.6 6.5 collective-permute-done.15
  1327.2 131.1 %collective-permute-done.16 = bf16[24,12,768]{2,0,1:T(8,128)(2,1)S(1)} collective-permute-done((bf16[24,12,768]{2,0,1:T(8,128)(2,1)S(1)}, bf16[24,12,768]{2,0,1:T(8,128)(2,1)S(1)}, u32[]{:S(2)}, u32[]{:S(2)}) %collective-permute-start.16) | collective-permute-done | bytes 442400 | tf_op jit(solution)/shard_map/ppermute | solution.py:50
  1458.6 11.6 fusion.218
  1470.3 4.6 fusion.181
  1480.0 55.9 %conditional.11 = (f32[24,12,2304]{2,1,0:T(8,128)}, bf16[12,12,2304]{2,1,0:T(8,128)(2,1)S(1)}, f32[6,12,2304]{2,1,0:T(8,128)S(1)}) conditional(s32[]{:T(128)} %convert_element_type.662, (pred[36,12,2304]{2,1,0:T(8,128)(4,1)S(1)}, bf16[36,12,2304]{2,1,0:T(8,128)(2,1)}, bf16[36,12,2304]{2,1,0:T(8,128)(2,1)}, pred[36,24]{0,1:T(8,128)(4,1)S(1)}, ...), branch_computations={%region_102.106_spmd, %region_106.110_spmd} | conditional | flops 981549056 | bytes 233161728 | solution.py:352
  1545.8 5.4 collective-permute-done.19
  1559.3 4.7 multiply_reduce_fusion.15
  1576.6 7.2 convolution_bitcast_fusion.3
  1587.8 6.4 convolution_bitcast_fusion
  1597.2 7.6 convolution_bitcast_fusion.1
  1606.1 9.2 convolution_bitcast_fusion.2
  1623.5 157.0 %reduce-scatter.33.cloned.1.call-done = f32[48,1]{1,0:T(8,128)} async-done(((f32[768,1]{1,0:T(8,128)}), f32[48,1]{1,0:T(8,128)}) %reduce-scatter.33.cloned.1.call-update) | async-done | bytes 208
  1783.7 5.5 select_select_fusion.1
  1791.8 113.9 %reduce-scatter.31.cloned.1.call-done = f32[48,1]{1,0:T(8,128)} async-done(((f32[768,1]{1,0:T(8,128)}), f32[48,1]{1,0:T(8,128)}) %reduce-scatter.31.cloned.1.call-update) | async-done | bytes 208
  1907.1 131.4 %reduce-scatter.29.cloned.1.call-done = f32[1,48,768]{2,1,0:T(8,128)} async-done(((f32[1,768,768]{2,1,0:T(8,128)}), f32[1,48,768]{2,1,0:T(8,128)}) %reduce-scatter.29.cloned.1.call-update) | async-done | bytes 147472 | tf_op jit(solution)/shard_map/reduce_scatter | solution.py:554
  2038.5 132.1 %reduce-scatter.25.cloned.1.call-done = f32[1,48,768]{2,1,0:T(8,128)} async-done(((f32[1,768,768]{2,1,0:T(8,128)}), f32[1,48,768]{2,1,0:T(8,128)}) %reduce-scatter.25.cloned.1.call-update) | async-done | bytes 147472 | tf_op jit(solution)/shard_map/reduce_scatter | solution.py:552
  2170.6 132.8 %reduce-scatter.19.cloned.1.call-done = f32[1,48,768]{2,1,0:T(8,128)} async-done(((f32[1,768,768]{2,1,0:T(8,128)}), f32[1,48,768]{2,1,0:T(8,128)}) %reduce-scatter.19.cloned.1.call-update) | async-done | bytes 147472 | tf_op jit(solution)/shard_map/reduce_scatter | solution.py:549
  2303.4 141.8 %reduce-scatter.27.cloned.1.call-done = f32[1,48,1536]{2,1,0:T(8,128)} async-done(((f32[1,768,1536]{2,1,0:T(8,128)}), f32[1,48,1536]{2,1,0:T(8,128)}) %reduce-scatter.27.cloned.1.call-update) | async-done | bytes 294928 | tf_op jit(solution)/shard_map/reduce_scatter | solution.py:553
  2445.2 156.4 %reduce-scatter.17.cloned.1.call-done = f32[1,48,2304]{2,1,0:T(8,128)} async-done(((f32[1,768,2304]{2,1,0:T(8,128)}), f32[1,48,2304]{2,1,0:T(8,128)}) %reduce-scatter.17.cloned.1.call-update) | async-done | bytes 442384 | tf_op jit(solution)/shard_map/reduce_scatter | solution.py:548
  2601.6 177.1 %reduce-scatter.23.cloned.1.call-done = f32[1,192,768]{2,1,0:T(8,128)} async-done(((f32[1,3072,768]{2,1,0:T(8,128)}), f32[1,192,768]{2,1,0:T(8,128)}) %reduce-scatter.23.cloned.1.call-update) | async-done | bytes 589840 | tf_op jit(solution)/shard_map/reduce_scatter | solution.py:551
  2778.8 176.3 %reduce-scatter.21.cloned.1.call-done = f32[1,48,3072]{2,1,0:T(8,128)} async-done(((f32[1,768,3072]{2,1,0:T(8,128)}), f32[1,48,3072]{2,1,0:T(8,128)}) %reduce-scatter.21.cloned.1.call-update) | async-done | bytes 589840 | tf_op jit(solution)/shard_map/reduce_scatter | solution.py:550
  (1135 shorter events, 571.7 us)
Async XLA Ops:
  7.2 78.0 %all-gather.20.cloned.1.call-start = ((), (), s32[]{:S(2)}) async-start(), calls=%async_computation.10 | async-start | bytes 3760128 | tf_op jit(solution)/shard_map/all_gather | solution.py:412
  7.9 134.9 %all-gather.28.cloned.1.call-start = ((), (), s32[]{:S(2)}) async-start(), calls=%async_computation.14 | async-start | bytes 1253376 | tf_op jit(solution)/shard_map/all_gather | solution.py:416
  8.7 192.1 %all-gather.22.cloned.1.call-start = ((), (), s32[]{:S(2)}) async-start(), calls=%async_computation.11 | async-start | bytes 1253376 | tf_op jit(solution)/shard_map/all_gather | solution.py:413
  9.4 255.2 %all-gather.30.cloned.1.call-start = ((), (), s32[]{:S(2)}) async-start(), calls=%async_computation.15 | async-start | bytes 2506752 | tf_op jit(solution)/shard_map/all_gather | solution.py:417
  10.0 312.2 %all-gather.32.cloned.1.call-start = ((), (), s32[]{:S(2)}) async-start(), calls=%async_computation.17 | async-start | bytes 1253376 | tf_op jit(solution)/shard_map/all_gather | solution.py:418
  10.6 356.3 %all-reduce.20.cloned.1.call-start = ((), (), s32[]{:S(2)}) async-start(), calls=%async_computation.16 | async-start | bytes 393216 | tf_op jit(solution)/shard_map/psum | solution.py:245
  15.6 127.2 %copy-start.286 = (f32[128]{0:T(128)}, f32[128]{0:T(128)S(1)}, u32[]{:S(2)}) copy-start(f32[128]{0:T(128)S(1)} %broadcast_multiply_fusion.17) | copy-start | bytes 1540
  16.8 126.1 %copy-start.301 = (f32[128]{0:T(128)}, f32[128]{0:T(128)S(1)}, u32[]{:S(2)}) copy-start(f32[128]{0:T(128)S(1)} %add_rsqrt_fusion.8) | copy-start | bytes 1540
  69.0 642.4 %copy-start.194 = (f32[768]{0:T(1024)}, f32[768]{0:T(1024)S(1)}, u32[]{:S(2)}) copy-start(f32[768]{0:T(1024)S(1)} %mul.1302) | copy-start | bytes 9220
  70.9 469.9 %copy-start.161 = (f32[768]{0:T(1024)}, f32[768]{0:T(1024)S(1)}, u32[]{:S(2)}) copy-start(f32[768]{0:T(1024)S(1)} %mul.1304) | copy-start | bytes 9220
  70.9 871.6 %copy-start.210 = (f32[768]{0:T(1024)}, f32[768]{0:T(1024)S(1)}, u32[]{:S(2)}) copy-start(f32[768]{0:T(1024)S(1)} %mul.1303) | copy-start | bytes 9220
  75.7 682.5 %copy-start.207 = (pred[36,24]{0,1:T(8,128)(4,1)}, pred[36,24]{0,1:T(8,128)(4,1)S(1)}, u32[]{:S(2)}) copy-start(pred[36,24]{0,1:T(8,128)(4,1)S(1)} %broadcast_and_fusion) | copy-start | bytes 2596
  89.3 59.2 %collective-permute-start = (bf16[6,12,2304]{2,1,0:T(8,128)(2,1)}, bf16[6,12,2304]{2,1,0:T(8,128)(2,1)}, u32[]{:S(2)}, u32[]{:S(2)}) collective-permute-start(bf16[6,12,2304]{2,1,0:T(8,128)(2,1)} %slice.496), channel_id=1, source_target_pairs={{0,1},{1,2},{2,3},{4,5},{5,6},{6,7},{8,9},{9,10},{10,11},{12,13},{... | collective-permute-start | bytes 995336 | tf_op jit(solution)/shard_map/ppermute | solution.py:38
  147.3 13.1 collective-permute-start.1
  176.5 90.7 %copy-start.80 = (bf16[288,768]{1,0:T(8,128)(2,1)}, bf16[288,768]{1,0:T(8,128)(2,1)S(1)}, u32[]{:S(2)}) copy-start(bf16[288,768]{1,0:T(8,128)(2,1)S(1)} %get-tuple-element.1230) | copy-start | bytes 1327108
  288.2 78.7 %copy-start.69 = (bf16[2,128,768]{2,1,0:T(8,128)(2,1)S(1)}, bf16[2,128,768]{2,1,0:T(8,128)(2,1)}, u32[]{:S(2)}) copy-start(bf16[2,128,768]{2,1,0:T(8,128)(2,1)} %param.49) | copy-start | bytes 1179652
  288.2 81.9 %copy-start.136 = (bf16[2,128,768]{2,1,0:T(8,128)(2,1)S(1)}, bf16[2,128,768]{2,1,0:T(8,128)(2,1)}, u32[]{:S(2)}) copy-start(bf16[2,128,768]{2,1,0:T(8,128)(2,1)} %param.65) | copy-start | bytes 1179652
  289.1 161.4 %all-gather.24.cloned.1.call-start = ((), (), s32[]{:S(2)}) async-start(), calls=%async_computation.12 | async-start | bytes 5013504 | tf_op jit(solution)/shard_map/all_gather | solution.py:414
  289.9 243.0 %all-gather.26.cloned.1.call-start = ((), (), s32[]{:S(2)}) async-start(), calls=%async_computation.13 | async-start | bytes 5013504 | tf_op jit(solution)/shard_map/all_gather | solution.py:415
  290.6 630.0 %all-reduce.26.cloned.1.call-start = ((), (), s32[]{:S(2)}) async-start(), calls=%async_computation.30 | async-start | bytes 786432 | tf_op jit(solution)/shard_map/psum | solution.py:319
  291.7 158.8 %copy-start.230 = (f32[288]{0:T(512)S(1)}, f32[288]{0:T(512)}, u32[]{:S(2)}) copy-start(f32[288]{0:T(512)} %copy-done.229) | copy-start | bytes 3460
  291.7 158.8 %copy-start.252 = (f32[288]{0:T(512)S(1)}, f32[288]{0:T(512)}, u32[]{:S(2)}) copy-start(f32[288]{0:T(512)} %copy-done.251) | copy-start | bytes 3460
  292.0 397.2 %copy-start.74 = (bf16[288,768]{1,0:T(8,128)(2,1)}, bf16[288,768]{1,0:T(8,128)(2,1)S(1)}, u32[]{:S(2)}) copy-start(bf16[288,768]{1,0:T(8,128)(2,1)S(1)} %select_n.630) | copy-start | bytes 1327108
  293.9 168.6 %copy-start.284 = (f32[128]{0:T(128)}, f32[128]{0:T(128)S(1)}, u32[]{:S(2)}) copy-start(f32[128]{0:T(128)S(1)} %broadcast_select_fusion.38) | copy-start | bytes 1540
  368.6 4.2 collective-permute-start.5
  373.5 167.3 %copy-start.33 = (bf16[128,768]{1,0:T(8,128)(2,1)}, bf16[128,768]{1,0:T(8,128)(2,1)S(1)}, u32[]{:S(2)}) copy-start(bf16[128,768]{1,0:T(8,128)(2,1)S(1)} %get-tuple-element.837) | copy-start | bytes 589828
  373.7 167.2 %copy-start.270 = (f32[128]{0:T(128)}, f32[128]{0:T(128)S(1)}, u32[]{:S(2)}) copy-start(f32[128]{0:T(128)S(1)} %broadcast_multiply_fusion.16) | copy-start | bytes 1540
  539.5 2.7 collective-permute-start.2
  552.0 24.0 collective-permute-start.3
  572.5 14.4 collective-permute-start.4
  636.4 69.8 %collective-permute-start.9 = (bf16[24,12,768]{2,0,1:T(8,128)(2,1)S(1)}, bf16[24,12,768]{2,0,1:T(8,128)(2,1)S(1)}, u32[]{:S(2)}, u32[]{:S(2)}) collective-permute-start(bf16[24,12,768]{2,0,1:T(8,128)(2,1)S(1)} %copy.744), channel_id=1, source_target_pairs={{0,16},{1,17},{2,18},{3,19},{4,20},{5,21},{6,22},{7,23},{8,24},{9,... | collective-permute-start | bytes 1327112 | tf_op jit(solution)/shard_map/ppermute | solution.py:50
  731.4 13.7 collective-permute-start.10
  743.8 13.5 collective-permute-start.11
  836.0 237.4 %all-reduce.22.cloned.1.call-start = ((), (), s32[]{:S(2)}) async-start(), calls=%async_computation.18 | async-start | bytes 393216 | tf_op jit(solution)/shard_map/psum | solution.py:319
  922.0 6.4 collective-permute-start.12
  926.7 18.8 collective-permute-start.13
  996.4 302.8 %all-reduce.24.cloned.1.call-start = ((), (), s32[]{:S(2)}) async-start(), calls=%async_computation.29 | async-start | bytes 786432 | tf_op jit(solution)/shard_map/psum | solution.py:245
  1068.2 12.0 collective-permute-start.6
  1071.5 12.9 collective-permute-start.7
  1078.7 109.5 %collective-permute-start.17 = (bf16[128,768]{1,0:T(8,128)(2,1)}, bf16[128,768]{1,0:T(8,128)(2,1)}, u32[]{:S(2)}, u32[]{:S(2)}) collective-permute-start(bf16[128,768]{1,0:T(8,128)(2,1)} %get-tuple-element.808), channel_id=1, source_target_pairs={{16,0},{17,1},{18,2},{19,3},{20,4},{21,5},{22,6},{23,7},{24,8},{25... | collective-permute-start | bytes 589832 | tf_op jit(solution)/shard_map/ppermute | solution.py:50
  1099.9 90.0 %copy-start.24 = (bf16[1,768,768]{2,1,0:T(8,128)(2,1)S(1)}, bf16[1,768,768]{2,1,0:T(8,128)(2,1)}, u32[]{:S(2)}) copy-start(bf16[1,768,768]{2,1,0:T(8,128)(2,1)} %all-gather.32.cloned.1.call-done) | copy-start | bytes 3538948
  1100.4 90.3 %copy-start.187 = (f32[12,128]{1,0:T(8,128)S(1)}, f32[12,128]{1,0:T(8,128)}, u32[]{:S(2)}) copy-start(f32[12,128]{1,0:T(8,128)} %copy-done.186) | copy-start | bytes 18436
  1103.4 111.1 %collective-permute-start.8 = (bf16[24,12,768]{2,0,1:T(8,128)(2,1)}, bf16[24,12,768]{2,0,1:T(8,128)(2,1)}, u32[]{:S(2)}, u32[]{:S(2)}) collective-permute-start(bf16[24,12,768]{2,0,1:T(8,128)(2,1)} %copy.742), channel_id=1, source_target_pairs={{16,0},{17,1},{18,2},{19,3},{20,4},{21,5},{22,6},{23,7},{24,8},{25... | collective-permute-start | bytes 1327112 | tf_op jit(solution)/shard_map/ppermute | solution.py:50
  1209.8 412.4 %reduce-scatter.35.cloned.1.call-start = ((), (), s32[]{:S(2)}) async-start(), calls=%async_computation.28 | async-start | bytes 417792
  1294.6 9.1 collective-permute-start.14
  1297.6 12.6 collective-permute-start.15
  1323.0 135.3 %copy-start.113 = (bf16[2,24,12,768]{3,1,2,0:T(8,128)(2,1)S(1)}, bf16[2,24,12,768]{3,1,2,0:T(8,128)(2,1)}, u32[]{:S(2)}) copy-start(bf16[2,24,12,768]{3,1,2,0:T(8,128)(2,1)} %param.64) | copy-start | bytes 2654212
  1323.3 135.3 %copy-start.130 = (bf16[288,768]{1,0:T(8,128)(2,1)}, bf16[288,768]{1,0:T(8,128)(2,1)S(1)}, u32[]{:S(2)}) copy-start(bf16[288,768]{1,0:T(8,128)(2,1)S(1)} %add_convert_fusion.1) | copy-start | bytes 1327108
  1323.5 134.8 %collective-permute-start.16 = (bf16[24,12,768]{2,0,1:T(8,128)(2,1)S(1)}, bf16[24,12,768]{2,0,1:T(8,128)(2,1)S(1)}, u32[]{:S(2)}, u32[]{:S(2)}) collective-permute-start(bf16[24,12,768]{2,0,1:T(8,128)(2,1)S(1)} %copy.759), channel_id=1, source_target_pairs={{16,0},{17,1},{18,2},{19,3},{20,4},{21,5},{22,6},{23,7},{24,8},{25... | collective-permute-start | bytes 1327112 | tf_op jit(solution)/shard_map/ppermute | solution.py:50
  1325.8 454.7 %reduce-scatter.33.cloned.1.call-start = ((), (), s32[]{:S(2)}) async-start(), calls=%async_computation.27 | async-start | bytes 417792
  1537.2 8.6 collective-permute-start.18
  1540.0 11.2 collective-permute-start.19
  1543.0 362.8 %reduce-scatter.31.cloned.1.call-start = ((), (), s32[]{:S(2)}) async-start(), calls=%async_computation.26 | async-start | bytes 417792
  1564.9 473.6 %reduce-scatter.29.cloned.1.call-start = ((), (), s32[]{:S(2)}) async-start(), calls=%async_computation.25 | async-start | bytes 2506752 | tf_op jit(solution)/shard_map/reduce_scatter | solution.py:554
  1567.4 603.2 %reduce-scatter.25.cloned.1.call-start = ((), (), s32[]{:S(2)}) async-start(), calls=%async_computation.23 | async-start | bytes 2506752 | tf_op jit(solution)/shard_map/reduce_scatter | solution.py:552
  1570.7 732.7 %reduce-scatter.19.cloned.1.call-start = ((), (), s32[]{:S(2)}) async-start(), calls=%async_computation.20 | async-start | bytes 2506752 | tf_op jit(solution)/shard_map/reduce_scatter | solution.py:549
  1574.9 870.3 %reduce-scatter.27.cloned.1.call-start = ((), (), s32[]{:S(2)}) async-start(), calls=%async_computation.24 | async-start | bytes 5013504 | tf_op jit(solution)/shard_map/reduce_scatter | solution.py:553
  1583.9 1017.7 %reduce-scatter.17.cloned.1.call-start = ((), (), s32[]{:S(2)}) async-start(), calls=%async_computation.19 | async-start | bytes 7520256 | tf_op jit(solution)/shard_map/reduce_scatter | solution.py:548
  1594.3 1184.5 %reduce-scatter.23.cloned.1.call-start = ((), (), s32[]{:S(2)}) async-start(), calls=%async_computation.22 | async-start | bytes 10027008 | tf_op jit(solution)/shard_map/reduce_scatter | solution.py:551
  1604.8 1350.2 %reduce-scatter.21.cloned.1.call-start = ((), (), s32[]{:S(2)}) async-start(), calls=%async_computation.21 | async-start | bytes 10027008 | tf_op jit(solution)/shard_map/reduce_scatter | solution.py:550
  1615.3 166.5 %copy-start.240 = (f32[288]{0:T(512)S(1)}, f32[288]{0:T(512)}, u32[]{:S(2)}) copy-start(f32[288]{0:T(512)} %copy-done.239) | copy-start | bytes 3460
  1615.3 168.4 %copy-start.42 = (f32[288,768]{1,0:T(8,128)S(1)}, f32[288,768]{1,0:T(8,128)}, u32[]{:S(2)}) copy-start(f32[288,768]{1,0:T(8,128)} %copy-done.41) | copy-start | bytes 2654212
  1615.3 168.4 %copy-start.131 = (bf16[288,768]{1,0:T(8,128)(2,1)S(1)}, bf16[288,768]{1,0:T(8,128)(2,1)}, u32[]{:S(2)}) copy-start(bf16[288,768]{1,0:T(8,128)(2,1)} %copy-done.130) | copy-start | bytes 1327108
  1615.4 168.4 %copy-start.268 = (f32[288]{0:T(512)S(1)}, f32[288]{0:T(512)}, u32[]{:S(2)}) copy-start(f32[288]{0:T(512)} %copy-done.267) | copy-start | bytes 3460
  (281 other events, 2862.5 us)
Sparse Core Ops, SparseCore 0:
  10.8 74.3 all-gather.19
  88.0 54.7 all-gather.27
  145.6 55.0 all-gather.21
  203.4 61.1 all-gather.29
  267.2 54.9 all-gather.31
  325.5 41.3 all-reduce.19
  370.1 80.4 all-gather.23
  453.7 79.0 all-gather.25
  836.1 84.4 all-reduce.25
  996.4 42.4 all-reduce.21
  1210.0 62.7 all-reduce.23
  1325.9 252.8 reduce-scatter.34
  1584.2 196.3 reduce-scatter.32
  1785.0 120.6 reduce-scatter.30
  1911.8 126.6 reduce-scatter.28
  2043.8 126.6 reduce-scatter.24
  2176.7 126.6 reduce-scatter.18
  2309.0 136.1 reduce-scatter.26
  2452.0 149.6 reduce-scatter.16
  2608.7 170.0 reduce-scatter.22
  2785.0 169.9 reduce-scatter.20
where the time goes:
time: 2980 us; the launch traced here: 2960 us
  waiting for transfers between devices  2000 us (67%)
  matrix products  301 us (10%)
  local copies, waits for them, and re-layouts  279 us (9%)
  blocking collectives  120 us (4%)
  starting transfers between devices  94.6 us (3%)
  other arithmetic  94.5 us (3%)
  loops' own time  48.3 us (2%)
    unnamed x24, waiting for transfers between devices  276 us
    ppermute x8, waiting for transfers between devices, shifted(): return lax.ppermute(array, axis, pairs)  215 us
    reduce_scatter x1, waiting for transfers between devices, per_device(): lax.psum_scatter(grad_totals[6][None], ('dp', 'seq'), scatter_dimension=1...  177 us
    reduce_scatter x1, waiting for transfers between devices, per_device(): lax.psum_scatter(grad_totals[5][None], ('dp', 'seq'), scatter_dimension=1...  176 us
    reduce_scatter x1, waiting for transfers between devices, per_device(): lax.psum_scatter(grad_totals[3][None], ('dp', 'seq'), scatter_dimension=1...  156 us
    reduce_scatter x1, waiting for transfers between devices, per_device(): lax.psum_scatter(grad_totals[8][None], ('dp', 'seq'), scatter_dimension=1...  142 us
    reduce_scatter x1, waiting for transfers between devices, per_device(): lax.psum_scatter(grad_totals[4][None], ('dp', 'seq'), scatter_dimension=1...  133 us
    reduce_scatter x1, waiting for transfers between devices, per_device(): lax.psum_scatter(grad_totals[7][None], ('dp', 'seq'), scatter_dimension=1...  132 us
  transfers between devices with their start and end apart: 41, of which 29 were waited for; matrix products, arithmetic and copies ran while one was open for 16% of the time, Pallas kernels for 0%

commit v1 on v0

v1 whole, which is shorter than its diff:
```python
from functools import partial
import math

import jax
import jax.numpy as jnp
from jax import lax
from jax.experimental import pallas as pl
from jax.experimental.pallas import tpu as pltpu
from jax.sharding import PartitionSpec as P

D = 768
HEADS = 12
HDIM = 64
WIN = 12
NQ = 128
CELLS = WIN * WIN
HALF = D // 2
HH = HEADS // 2
PAIRS = HH // 2
RIM = WIN // 2 * WIN

epsilon = 1e-05
hidden_value = -1e30
scaling = 1.0 / math.sqrt(HDIM)
bf16 = jnp.bfloat16
f32 = jnp.float32
SWAP = [(0, 1), (1, 0)]
ANY = pl.BlockSpec(memory_space=pl.ANY)
SMEM = pl.BlockSpec(memory_space=pltpu.SMEM)


def whole(shape):
    return pl.BlockSpec(shape, lambda *_: (0,) * len(shape))


def per_batch(shape):
    return pl.BlockSpec((1,) + tuple(shape[1:]), lambda m: (m,) + (0,) * (len(shape) - 1))


def run(kernel, name, grid, ins, outs, scratch, flops):
    arrays = [a for a, _ in ins]
    nbytes = sum(a.size * a.dtype.itemsize for a in arrays)
    return pl.pallas_call(
        kernel,
        grid=grid,
        in_specs=[s for _, s in ins],
        out_specs=[s for _, _, s in outs],
        out_shape=[jax.ShapeDtypeStruct(sh, dt) for sh, dt, _ in outs],
        scratch_shapes=scratch,
        compiler_params=pltpu.CompilerParams(vmem_limit_bytes=52 * 1024 * 1024),
        cost_estimate=pl.CostEstimate(flops=int(flops), bytes_accessed=int(nbytes), transcendentals=0),
        name=name,
    )(*arrays)


def start_fetch(dst, pieces, order, rows, row0, col0, sem):
    cols = dst.shape[1]
    for p, piece in enumerate(pieces):
        slots = piece.shape[0]
        for s in range(slots):
            at = pl.multiple_of(order[p * slots + s] * rows, 16)
            pltpu.make_async_copy(
                piece.at[s, pl.ds(row0, rows), pl.ds(col0, cols)], dst.at[pl.ds(at, rows), :], sem
            ).start()


def end_fetch(dst, sem):
    pltpu.make_async_copy(dst, dst, sem).wait()


def spread_rows(values, outs, order, rows, row0, col0):
    cols = values.shape[1]
    for p, out in enumerate(outs):
        slots = out.shape[0]
        for s in range(slots):
            at = pl.multiple_of(order[p * slots + s] * rows, 8)
            out[s, row0 : row0 + rows, col0 : col0 + cols] = values[pl.ds(at, rows), :].astype(bf16)


def nn(a, b):
    return jnp.dot(a, b, preferred_element_type=f32)


def nt(a, b):
    return lax.dot_general(a, b, (((1,), (1,)), ((), ())), preferred_element_type=f32)


def tn(a, b):
    return lax.dot_general(a, b, (((0,), (0,)), ((), ())), preferred_element_type=f32)


def norm_parts(values):
    center = values - jnp.mean(values, axis=-1, keepdims=True)
    inv = lax.rsqrt(jnp.mean(center * center, axis=-1, keepdims=True) + epsilon)
    return center * inv, inv


def norm_back(unit, inv, gain, grad):
    scaled = grad * gain
    return inv * (
        scaled
        - jnp.mean(scaled, axis=-1, keepdims=True)
        - unit * jnp.mean(scaled * unit, axis=-1, keepdims=True)
    )


def lane_halves(rows):
    lane = lax.broadcasted_iota(jnp.int32, (rows, 128), 1)
    return lane < HDIM


def half_masks():
    lane = lax.broadcasted_iota(jnp.int32, (1, 128), 1)
    low = (lane < HDIM).astype(f32)
    return low.astype(bf16), (1.0 - low).astype(bf16)


def attn_forward(n, shifted, *refs):
    order_c, order_r, x_ref = refs[:3]
    refs = refs[3:]
    if shifted:
        mask_ref, refs = refs[0], refs[1:]
    u0, u1, refs = refs[:n], refs[n : 2 * n], refs[2 * n :]
    h_ref, qkv_ref, p_ref, o_ref, part_ref, gain_ref, w_in, w_out, mixed, hidden, sem0, sem1 = refs
    tokens = x_ref.shape[1]
    own = o_ref.shape[1]
    lo = (tokens - own) // 2

    @pl.when(pl.program_id(0) == 0)
    def _():
        start_fetch(w_in, u0, order_c, w_in.shape[0] // (n * u0[0].shape[0]), 0, 0, sem0)
        start_fetch(w_out, u1, order_r, w_out.shape[0] // (n * u1[0].shape[0]), 0, 0, sem1)
        end_fetch(w_in, sem0)
        end_fetch(w_out, sem1)
        gain_ref[...] = w_in[:, :128].astype(f32).T[0:8]

    unit, _ = norm_parts(x_ref[0].astype(f32))
    hidden[...] = unit * gain_ref[0:1]
    h_ref[0] = hidden[lo : lo + own].astype(bf16)
    qkv_ref[0] = nn(hidden[...].astype(bf16), w_in[:, 128:]).astype(bf16)
    first_half = lane_halves(CELLS)
    masks = half_masks()
    for block in range(tokens // CELLS):
        rows = slice(block * CELLS, (block + 1) * CELLS)
        for pair in range(PAIRS):
            q2 = qkv_ref[0, rows, pair * 128 : pair * 128 + 128]
            k2 = qkv_ref[0, rows, HALF + pair * 128 : HALF + pair * 128 + 128]
            v2 = qkv_ref[0, rows, 2 * HALF + pair * 128 : 2 * HALF + pair * 128 + 128]
            mixed_two = []
            for side in range(2):
                scores = nt(q2 * masks[side], k2) * scaling
                if shifted:
                    scores = scores + mask_ref[block]
                weights = jnp.exp(scores - jnp.max(scores, axis=-1, keepdims=True))
                probs = (weights / jnp.sum(weights, axis=-1, keepdims=True)).astype(bf16)
                p_ref[0, block * HH + pair * 2 + side] = probs
                mixed_two.append(nn(probs, v2))
            mixed[rows, pair * 128 : pair * 128 + 128] = jnp.where(
                first_half, mixed_two[0], mixed_two[1]
            )
    out = mixed[lo : lo + own].astype(bf16)
    o_ref[0] = out
    part_ref[0] = nn(out, w_out[...]).astype(bf16)


def mlp_forward(n, *refs):
    order_c, order_r, x_ref, pa_ref, pb_ref, gain_ref, cq_ref, valid_ref = refs[:8]
    refs = refs[8:]
    u2, u3, refs = refs[:n], refs[n : 2 * n], refs[2 * n :]
    first_ref, h_ref, slope_ref, act_ref, part_ref, ckv_ref, e_ref, o_ref, stat_ref = refs[:9]
    w_up, w_down, sem0, sem1 = refs[9:]
    hid = slope_ref.shape[2]
    tokens = x_ref.shape[1]

    @pl.when(pl.program_id(0) == 0)
    def _():
        start_fetch(w_up, u2, order_c, w_up.shape[0] // (n * u2[0].shape[0]), 0, 0, sem0)
        start_fetch(w_down, u3, order_r, w_down.shape[0] // (n * u3[0].shape[0]), 0, 0, sem1)
        end_fetch(w_up, sem0)
        end_fetch(w_down, sem1)

    first = x_ref[0].astype(f32) + (pa_ref[0].astype(f32) + pb_ref[0].astype(f32))
    first_ref[0] = first
    unit, _ = norm_parts(first)
    hidden = (unit * gain_ref[1:2]).astype(bf16)
    h_ref[0] = hidden
    ckv_ref[0] = nn(hidden, w_up[:, hid:]).astype(bf16)
    step = 512
    for at in range(0, hid, step):
        lifted = nn(hidden, w_up[:, at : at + step])
        cdf = 0.5 + 0.5 * lax.erf(lifted * math.sqrt(0.5))
        act_ref[0, :, at : at + step] = (lifted * cdf).astype(bf16)
        pdf = jnp.exp(lifted * lifted * -0.5) * (1.0 / math.sqrt(2.0 * math.pi))
        slope_ref[0, :, at : at + step] = (cdf + lifted * pdf).astype(bf16)
    part_ref[0] = nn(act_ref[0], w_down[...]).astype(bf16)

    valid = jnp.broadcast_to(valid_ref[0], (NQ, tokens)) > 0.5
    first_half = lane_halves(NQ)
    masks = half_masks()
    lane = lax.broadcasted_iota(jnp.int32, (NQ, 128), 1)
    stats = jnp.zeros((NQ, 128), f32)
    for pair in range(PAIRS):
        q2 = cq_ref[0, :, pair * 128 : pair * 128 + 128]
        k2 = ckv_ref[0, :, pair * 128 : pair * 128 + 128]
        v2 = ckv_ref[0, :, HALF + pair * 128 : HALF + pair * 128 + 128]
        mixed_two = []
        for side in range(2):
            head = pair * 2 + side
            scores = jnp.where(valid, nt(q2 * masks[side], k2) * scaling, hidden_value)
            peak = jnp.max(scores, axis=-1, keepdims=True)
            weights = jnp.where(valid, jnp.exp(scores - peak), 0.0)
            total = jnp.sum(weights, axis=-1, keepdims=True)
            stats = jnp.where(lane == head, peak, stats)
            stats = jnp.where(lane == 8 + head, total, stats)
            low = weights.astype(bf16)
            e_ref[0, head] = low
            mixed_two.append(nn(low, v2))
        o_ref[0, :, pair * 128 : pair * 128 + 128] = jnp.where(
            first_half, mixed_two[0], mixed_two[1]
        ).astype(bf16)
    stat_ref[0] = stats.T[0:16]


def query_in(n, has_parts, *refs):
    order_c, q_ref, gain_ref = refs[:3]
    refs = refs[3:]
    if has_parts:
        pa_ref, pb_ref, live_ref, refs = refs[0], refs[1], refs[2], refs[3:]
    u2, refs = refs[:n], refs[n:]
    if has_parts:
        new_ref, refs = refs[0], refs[1:]
    h_ref, cq_ref, w_q, sem = refs
    start_fetch(
        w_q, u2, order_c, w_q.shape[0] // (n * u2[0].shape[0]), 0, u2[0].shape[2] - HALF, sem
    )
    end_fetch(w_q, sem)
    for m in range(q_ref.shape[0]):
        query = q_ref[m].astype(f32)
        if has_parts:
            query = query + live_ref[m] * (pa_ref[m].astype(f32) + pb_ref[m].astype(f32))
            low = query.astype(bf16)
            new_ref[m] = low
            query = low.astype(f32)
        unit, _ = norm_parts(query)
        hidden = (unit * gain_ref[2:3]).astype(bf16)
        h_ref[m] = hidden
        cq_ref[m] = nn(hidden, w_q[...]).astype(bf16)


def query_out(n, ns, *refs):
    order_r, order_s = refs[:2]
    refs = refs[2:]
    os, ss, refs = refs[:ns], refs[ns : 2 * ns], refs[2 * ns :]
    u3, refs = refs[:n], refs[n:]
    att_ref, low_ref, coef_ref, part_ref, w_co, o_all, s_all, sem = refs
    rows = w_co.shape[0] // (n * u3[0].shape[0])
    start_fetch(w_co, u3, order_r, rows, u3[0].shape[1] - rows, 0, sem)
    for p in range(ns):
        o_all[order_s[p]] = os[p][...]
        s_all[order_s[p]] = ss[p][...]
    first_half = lane_halves(NQ)
    end_fetch(w_co, sem)
    for m in range(att_ref.shape[0]):
        peak = s_all[0, m, 0:8]
        for s in range(1, ns):
            peak = jnp.maximum(peak, s_all[s, m, 0:8])
        scales = [jnp.exp(s_all[s, m, 0:8] - peak) for s in range(ns)]
        total = scales[0] * s_all[0, m, 8:16]
        for s in range(1, ns):
            total = total + scales[s] * s_all[s, m, 8:16]
        inverse = 1.0 / jnp.where(total > 0.0, total, 1.0)
        blocks = [scale * inverse for scale in scales]
        if ns * 8 < 128:
            blocks.append(jnp.zeros((128 - ns * 8, 128), f32))
        columns = jnp.concatenate(blocks, axis=0).T
        mine = jnp.exp(ss[0][m, 0:8] - peak) * inverse
        coef_ref[m] = jnp.concatenate([mine, jnp.zeros((120, 128), f32)], axis=0).T
        for pair in range(PAIRS):
            mixed = jnp.zeros((NQ, 128), f32)
            for s in range(ns):
                at = s * 8 + pair * 2
                factor = jnp.where(first_half, columns[:, at : at + 1], columns[:, at + 1 : at + 2])
                mixed = mixed + factor * o_all[s, m, :, pair * 128 : pair * 128 + 128].astype(f32)
            att_ref[m, :, pair * 128 : pair * 128 + 128] = mixed
        low = att_ref[m].astype(bf16)
        low_ref[m] = low
        part_ref[m] = nn(low, w_co[...]).astype(bf16)


def mlp_backward(n, *refs):
    order_c, order_r, ds_ref, slope_ref, e_ref, coef_ref, dq_ref, live_ref, att_ref, cq_ref, ckv_ref = refs[:11]
    refs = refs[11:]
    u2, u3, refs = refs[:n], refs[n : 2 * n], refs[2 * n :]
    du_ref, dckv_ref, dcq_ref, part_ref, dc_ref, w_up, w_down, w_co, sem0, sem1, sem2 = refs
    hid = slope_ref.shape[2]
    tokens = ds_ref.shape[1]

    @pl.when(pl.program_id(0) == 0)
    def _():
        down_rows = w_down.shape[0] // (n * u3[0].shape[0])
        start_fetch(w_down, u3, order_r, down_rows, 0, 0, sem1)
        start_fetch(w_co, u3, order_r, w_co.shape[0] // (n * u3[0].shape[0]), down_rows, 0, sem2)
        start_fetch(w_up, u2, order_c, w_up.shape[0] // (n * u2[0].shape[0]), 0, 0, sem0)
        end_fetch(w_down, sem1)
        end_fetch(w_co, sem2)
        end_fetch(w_up, sem0)

    grad_second = ds_ref[0]
    step = 512
    for at in range(0, hid, step):
        grad_act = nt(grad_second, w_down[at : at + step, :])
        du_ref[0, :, at : at + step] = (
            grad_act * slope_ref[0, :, at : at + step].astype(f32)
        ).astype(bf16)

    grad_cross = (live_ref[0] * dq_ref[0].astype(f32)).astype(bf16)
    dc_ref[0] = grad_cross
    grad_att = nt(grad_cross, w_co[...]).astype(bf16)
    first_q = lane_halves(NQ)
    first_k = lane_halves(tokens)
    masks = half_masks()
    for pair in range(PAIRS):
        lanes = slice(pair * 128, pair * 128 + 128)
        upper = slice(HALF + pair * 128, HALF + pair * 128 + 128)
        a2 = grad_att[:, lanes]
        q2 = cq_ref[0, :, lanes]
        k2 = ckv_ref[0, :, lanes]
        v2 = ckv_ref[0, :, upper]
        inner = a2.astype(f32) * att_ref[0, :, lanes]
        dq_two, dk_two, dv_two = [], [], []
        for side in range(2):
            head = pair * 2 + side
            keep = first_q if side == 0 else jnp.logical_not(first_q)
            delta = jnp.sum(jnp.where(keep, inner, 0.0), axis=-1, keepdims=True)
            probs = e_ref[0, head].astype(f32) * coef_ref[0, :, head : head + 1]
            grad_probs = nt(a2 * masks[side], v2)
            grad_scores = (probs * (grad_probs - delta)).astype(bf16)
            dq_two.append(nn(grad_scores, k2))
            dk_two.append(tn(grad_scores, q2))
            dv_two.append(tn(probs.astype(bf16), a2))
        dcq_ref[0, :, lanes] = (jnp.where(first_q, dq_two[0], dq_two[1]) * scaling).astype(bf16)
        dckv_ref[0, :, lanes] = (jnp.where(first_k, dk_two[0], dk_two[1]) * scaling).astype(bf16)
        dckv_ref[0, :, upper] = jnp.where(first_k, dv_two[0], dv_two[1]).astype(bf16)
    part_ref[0] = (
        nt(du_ref[0], w_up[:, :hid]) + nt(dckv_ref[0], w_up[:, hid:])
    ).astype(bf16)


def first_backward(n, *refs):
    order_r, ds_ref, da_ref, db_ref, first_ref, gain_ref = refs[:6]
    u1, refs = refs[6 : 6 + n], refs[6 + n :]
    df_ref, low_ref, do_ref, dg_ref, w_out, sem = refs

    @pl.when(pl.program_id(0) == 0)
    def _():
        start_fetch(w_out, u1, order_r, w_out.shape[0] // (n * u1[0].shape[0]), 0, 0, sem)
        dg_ref[...] = jnp.zeros_like(dg_ref)
        end_fetch(w_out, sem)

    grad = da_ref[0].astype(f32) + db_ref[0].astype(f32)
    unit, inv = norm_parts(first_ref[0])
    dg_ref[0:1] += jnp.sum(grad * unit, axis=0, keepdims=True)
    grad_first = ds_ref[0].astype(f32) + norm_back(unit, inv, gain_ref[1:2], grad)
    df_ref[0] = grad_first
    low = grad_first.astype(bf16)
    low_ref[0] = low
    do_ref[0] = nt(low, w_out[...]).astype(bf16)


def attn_backward(n, *refs):
    order_c, do_ref, qkv_ref, p_ref = refs[:4]
    u0, refs = refs[4 : 4 + n], refs[4 + n :]
    dqkv_ref, part_ref, w_in, wide, sem = refs
    tokens = do_ref.shape[1]
    own = dqkv_ref.shape[1]
    lo = (tokens - own) // 2

    @pl.when(pl.program_id(0) == 0)
    def _():
        start_fetch(w_in, u0, order_c, w_in.shape[0] // (n * u0[0].shape[0]), 0, 128, sem)
        end_fetch(w_in, sem)

    first_half = lane_halves(CELLS)
    masks = half_masks()
    for block in range(tokens // CELLS):
        rows = slice(block * CELLS, (block + 1) * CELLS)
        for pair in range(PAIRS):
            lanes = slice(pair * 128, pair * 128 + 128)
            q2 = qkv_ref[0, rows, lanes]
            k2 = qkv_ref[0, rows, HALF + pair * 128 : HALF + pair * 128 + 128]
            v2 = qkv_ref[0, rows, 2 * HALF + pair * 128 : 2 * HALF + pair * 128 + 128]
            g2 = do_ref[0, rows, lanes]
            dq_two, dk_two, dv_two = [], [], []
            for side in range(2):
                probs = p_ref[0, block * HH + pair * 2 + side]
                wide_probs = probs.astype(f32)
                grad_probs = nt(g2 * masks[side], v2)
                delta = jnp.sum(wide_probs * grad_probs, axis=-1, keepdims=True)
                grad_scores = (wide_probs * (grad_probs - delta)).astype(bf16)
                dq_two.append(nn(grad_scores, k2))
                dk_two.append(tn(grad_scores, q2))
                dv_two.append(tn(probs, g2))
            wide[rows, lanes] = jnp.where(first_half, dq_two[0], dq_two[1]) * scaling
            wide[rows, HALF + pair * 128 : HALF + pair * 128 + 128] = (
                jnp.where(first_half, dk_two[0], dk_two[1]) * scaling
            )
            wide[rows, 2 * HALF + pair * 128 : 2 * HALF + pair * 128 + 128] = jnp.where(
                first_half, dv_two[0], dv_two[1]
            )
    low = wide[lo : lo + own].astype(bf16)
    dqkv_ref[0] = low
    part_ref[0] = nt(low, w_in[...]).astype(bf16)


def input_backward(x_ref, df_ref, da_ref, db_ref, gain_ref, dx_ref, dg_ref):
    @pl.when(pl.program_id(0) == 0)
    def _():
        dg_ref[...] = jnp.zeros_like(dg_ref)

    grad = da_ref[0].astype(f32) + db_ref[0].astype(f32)
    unit, inv = norm_parts(x_ref[0].astype(f32))
    dg_ref[0:1] += jnp.sum(grad * unit, axis=0, keepdims=True)
    dx_ref[0] = (df_ref[0] + norm_back(unit, inv, gain_ref[0:1], grad)).astype(bf16)


def query_back_one(n, ns, *refs):
    order_c, order_s = refs[:2]
    parts, refs = refs[2 : 2 + ns], refs[2 + ns :]
    u2, refs = refs[:n], refs[n:]
    dcq_ref, part_ref, w_q, all_parts, sem = refs
    start_fetch(
        w_q, u2, order_c, w_q.shape[0] // (n * u2[0].shape[0]), 0, u2[0].shape[2] - HALF, sem
    )
    for p in range(ns):
        all_parts[order_s[p]] = parts[p][...]
    end_fetch(w_q, sem)
    for m in range(dcq_ref.shape[0]):
        total = all_parts[0, m].astype(f32)
        for s in range(1, ns):
            total = total + all_parts[s, m].astype(f32)
        low = total.astype(bf16)
        dcq_ref[m] = low
        part_ref[m] = nt(low, w_q[...]).astype(bf16)


def query_back_two(q_ref, dq_ref, da_ref, db_ref, gain_ref, out_ref, dg_ref):
    total = jnp.zeros((1, D), f32)
    for m in range(q_ref.shape[0]):
        grad = da_ref[m].astype(f32) + db_ref[m].astype(f32)
        unit, inv = norm_parts(q_ref[m].astype(f32))
        total = total + jnp.sum(grad * unit, axis=0, keepdims=True)
        out_ref[m] = (dq_ref[m].astype(f32) + norm_back(unit, inv, gain_ref[2:3], grad)).astype(bf16)
    dg_ref[...] = jnp.broadcast_to(total, dg_ref.shape)


def weight_grads(n, plan, order_by, *refs):
    order_c, order_r = refs[:2]
    count = 1 + max(max(item[0], item[1]) for item in plan)
    sides, refs = refs[2 : 2 + count], refs[2 + count :]
    units = len(order_by)
    outs, acc = [refs[u * n : (u + 1) * n] for u in range(units)], refs[units * n]
    for left, right, unit, rows, row0, col0 in plan:
        order = order_c if order_by[unit] == "c" else order_r
        height, width = sides[left].shape[1], sides[right].shape[1]
        step = 384
        for at in range(0, width, step):
            acc[0:height] = tn(sides[left][...], sides[right][:, at : at + step])
            spread_rows(acc, outs[unit], order, rows, row0, col0 + at)


def per_device(
    patches,
    queries,
    page_rows,
    window_mask,
    query_lengths,
    plan,
    norm_attn,
    norm_mlp,
    norm_query,
    attn_input,
    attn_output,
    mlp_up,
    mlp_down,
    cross_query,
    cross_pair,
    cross_output,
    patch_cotangent,
    query_cotangent,
):
    core = lax.axis_index("section")
    zi = lax.axis_index("dp")
    qi = lax.axis_index("seq")
    nz, ns = lax.axis_size("dp"), lax.axis_size("seq")
    rows = attn_input.shape[1]
    hid = mlp_up.shape[2] // 2
    manual = rows % 16 == 0 and ns == 4 and nz & (nz - 1) == 0
    near = nz // 2
    batches, row_count, col_count = patches.shape[:3]
    tokens = row_count * col_count
    core_zero = core == 0

    def swap(x):
        return lax.ppermute(x, "section", SWAP)

    def across(x, r):
        return lax.ppermute(x, "seq", [(j, j ^ r) for j in range(ns)])

    if manual:
        n = ns
        far = (zi // near) ^ core
        order_c = jnp.stack([((zi ^ r) * ns + (qi ^ p)) for p in range(ns) for r in range(nz)])
        order_r = jnp.stack(
            [
                (((zi ^ (far * near + k)) - core * near) * ns + (qi ^ p))
                for p in range(ns)
                for k in range(near)
            ]
        )
    else:
        n = 1
        order_c = jnp.zeros((1,), jnp.int32)
        order_r = jnp.zeros((1,), jnp.int32)
    order_s = jnp.stack([qi ^ p for p in range(ns)])
    order_c, order_r, order_s = (o.astype(jnp.int32) for o in (order_c, order_r, order_s))

    gain_block = jnp.stack([norm_attn[0], norm_mlp[0], norm_query[0]], axis=1)
    gain_block = jnp.pad(gain_block, ((0, 0), (0, 125)))

    def columns(arrays, half):
        return [a[:, half * w : (half + 1) * w] for a, w in arrays]

    win, up, cq, cp = attn_input[0], mlp_up[0], cross_query[0], cross_pair[0]
    col_parts = [
        [(win[:, :D], HALF), (win[:, D : 2 * D], HALF), (win[:, 2 * D :], HALF)],
        [(up, hid), (cp[:, :D], HALF), (cp[:, D:], HALF), (cq, HALF)],
    ]
    row_units = [attn_output[0], jnp.concatenate([mlp_down[0], cross_output[0]], axis=0)]
    halves = []
    for index, parts in enumerate(col_parts):
        lead = [gain_block] if index == 0 else []
        halves.append([jnp.concatenate(lead + columns(parts, h), axis=1) for h in range(2)])

    def spread_xy(own, by_y):
        one = across(own, 1)
        two = across(own, 2)
        three = across(one, 2) if by_y else across(two, 1)
        return [own, one, two, three]

    def gather_col(mine, theirs, layer, by_y):
        unit = jnp.where(core == layer, mine, theirs)
        stack = jnp.stack(
            [unit]
            + [lax.ppermute(unit, "dp", [(j, j ^ r) for j in range(nz)]) for r in range(1, nz)]
        )
        return spread_xy(stack, by_y)

    def gather_row(mine, theirs, layer, by_y):
        unit = jnp.where(core == layer, mine, theirs)
        got = [unit]
        for r in range(1, nz):
            pairs = [
                (c * nz + j, c * nz + (j ^ r))
                for c in range(2)
                for j in range(c * near, (c + 1) * near)
            ]
            got.append(lax.ppermute(unit, ("section", "dp"), pairs))
        stack = jnp.where(far == 0, jnp.stack(got[:near]), jnp.stack(got[near:]))
        return spread_xy(stack, by_y)

    units = [[None] * 4 for _ in range(2)]
    if manual:
        col_mine = [jnp.where(core_zero, h[0], h[1]) for h in halves]
        col_send = [jnp.where(core_zero, h[1], h[0]) for h in halves]
        col_recv = [swap(s) for s in col_send]
        row_recv = [swap(s) for s in row_units]
        for layer in range(2):
            units[layer][0] = gather_col(col_mine[0], col_recv[0], layer, True)
            units[layer][1] = gather_row(row_units[0], row_recv[0], layer, False)
            units[layer][2] = gather_col(col_mine[1], col_recv[1], layer, False)
            units[layer][3] = gather_row(row_units[1], row_recv[1], layer, True)
    else:

        def gather_all(x):
            return lax.all_gather(
                lax.all_gather(x, ("dp", "seq"), axis=0, tiled=True), "section", axis=0
            )

        whole_cols = [[gather_all(half) for half in h] for h in halves]
        whole_rows = [gather_all(x) for x in (attn_output[0], mlp_down[0], cross_output[0])]
        for layer in range(2):
            for index in range(2):
                units[layer][2 * index] = [
                    jnp.where(core_zero, whole_cols[index][0][layer], whole_cols[index][1][layer])[None]
                ]
            mine = [
                lax.dynamic_slice_in_dim(w[layer], core * (w.shape[1] // 2), w.shape[1] // 2, 0)
                for w in whole_rows
            ]
            units[layer][1] = [mine[0][None]]
            units[layer][3] = [jnp.concatenate(mine[1:], axis=0)[None]]

    order = jnp.arange(batches)
    inverse = jnp.sum(jnp.where(plan[0][None, :] == order[:, None], order[None, :], 0), axis=1)
    query_start = jnp.take(queries, inverse, axis=0)
    query_given = jnp.take(query_cotangent, inverse, axis=0)
    lengths = jnp.take(query_lengths, inverse)
    live = (jnp.arange(NQ)[None, :] < lengths[:, None]).astype(f32)[:, :, None]
    window_rows = qi * (row_count // WIN) + jnp.arange(row_count // WIN)
    marks = (window_rows[None, :, None] < page_rows[:, None, None]) & (window_mask == 1)
    valid = jnp.repeat(jnp.repeat(marks, WIN, axis=1), WIN, axis=2)
    valid = valid.reshape(batches, 1, tokens).astype(f32)
    blocks_wide = (row_count + WIN) // WIN
    cell = jnp.arange(CELLS)
    frame_row = qi * row_count - WIN // 2 + jnp.arange(blocks_wide)[:, None] * WIN + cell // WIN
    inside = (frame_row >= 0) & (frame_row < row_count * ns)
    side_of = (cell % WIN) < WIN // 2
    same = side_of[:, None] == side_of[None, :]
    mask = jnp.where(inside[:, None, :] & same[None], 0.0, hidden_value).astype(f32)

    pages = patches.reshape(batches, tokens, D)
    given = patch_cotangent.reshape(batches, tokens, D)

    def widened(edge_source):
        top = lax.ppermute(
            edge_source[:, tokens - RIM :], "seq", [(j, j + 1) for j in range(ns - 1)]
        )
        bottom = lax.ppermute(edge_source[:, :RIM], "seq", [(j + 1, j) for j in range(ns - 1)])
        return jnp.concatenate([top, edge_source, bottom], axis=1)

    def pieces(unit):
        return [(piece, ANY) for piece in unit]

    def shaped(shape, dtype, batched=True):
        return (shape, dtype, per_batch(shape) if batched else whole(shape))

    def batched(a):
        return (a, per_batch(a.shape))

    def full(a):
        return (a, whole(a.shape))

    dma = pltpu.SemaphoreType.DMA

    def forward(layer, x, query, query_parts):
        u = units[layer]
        shifted = layer == 1
        wide_x = widened(x) if shifted else x
        wide = wide_x.shape[1]
        blocks = wide // CELLS
        ins = [(order_c, SMEM), (order_r, SMEM), batched(wide_x)]
        if shifted:
            ins.append(full(mask))
        h1, qkv, probs, mixed, part, gains = run(
            partial(attn_forward, n, shifted),
            "attn_forward",
            (batches,),
            ins + pieces(u[0]) + pieces(u[1]),
            [
                shaped((batches, tokens, D), bf16),
                shaped((batches, wide, 3 * HALF), bf16),
                shaped((batches, blocks * HH, CELLS, CELLS), bf16),
                shaped((batches, tokens, HALF), bf16),
                shaped((batches, tokens, D), bf16),
                shaped((8, D), f32, False),
            ],
            [
                pltpu.VMEM((D, 128 + 3 * HALF), bf16),
                pltpu.VMEM((HALF, D), bf16),
                pltpu.VMEM((wide, HALF), f32),
                pltpu.VMEM((wide, D), f32),
                dma,
                dma,
            ],
            2e9,
        )
        other = swap(part)
        q_ins = [(order_c, SMEM), full(query), full(gains)]
        q_outs = [
            shaped((batches, NQ, D), bf16, False),
            shaped((batches, NQ, HALF), bf16, False),
        ]
        if query_parts is not None:
            q_ins += [full(query_parts[0]), full(query_parts[1]), full(live)]
            q_outs = [shaped((batches, NQ, D), bf16, False)] + q_outs
        got = run(
            partial(query_in, n, query_parts is not None),
            "query_in",
            (),
            q_ins + pieces(u[2]),
            q_outs,
            [pltpu.VMEM((D, HALF), bf16), dma],
            2e8,
        )
        if query_parts is not None:
            query, got = got[0], got[1:]
        hq, cq_now = got
        first, h2, slope, act, second_part, ckv, e, o, stat = run(
            partial(mlp_forward, n),
            "mlp_forward",
            (batches,),
            [
                (order_c, SMEM),
                (order_r, SMEM),
                batched(x),
                batched(part),
                batched(other),
                full(gains),
                batched(cq_now),
                batched(valid),
            ]
            + pieces(u[2])
            + pieces(u[3]),
            [
                shaped((batches, tokens, D), f32),
                shaped((batches, tokens, D), bf16),
                shaped((batches, tokens, hid), bf16),
                shaped((batches, tokens, hid), bf16),
                shaped((batches, tokens, D), bf16),
                shaped((batches, tokens, D), bf16),
                shaped((batches, HH, NQ, tokens), bf16),
                shaped((batches, NQ, HALF), bf16),
                shaped((batches, 16, NQ), f32),
            ],
            [pltpu.VMEM((D, hid + D), bf16), pltpu.VMEM((hid, D), bf16), dma, dma],
            4e9,
        )
        second_other = swap(second_part)
        os = [o] + [across(o, r) for r in range(1, ns)]
        stats = [stat] + [across(stat, r) for r in range(1, ns)]
        att, att_low, coef, q_part = run(
            partial(query_out, n, ns),
            "query_out",
            (),
            [(order_r, SMEM), (order_s, SMEM)]
            + [full(a) for a in os]
            + [full(a) for a in stats]
            + pieces(u[3]),
            [
                shaped((batches, NQ, HALF), f32, False),
                shaped((batches, NQ, HALF), bf16, False),
                shaped((batches, NQ, 128), f32, False),
                shaped((batches, NQ, D), bf16, False),
            ],
            [
                pltpu.VMEM((HALF, D), bf16),
                pltpu.VMEM((ns, batches, NQ, HALF), bf16),
                pltpu.VMEM((ns, batches, 16, NQ), f32),
                dma,
            ],
            2e8,
        )
        q_other = swap(q_part)
        x_next = (first + (second_part.astype(f32) + second_other.astype(f32))).astype(bf16)
        kept = dict(
            x=x, query=query, h1=h1, qkv=qkv, probs=probs, mixed=mixed, gains=gains, hq=hq,
            cq=cq_now, first=first, h2=h2, slope=slope, act=act, ckv=ckv, e=e, att=att,
            att_low=att_low, coef=coef,
        )
        return x_next, (q_part, q_other), kept

    def sums(kernel_plan, order_by, sides, shapes, height, name):
        outs = [shaped(shape, bf16, False) for shape in shapes for _ in range(n)]
        flat = run(
            partial(weight_grads, n, kernel_plan, order_by),
            name,
            (),
            [(order_c, SMEM), (order_r, SMEM)] + [full(s) for s in sides],
            outs,
            [pltpu.VMEM((height, 384), f32)],
            4e9,
        )
        return [flat[k * n : (k + 1) * n] for k in range(len(shapes))]

    def reduce_xy(parts, by_y):
        own, one, two, three = parts
        if by_y:
            got_one, got_three = across(one, 1), across(three, 1)
            got_two = across(two + got_three, 2)
        else:
            got_two, got_three = across(two, 2), across(three, 2)
            got_one = across(one + got_three, 1)
        return own.astype(f32) + got_one.astype(f32) + got_two.astype(f32)

    def reduce_col(parts, by_y):
        if not manual:
            return lax.psum_scatter(
                parts[0][0], ("dp", "seq"), scatter_dimension=0, tiled=True
            ).astype(f32)
        mine = reduce_xy(parts, by_y)
        total = mine[0]
        for r in range(1, nz):
            total = total + lax.ppermute(
                mine[r].astype(bf16), "dp", [(j, j ^ r) for j in range(nz)]
            ).astype(f32)
        return total

    def reduce_row(parts, by_y, splits):
        if not manual:
            out = []
            at = 0
            for height in splits:
                part = parts[0][0][at : at + height * nz * ns // 2]
                at += height * nz * ns // 2
                both = lax.all_gather(part, "section", axis=0, tiled=True)
                out.append(
                    lax.psum_scatter(both, ("dp", "seq"), scatter_dimension=0, tiled=True).astype(f32)
                )
            return out
        mine = reduce_xy(parts, by_y)
        total = mine[0]
        for r in range(1, nz):
            pairs = [
                (c * nz + (j ^ r), c * nz + j)
                for c in range(2)
                for j in range(c * near, (c + 1) * near)
            ]
            total = total + lax.ppermute(
                mine[r % near].astype(bf16), ("section", "dp"), pairs
            ).astype(f32)
        out = []
        at = 0
        for height in splits:
            out.append(total[at : at + height])
            at += height
        return out

    share = 1.0 / ns
    height_down = hid // (nz * ns // 2) if manual else hid
    height_out = HALF // (nz * ns // 2) if manual else HALF
    slots_c, rows_c = (nz, rows) if manual else (1, D)
    slots_r = near if manual else 1

    def backward(layer, grad_patch, grad_query, kept):
        u = units[layer]
        shifted = layer == 1
        gains = kept["gains"]
        du, dckv, dcq_part, part, dcross = run(
            partial(mlp_backward, n),
            "mlp_backward",
            (batches,),
            [(order_c, SMEM), (order_r, SMEM)]
            + [
                batched(a)
                for a in (
                    grad_patch, kept["slope"], kept["e"], kept["coef"], grad_query, live,
                    kept["att"], kept["cq"], kept["ckv"],
                )
            ]
            + pieces(u[2])
            + pieces(u[3]),
            [
                shaped((batches, tokens, hid), bf16),
                shaped((batches, tokens, D), bf16),
                shaped((batches, NQ, HALF), bf16),
                shaped((batches, tokens, D), bf16),
                shaped((batches, NQ, D), bf16),
            ],
            [
                pltpu.VMEM((D, hid + D), bf16),
                pltpu.VMEM((hid, D), bf16),
                pltpu.VMEM((HALF, D), bf16),
                dma,
                dma,
                dma,
            ],
            4e9,
        )
        other = swap(part)
        dcq_all = [dcq_part] + [across(dcq_part, r) for r in range(1, ns)]

        def flat(a):
            return a.reshape(-1, a.shape[-1])

        early_c, early_r = sums(
            (
                (0, 1, 0, rows_c, 0, 0),
                (0, 2, 0, rows_c, 0, hid),
                (3, 4, 1, height_down, 0, 0),
                (5, 6, 1, height_out, height_down, 0),
            ),
            "cr",
            [
                flat(kept["h2"]), flat(du), flat(dckv), flat(kept["act"]), flat(grad_patch),
                flat(kept["att_low"]), flat(dcross * jnp.asarray(share, bf16)),
            ],
            [(slots_c, rows_c, hid + D), (slots_r, height_down + height_out, D)],
            hid,
            "early_grads",
        )
        grad_first, first_low, grad_mixed, dg_mlp = run(
            partial(first_backward, n),
            "first_backward",
            (batches,),
            [(order_r, SMEM)]
            + [batched(a) for a in (grad_patch, part, other, kept["first"])]
            + [full(gains)]
            + pieces(u[1]),
            [
                shaped((batches, tokens, D), f32),
                shaped((batches, tokens, D), bf16),
                shaped((batches, tokens, HALF), bf16),
                shaped((8, D), f32, False),
            ],
            [pltpu.VMEM((HALF, D), bf16), dma],
            4e8,
        )
        wide_grad = widened(grad_mixed) if shifted else grad_mixed
        wide = wide_grad.shape[1]
        dqkv, part = run(
            partial(attn_backward, n),
            "attn_backward",
            (batches,),
            [(order_c, SMEM)]
            + [batched(a) for a in (wide_grad, kept["qkv"], kept["probs"])]
            + pieces(u[0]),
            [shaped((batches, tokens, 3 * HALF), bf16), shaped((batches, tokens, D), bf16)],
            [pltpu.VMEM((D, 3 * HALF), bf16), pltpu.VMEM((wide, 3 * HALF), f32), dma],
            2e9,
        )
        other = swap(part)
        dcq, q_part = run(
            partial(query_back_one, n, ns),
            "query_back_one",
            (),
            [(order_c, SMEM), (order_s, SMEM)] + [full(a) for a in dcq_all] + pieces(u[2]),
            [shaped((batches, NQ, HALF), bf16, False), shaped((batches, NQ, D), bf16, False)],
            [pltpu.VMEM((D, HALF), bf16), pltpu.VMEM((ns, batches, NQ, HALF), bf16), dma],
            2e8,
        )
        q_other = swap(q_part)
        late_c, late_r = sums(
            (
                (0, 1, 0, rows_c, 0, 0),
                (2, 3, 0, rows_c, 0, 3 * HALF),
                (4, 5, 1, height_out, 0, 0),
            ),
            "cr",
            [
                flat(kept["h1"]), flat(dqkv), flat(kept["hq"]), flat(dcq * jnp.asarray(share, bf16)),
                flat(kept["mixed"]), flat(first_low),
            ],
            [(slots_c, rows_c, 4 * HALF), (slots_r, height_out, D)],
            D,
            "late_grads",
        )
        dx, dg_attn = run(
            input_backward,
            "input_backward",
            (batches,),
            [batched(a) for a in (kept["x"], grad_first, part, other)] + [full(gains)],
            [shaped((batches, tokens, D), bf16), shaped((8, D), f32, False)],
            [],
            1e8,
        )
        dq, dg_query = run(
            query_back_two,
            "query_back_two",
            (),
            [full(a) for a in (kept["query"], grad_query, q_part, q_other, gains)],
            [shaped((batches, NQ, D), bf16, False), shaped((8, D), f32, False)],
            [],
            1e8,
        )
        dgains = jnp.concatenate([dg_attn[0:1], dg_mlp[0:1], dg_query[0:1] * share], axis=0)
        return dx, dq, dgains, (early_c, early_r, late_c, late_r)

    x1, q_parts, kept0 = forward(0, pages, query_start, None)
    x2, q_parts_two, kept1 = forward(1, x1, query_start, q_parts)
    query_last = (
        kept1["query"].astype(f32)
        + live * (q_parts_two[0].astype(f32) + q_parts_two[1].astype(f32))
    ).astype(bf16)
    dx1, dq1, dgains1, raw1 = backward(1, given, query_given, kept1)
    down_rows, out_rows = mlp_down.shape[1], attn_output.shape[1]

    def reduced(raw):
        early_c, early_r, late_c, late_r = raw
        return (
            [reduce_col(early_c, True)]
            + reduce_row(early_r, False, (down_rows, out_rows))
            + [reduce_col(late_c, False)]
            + reduce_row(late_r, True, (out_rows,))
        )

    res1 = reduced(raw1)
    sent1 = [lax.ppermute(r, "section", [(0, 1)]) for r in res1]
    dx0, dq0, dgains0, raw0 = backward(0, dx1, dq1, kept0)
    res0 = reduced(raw0)
    sent0 = [lax.ppermute(r, "section", [(1, 0)]) for r in res0]

    def col_halves(k):
        low = jnp.where(core_zero, res0[k], sent1[k])
        high = jnp.where(core_zero, sent0[k], res1[k])
        return low, high

    holder = zi // near if manual else core

    def row_block(k):
        own = jnp.where(core_zero, res0[k], res1[k])
        sent = jnp.where(core_zero, sent0[k], sent1[k])
        return jnp.where(holder == core, own, sent)

    low, high = col_halves(0)
    grad_up = jnp.concatenate([low[:, :hid], high[:, :hid]], axis=1)
    grad_pair = jnp.concatenate(
        [
            low[:, hid : hid + HALF], high[:, hid : hid + HALF],
            low[:, hid + HALF :], high[:, hid + HALF :],
        ],
        axis=1,
    )
    low, high = col_halves(3)
    grad_in = jnp.concatenate(
        [side[:, k * HALF : (k + 1) * HALF] for k in range(3) for side in (low, high)], axis=1
    )
    grad_cq = jnp.concatenate([low[:, 3 * HALF :], high[:, 3 * HALF :]], axis=1)
    grad_down, grad_co, grad_out = row_block(1), row_block(2), row_block(4)

    gain_sums = jnp.concatenate([dgains0, dgains1, jnp.zeros((2, D), f32)], axis=0)
    if manual:
        for axis, count in (("seq", ns), ("dp", nz)):
            base = gain_sums
            for r in range(1, count):
                gain_sums = gain_sums + lax.ppermute(
                    base, axis, [(j, j ^ r) for j in range(count)]
                )
    else:
        gain_sums = lax.psum(gain_sums, ("dp", "seq"))
    mine = jnp.where(core_zero, gain_sums[0:3], gain_sums[3:6])
    mine = lax.dynamic_slice_in_dim(mine, (zi * ns + qi) * rows, rows, axis=1)

    patch_ends = jnp.where(core_zero, dx0, x2).reshape(1, batches, row_count, col_count, D)
    query_ends = jnp.take(jnp.where(core_zero, dq0, query_last), plan[0], axis=0)[None]
    return (
        patch_ends,
        query_ends,
        mine[0:1],
        mine[1:2],
        mine[2:3],
        grad_in[None],
        grad_out[None],
        grad_up[None],
        grad_down[None],
        grad_cq[None],
        grad_pair[None],
        grad_co[None],
    )


def solution(mesh):
    return jax.shard_map(
        per_device,
        mesh=mesh,
        in_specs=(
            P("dp", "seq", None, None),
            P("dp", None, None),
            P("dp"),
            P("dp", "seq", None),
            P("dp"),
            P("dp", None),
            P("section", ("dp", "seq")),
            P("section", ("dp", "seq")),
            P("section", ("dp", "seq")),
            P("section", ("dp", "seq"), None),
            P("section", ("dp", "seq"), None),
            P("section", ("dp", "seq"), None),
            P("section", ("dp", "seq"), None),
            P("section", ("dp", "seq"), None),
            P("section", ("dp", "seq"), None),
            P("section", ("dp", "seq"), None),
            P("dp", "seq", None, None),
            P("dp", None, None),
        ),
        out_specs=(
            P("section", "dp", "seq", None, None),
            P("section", "dp", None, None),
            P("section", ("dp", "seq")),
            P("section", ("dp", "seq")),
            P("section", ("dp", "seq")),
            P("section", ("dp", "seq"), None),
            P("section", ("dp", "seq"), None),
            P("section", ("dp", "seq"), None),
            P("section", ("dp", "seq"), None),
            P("section", ("dp", "seq"), None),
            P("section", ("dp", "seq"), None),
            P("section", ("dp", "seq"), None),
        ),
        check_vma=False,
    )
```

time: 2980 us -> 776 us (0.26)
  waiting for transfers between devices: 2000 us -> 306 us
  matrix products: 301 us -> 0 us
  local copies, waits for them, and re-layouts: 279 us -> 34.4 us
  Pallas kernels: 0 us -> 176 us
  blocking collectives: 120 us -> 0 us
  starting transfers between devices: 94.6 us -> 209 us
  other arithmetic: 94.5 us -> 38.9 us
  loops' own time: 48.3 us -> 0 us
    reduce_scatter x7 -> x0, waiting for transfers between devices: 1050 us -> none  [the longest x1 177 us: per_device(): lax.psum_scatter(grad_totals[6][None], ('dp', 'seq'), scatter_dimension=1...]
    all_gather x7 -> x0, waiting for transfers between devices: 310 us -> none  [the longest x1 76.7 us: per_device(): lax.all_gather(mlp_up, ('dp', 'seq'), axis=1, tiled=True)]
    dot_general x82 -> x0, matrix products: 277 us -> none  [the longest x21 82.9 us: times_transpose(): lax.dot_general(left_side, right_side, (((1,), (1,)), ((), ())), preferre...]
    unnamed x24 -> x0, waiting for transfers between devices: 276 us -> none
    pallas_call x0 -> x24, Pallas kernels: none -> 176 us  [run(): pl.pallas_call(kernel, grid=grid, in_specs=[s for _, s in ins], out_specs...]
    ppermute x20 -> x150, starting transfers between devices: 92.1 us -> 209 us  [the longest x66 77.8 us: across(): return lax.ppermute(x, 'seq', [(j, j ^ r) for j in range(ns)])]
    psum x4 -> x0, waiting for transfers between devices: 104 us -> none  [the longest x2 59.8 us: layer_backward(): grad_proj = lax.psum(query_part.astype(jnp.bfloat16), 'seq')]
    slice x62 -> x21, local copies, waits for them, and re-layouts: 61 us -> 4.31 us  [the longest x3 1.99 us: columns(): return [a[:, half * w:(half + 1) * w] for a, w in arrays]]
  transfers between devices with their start and end apart: 41 -> 150, of which waited for: 29 -> 48; matrix products, arithmetic and copies ran while one was open for 16% -> 7% of each run, Pallas kernels for 0% -> 19%
where the time goes in v1:
time: 776 us; the launch traced here: 767 us
  waiting for transfers between devices  306 us (39%)
  starting transfers between devices  209 us (27%)
  Pallas kernels  176 us (23%)
  other arithmetic  38.9 us (5%)
  local copies, waits for them, and re-layouts  34.4 us (4%)
    pallas_call x24, Pallas kernels, run(): pl.pallas_call(kernel, grid=grid, in_specs=[s for _, s in ins], out_specs...  176 us
    ppermute x66, waiting for transfers between devices, across(): return lax.ppermute(x, 'seq', [(j, j ^ r) for j in range(ns)])  169 us
    ppermute x66, starting transfers between devices, across(): return lax.ppermute(x, 'seq', [(j, j ^ r) for j in range(ns)])  77.8 us
    ppermute x12, waiting for transfers between devices, reduce_row(): lax.ppermute(mine[r % near].astype(bf16), ('section', 'dp'), pairs)  68.3 us
    ppermute x12, starting transfers between devices, gather_row(): got.append(lax.ppermute(unit, ('section', 'dp'), pairs))  34.1 us
    ppermute x12, starting transfers between devices, reduce_row(): lax.ppermute(mine[r % near].astype(bf16), ('section', 'dp'), pairs)  29.1 us
    ppermute x12, starting transfers between devices, gather_col(): lax.ppermute(unit, 'dp', [(j, j ^ r) for j in range(nz)])  20.5 us
    unnamed x242, local copies, waits for them, and re-layouts  20.1 us
  transfers between devices with their start and end apart: 150, of which 48 were waited for; matrix products, arithmetic and copies ran while one was open for 7% of the time, Pallas kernels for 19%

profile of v1, /device:TPU:0, one launch (start us, length us, event | category | flops | bytes accessed | tf_op | source)
XLA Modules:
  0.0 767.2 jit_solution(18153296365023638009)
XLA Ops:
  5.1 4.9 collective-permute-start.8
  12.1 3.0 collective-permute-start.3
  18.3 4.0 collective-permute-done.2
  23.8 5.2 collective-permute-start.9
  32.6 12.4 %collective-permute-done.17 = bf16[48,2688]{1,0:T(8,128)(2,1)S(1)} collective-permute-done((bf16[48,2688]{1,0:T(8,128)(2,1)S(1)}, bf16[48,2688]{1,0:T(8,128)(2,1)S(1)}, u32[]{:S(2)}, u32[]{:S(2)}) %collective-permute-start.17) | collective-permute-done | bytes 258080 | tf_op jit(solution)/shard_map/ppermute | solution.py:554
  46.8 5.7 collective-permute-start.23
  68.3 15.2 %collective-permute-done.12.refs_9_.refs_8_ = bf16[2,48,768]{2,1,0:T(8,128)(2,1)S(1)} collective-permute-done((bf16[2,48,768]{2,1,0:T(8,128)(2,1)S(1)}, bf16[2,48,768]{2,1,0:T(8,128)(2,1)S(1)}, u32[]{:S(2)}, u32[]{:S(2)}) %collective-permute-start.12) | collective-permute-done | bytes 147488 | tf_op jit(solution)/shard_map/ppermute | solution.py:507
  86.8 19.2 %collective-permute-done.13.refs_10_.refs_9_ = bf16[2,48,768]{2,1,0:T(8,128)(2,1)S(1)} collective-permute-done((bf16[2,48,768]{2,1,0:T(8,128)(2,1)S(1)}, bf16[2,48,768]{2,1,0:T(8,128)(2,1)S(1)}, u32[]{:S(2)}, u32[]{:S(2)}) %collective-permute-start.13) | collective-permute-done | bytes 147488 | tf_op jit(solution)/shard_map/ppermute | solution.py:507
  114.8 10.0 %attn_forward.2 = (bf16[2,288,768]{2,1,0:T(8,128)(2,1)}, bf16[2,288,1152]{2,1,0:T(8,128)(2,1)}, bf16[2,12,144,144]{3,2,1,0:T(8,128)(2,1)}, bf16[2,288,384]{2,1,0...) custom-call(s32[16]{0:T(128)S(1)} %stack.253.refs_0_, s32[8]{0:T(128)S(1)} %stack.236.refs_1_.refs_0_, ...), custom_call_target="tpu_custom_call" | custom-call | flops 2000000000 | bytes 3440736 | tf_op jit(solution)/shard_map/attn_forward/pallas_call | solution.py:43
  135.9 5.0 collective-permute-done.21.refs_6_.refs_11_.refs_14_.refs_9_
  140.8 8.1 %collective-permute-start.33 = (bf16[48,1280]{1,0:T(8,128)(2,1)}, bf16[48,1280]{1,0:T(8,128)(2,1)S(1)}, u32[]{:S(2)}, u32[]{:S(2)}) collective-permute-start(bf16[48,1280]{1,0:T(8,128)(2,1)} %get-tuple-element.321), channel_id=1, source_target_pairs={{0,8},{4,12},{8,0},{12,4},{1,9},{5,13},{9,1},{13,5},{2,10},{6,14},... | collective-permute-start | bytes 368648 | tf_op jit(solution)/shard_map/ppermute | solution.py:554
  152.5 3.8 collective-permute-start.53
  156.3 6.3 collective-permute-done.28.refs_15_.refs_13_.refs_18_
  162.7 13.4 %mlp_forward.2 = (f32[2,288,768]{2,1,0:T(8,128)}, bf16[2,288,768]{2,1,0:T(8,128)(2,1)}, bf16[2,288,1536]{2,1,0:T(8,128)(2,1)}, bf16[2,288,1536]{2,1,0:T(8,128)(2...) custom-call(s32[16]{0:T(128)S(1)} %stack.253.refs_0_, ...), custom_call_target="tpu_custom_call" | custom-call | flops 4000000000 | bytes 9955680 | tf_op jit(solution)/shard_map/mlp_forward/pallas_call | solution.py:43
  176.1 3.9 collective-permute-start.58
  200.7 18.4 %collective-permute-done.43.refs_11_.refs_9_ = bf16[2,48,768]{2,1,0:T(8,128)(2,1)S(1)} collective-permute-done((bf16[2,48,768]{2,1,0:T(8,128)(2,1)S(1)}, bf16[2,48,768]{2,1,0:T(8,128)(2,1)S(1)}, u32[]{:S(2)}, u32[]{:S(2)}) %collective-permute-start.43) | collective-permute-done | bytes 147488 | tf_op jit(solution)/shard_map/ppermute | solution.py:507
  220.0 7.4 collective-permute-done.36.refs_6_
  228.7 8.3 %collective-permute-done.37.refs_7_ = bf16[4,48,1280]{2,1,0:T(8,128)(2,1)S(1)} collective-permute-done((bf16[4,48,1280]{2,1,0:T(8,128)(2,1)S(1)}, bf16[4,48,1280]{2,1,0:T(8,128)(2,1)S(1)}, u32[]{:S(2)}, u32[]{:S(2)}) %collective-permute-start.37) | collective-permute-done | bytes 491552 | tf_op jit(solution)/shard_map/ppermute | solution.py:507
  242.2 4.5 collective-permute-done.30
  246.8 4.9 collective-permute-start.50
  253.3 3.1 collective-permute-start.45
  257.8 3.4 collective-permute-start.47
  261.2 13.1 %attn_forward.3 = (bf16[2,288,768]{2,1,0:T(8,128)(2,1)}, bf16[2,432,1152]{2,1,0:T(8,128)(2,1)}, bf16[2,18,144,144]{3,2,1,0:T(8,128)(2,1)}, bf16[2,288,384]{2,1,0...) custom-call(s32[16]{0:T(128)S(1)} %stack.253.refs_0_, s32[8]{0:T(128)S(1)} %stack.236.refs_1_.refs_0_, ...), custom_call_target="tpu_custom_call" | custom-call | flops 2000000000 | bytes 4131936 | tf_op jit(solution)/shard_map/attn_forward/pallas_call | solution.py:43
  275.2 9.3 %collective-permute-done.47.refs_5_ = bf16[2,128,384]{2,1,0:T(8,128)(2,1)S(1)} collective-permute-done((bf16[2,128,384]{2,1,0:T(8,128)(2,1)S(1)}, bf16[2,128,384]{2,1,0:T(8,128)(2,1)S(1)}, u32[]{:S(2)}, u32[]{:S(2)}) %collective-permute-start.47) | collective-permute-done | bytes 196640 | tf_op jit(solution)/shard_map/ppermute | solution.py:507
  287.4 3.1 query_out.2
  298.1 15.1 %collective-permute-done.63.refs_15_.refs_13_.refs_18_ = bf16[2,240,768]{2,1,0:T(8,128)(2,1)S(1)} collective-permute-done((bf16[2,240,768]{2,1,0:T(8,128)(2,1)S(1)}, bf16[2,240,768]{2,1,0:T(8,128)(2,1)S(1)}, u32[]{:S(2)}, u32[]{:S(2)}) %collective-permute-start.63) | collective-permute-done | bytes 737312 | tf_op jit(solution)/shard_map/ppermute | solution.py:507
  314.3 13.3 %mlp_forward.3 = (f32[2,288,768]{2,1,0:T(8,128)}, bf16[2,288,768]{2,1,0:T(8,128)(2,1)}, bf16[2,288,1536]{2,1,0:T(8,128)(2,1)}, bf16[2,288,1536]{2,1,0:T(8,128)(2...) custom-call(s32[16]{0:T(128)S(1)} %stack.253.refs_0_, ...), custom_call_target="tpu_custom_call" | custom-call | flops 4000000000 | bytes 9955680 | tf_op jit(solution)/shard_map/mlp_forward/pallas_call | solution.py:43
  332.6 6.3 collective-permute-done.67.refs_7_
  343.6 3.1 query_out.3
  346.7 14.2 %mlp_backward.2 = (bf16[2,288,1536]{2,1,0:T(8,128)(2,1)}, bf16[2,288,768]{2,1,0:T(8,128)(2,1)}, bf16[2,128,384]{2,1,0:T(8,128)(2,1)S(1)}, bf16[2,288,768]{2,1,0:T(8,128)(2,1)}, bf16[2,128,768]{2,1,0:T(8,128)(2,1)S(1)}) custom-call(s32[16]{0:T(128)S(1)} %stack.253.refs_0_, s32[8]{0:T(128)S(1)} %stack.236.refs_1_.refs_0_, ...), custom_call_target="tpu_custom_call" | custom-call | flops 4000000000 | bytes 12616800 | tf_op jit(solution)/shard_map/mlp_backward/pallas_call | solution.py:43
  368.6 11.2 %early_grads.3 = (bf16[4,48,2304]{2,1,0:T(8,128)(2,1)}, bf16[4,48,2304]{2,1,0:T(8,128)(2,1)}, bf16[4,48,2304]{2,1,0:T(8,128)(2,1)}, bf16[4,48,2304]{2,1,0:T(8,12...) custom-call(s32[16]{0:T(128)S(1)} %stack.253.refs_0_, ...), custom_call_target="tpu_custom_call" | custom-call | flops 4000000000 | bytes 6783072 | tf_op jit(solution)/shard_map/early_grads/pallas_call | solution.py:43
  384.1 5.3 first_backward.2
  389.4 3.8 collective-permute-start.71
  394.6 7.6 collective-permute-done.71
  402.2 4.6 collective-permute-done.72
  407.7 16.8 %attn_backward.2 = (bf16[2,288,1152]{2,1,0:T(8,128)(2,1)}, bf16[2,288,768]{2,1,0:T(8,128)(2,1)}) custom-call(s32[16]{0:T(128)S(1)} %stack.253.refs_0_, bf16[2,432,384]{2,1,0:T(8,128)(2,1)} %pad_maximum_fusion.3.refs_1_, bf16[2,432,1152]{2,1,0:T(8,128)(2,1)} %get-tuple-element.144.refs_2_, bf16[2,18,144,144]{3,2,1,0:T(8,128)(2,1)} %get-tuple-element.145.refs_3_, ...), custom_call_target="tpu_custom_call" | custom-call | flops 2000000000 | bytes 6113344 | tf_op jit(solution)/shard_map/attn_backward/pallas_call | solution.py:43
  424.5 5.8 late_grads.3
  432.4 3.7 collective-permute-done.113
  444.6 5.4 collective-permute-start.115
  458.7 6.7 collective-permute-done.117
  467.0 20.8 %collective-permute-done.98 = bf16[4,48,1536]{2,1,0:T(8,128)(2,1)S(1)} collective-permute-done((bf16[4,48,1536]{2,1,0:T(8,128)(2,1)S(1)}, bf16[4,48,1536]{2,1,0:T(8,128)(2,1)S(1)}, u32[]{:S(2)}, u32[]{:S(2)}) %collective-permute-start.98) | collective-permute-done | bytes 589856 | tf_op jit(solution)/shard_map/ppermute | solution.py:507
  487.8 5.2 collective-permute-start.143
  497.0 4.9 collective-permute-done.143
  504.4 22.1 %collective-permute-done.144 = bf16[240,768]{1,0:T(8,128)(2,1)S(1)} collective-permute-done((bf16[240,768]{1,0:T(8,128)(2,1)S(1)}, bf16[240,768]{1,0:T(8,128)(2,1)S(1)}, u32[]{:S(2)}, u32[]{:S(2)}) %collective-permute-start.144) | collective-permute-done | bytes 368672 | tf_op jit(solution)/shard_map/ppermute | solution.py:818
  529.3 3.3 input_backward.2
  533.5 14.0 %mlp_backward.3 = (bf16[2,288,1536]{2,1,0:T(8,128)(2,1)}, bf16[2,288,768]{2,1,0:T(8,128)(2,1)}, bf16[2,128,384]{2,1,0:T(8,128)(2,1)S(1)}, bf16[2,288,768]{2,1,0:T(8,128)(2,1)}, bf16[2,128,768]{2,1,0:T(8,128)(2,1)S(1)}) custom-call(s32[16]{0:T(128)S(1)} %stack.253.refs_0_, s32[8]{0:T(128)S(1)} %stack.236.refs_1_.refs_0_, bf16[2,288,768]{2,1,0:T(8,128)(2,1)} %copy-done.7, ...), custom_call_target="tpu_custom_call" | custom-call | flops 4000000000 | bytes 12616800 | tf_op jit(solution)/shard_map/mlp_backward/pallas_call | solution.py:43
  549.1 11.3 %early_grads.2 = (bf16[4,48,2304]{2,1,0:T(8,128)(2,1)}, bf16[4,48,2304]{2,1,0:T(8,128)(2,1)}, bf16[4,48,2304]{2,1,0:T(8,128)(2,1)}, bf16[4,48,2304]{2,1,0:T(8,12...) custom-call(s32[16]{0:T(128)S(1)} %stack.253.refs_0_, ...), custom_call_target="tpu_custom_call" | custom-call | flops 4000000000 | bytes 6783072 | tf_op jit(solution)/shard_map/early_grads/pallas_call | solution.py:43
  564.0 4.3 collective-permute-done.82.refs_4_
  572.9 5.5 first_backward.3
  579.2 13.4 %attn_backward.3 = (bf16[2,288,1152]{2,1,0:T(8,128)(2,1)}, bf16[2,288,768]{2,1,0:T(8,128)(2,1)}) custom-call(s32[16]{0:T(128)S(1)} %stack.253.refs_0_, bf16[2,288,384]{2,1,0:T(8,128)(2,1)S(1)} %get-tuple-element.159.refs_1_, bf16[2,288,1152]{2,1,0:T(8,128)(2,1)} %get-tuple-element.160.refs_2_, bf16[2,12,144,144]{3,2,1,0:T(8,128)(2,1)} %get-tuple-element.161.refs_3_, ...), custom_call_target="tpu_custom_call" | custom-call | flops 2000000000 | bytes 4730944 | tf_op jit(solution)/shard_map/attn_backward/pallas_call | solution.py:43
  592.6 5.9 late_grads.2
  601.8 3.4 collective-permute-done.107
  611.8 5.2 collective-permute-start.109
  623.5 3.2 collective-permute-done.110
  640.1 7.1 collective-permute-done.135
  655.4 6.6 collective-permute-done.120
  668.5 3.2 collective-permute-start.89
  684.4 7.1 collective-permute-done.137
  692.6 22.0 %collective-permute-done.138 = bf16[240,768]{1,0:T(8,128)(2,1)S(1)} collective-permute-done((bf16[240,768]{1,0:T(8,128)(2,1)S(1)}, bf16[240,768]{1,0:T(8,128)(2,1)S(1)}, u32[]{:S(2)}, u32[]{:S(2)}) %collective-permute-start.138) | collective-permute-done | bytes 368672 | tf_op jit(solution)/shard_map/ppermute | solution.py:818
  718.1 5.7 collective-permute-done.124
  729.6 4.0 collective-permute-done.93
  734.1 4.3 collective-permute-start.97
  740.4 10.9 %collective-permute-done.96 = bf16[48,1536]{1,0:T(8,128)(2,1)S(1)} collective-permute-done((bf16[48,1536]{1,0:T(8,128)(2,1)S(1)}, bf16[48,1536]{1,0:T(8,128)(2,1)S(1)}, u32[]{:S(2)}, u32[]{:S(2)}) %collective-permute-start.96) | collective-permute-done | bytes 147488 | tf_op jit(solution)/shard_map/ppermute | solution.py:793
  761.7 3.1 collective-permute-start.104
  (631 shorter events, 249.1 us)
Async XLA Ops:
  5.1 48.6 %collective-permute-start.8 = (bf16[48,768]{1,0:T(8,128)(2,1)S(1)}, bf16[48,768]{1,0:T(8,128)(2,1)S(1)}, u32[]{:S(2)}, u32[]{:S(2)}) collective-permute-start(bf16[48,768]{1,0:T(8,128)(2,1)S(1)} %get-tuple-element.340), channel_id=1, source_target_pairs={{0,4},{4,0},{24,28},{28,24},{1,5},{5,1},{25,29},{29,25},{2,6},{6,2... | collective-permute-start | bytes 221192 | tf_op jit(solution)/shard_map/ppermute | solution.py:567
  22.3 22.7 %collective-permute-start.17 = (bf16[48,2688]{1,0:T(8,128)(2,1)S(1)}, bf16[48,2688]{1,0:T(8,128)(2,1)S(1)}, u32[]{:S(2)}, u32[]{:S(2)}) collective-permute-start(bf16[48,2688]{1,0:T(8,128)(2,1)S(1)} %get-tuple-element.306), channel_id=1, source_target_pairs={{0,8},{4,12},{8,0},{12,4},{1,9},{5,13},{9,1},{13,5},{2,10},{6,14},... | collective-permute-start | bytes 774152 | tf_op jit(solution)/shard_map/ppermute | solution.py:554
  22.3 24.5 %collective-permute-start.18 = (bf16[48,2688]{1,0:T(8,128)(2,1)S(1)}, bf16[48,2688]{1,0:T(8,128)(2,1)S(1)}, u32[]{:S(2)}, u32[]{:S(2)}) collective-permute-start(bf16[48,2688]{1,0:T(8,128)(2,1)S(1)} %get-tuple-element.306), channel_id=1, source_target_pairs={{0,12},{4,8},{8,4},{12,0},{1,13},{5,9},{9,5},{13,1},{2,14},{6,10},... | collective-permute-start | bytes 774152 | tf_op jit(solution)/shard_map/ppermute | solution.py:554
  23.8 31.3 %collective-permute-start.9 = (bf16[48,768]{1,0:T(8,128)(2,1)S(1)}, bf16[48,768]{1,0:T(8,128)(2,1)S(1)}, u32[]{:S(2)}, u32[]{:S(2)}) collective-permute-start(bf16[48,768]{1,0:T(8,128)(2,1)S(1)} %get-tuple-element.340), channel_id=1, source_target_pairs={{0,8},{4,12},{24,16},{28,20},{1,9},{5,13},{25,17},{29,21},{2,10},{... | collective-permute-start | bytes 221192 | tf_op jit(solution)/shard_map/ppermute | solution.py:567
  29.9 26.5 %collective-permute-start.10 = (bf16[48,768]{1,0:T(8,128)(2,1)S(1)}, bf16[48,768]{1,0:T(8,128)(2,1)S(1)}, u32[]{:S(2)}, u32[]{:S(2)}) collective-permute-start(bf16[48,768]{1,0:T(8,128)(2,1)S(1)} %get-tuple-element.340), channel_id=1, source_target_pairs={{0,12},{4,8},{24,20},{28,16},{1,13},{5,9},{25,21},{29,17},{2,14},{... | collective-permute-start | bytes 221192 | tf_op jit(solution)/shard_map/ppermute | solution.py:567
  56.4 57.1 %collective-permute-start.20 = (bf16[4,48,2688]{2,1,0:T(8,128)(2,1)}, bf16[4,48,2688]{2,1,0:T(8,128)(2,1)}, u32[]{:S(2)}, u32[]{:S(2)}) collective-permute-start(bf16[4,48,2688]{2,1,0:T(8,128)(2,1)} %pad_maximum_fusion.1.refs_3_.refs_8_.refs_11_.refs_6_), channel_id=1, source_target_pairs={{0,2},{1,3},{2,0},{3,1},{4,6},{5,7},{6,4},{7,5},{8,10},{9,11},{10,... | collective-permute-start | bytes 3096584 | tf_op jit(solution)/shard_map/ppermute | solution.py:507
  58.4 25.1 %collective-permute-start.12 = (bf16[2,48,768]{2,1,0:T(8,128)(2,1)S(1)}, bf16[2,48,768]{2,1,0:T(8,128)(2,1)S(1)}, u32[]{:S(2)}, u32[]{:S(2)}) collective-permute-start(bf16[2,48,768]{2,1,0:T(8,128)(2,1)S(1)} %maximum_select_fusion.2.refs_7_.refs_6_), channel_id=1, source_target_pairs={{0,2},{1,3},{2,0},{3,1},{4,6},{5,7},{6,4},{7,5},{8,10},{9,11},{10,... | collective-permute-start | bytes 442376 | tf_op jit(solution)/shard_map/ppermute | solution.py:507
  60.6 24.7 %collective-permute-start.11 = (bf16[2,48,768]{2,1,0:T(8,128)(2,1)S(1)}, bf16[2,48,768]{2,1,0:T(8,128)(2,1)S(1)}, u32[]{:S(2)}, u32[]{:S(2)}) collective-permute-start(bf16[2,48,768]{2,1,0:T(8,128)(2,1)S(1)} %maximum_select_fusion.2.refs_7_.refs_6_), channel_id=1, source_target_pairs={{0,1},{1,0},{2,3},{3,2},{4,5},{5,4},{6,7},{7,6},{8,9},{9,8},{10,11... | collective-permute-start | bytes 442376 | tf_op jit(solution)/shard_map/ppermute | solution.py:507
  62.3 47.9 %collective-permute-start.5 = (bf16[4,48,1280]{2,1,0:T(8,128)(2,1)S(1)}, bf16[4,48,1280]{2,1,0:T(8,128)(2,1)}, u32[]{:S(2)}, u32[]{:S(2)}) collective-permute-start(bf16[4,48,1280]{2,1,0:T(8,128)(2,1)S(1)} %pad_maximum_fusion.4.refs_3_.refs_4_), channel_id=1, source_target_pairs={{0,2},{1,3},{2,0},{3,1},{4,6},{5,7},{6,4},{7,5},{8,10},{9,11},{10,... | collective-permute-start | bytes 1474568 | tf_op jit(solution)/shard_map/ppermute | solution.py:507
  65.5 46.7 %collective-permute-start.6 = (bf16[4,48,1280]{2,1,0:T(8,128)(2,1)}, bf16[4,48,1280]{2,1,0:T(8,128)(2,1)}, u32[]{:S(2)}, u32[]{:S(2)}) collective-permute-start(bf16[4,48,1280]{2,1,0:T(8,128)(2,1)} %collective-permute-done.4.refs_4_.refs_5_), channel_id=1, source_target_pairs={{0,2},{1,3},{2,0},{3,1},{4,6},{5,7},{6,4},{7,5},{8,10},{9,11},{10,... | collective-permute-start | bytes 1474568 | tf_op jit(solution)/shard_map/ppermute | solution.py:507
  83.5 46.6 %collective-permute-start.26 = (bf16[2,240,768]{2,1,0:T(8,128)(2,1)S(1)}, bf16[2,240,768]{2,1,0:T(8,128)(2,1)S(1)}, u32[]{:S(2)}, u32[]{:S(2)}) collective-permute-start(bf16[2,240,768]{2,1,0:T(8,128)(2,1)S(1)} %maximum_select_fusion.refs_12_.refs_10_.refs_15_), channel_id=1, source_target_pairs={{0,1},{1,0},{2,3},{3,2},{4,5},{5,4},{6,7},{7,6},{8,9},{9,8},{10,11... | collective-permute-start | bytes 2211848 | tf_op jit(solution)/shard_map/ppermute | solution.py:507
  85.3 20.7 %collective-permute-start.13 = (bf16[2,48,768]{2,1,0:T(8,128)(2,1)S(1)}, bf16[2,48,768]{2,1,0:T(8,128)(2,1)S(1)}, u32[]{:S(2)}, u32[]{:S(2)}) collective-permute-start(bf16[2,48,768]{2,1,0:T(8,128)(2,1)S(1)} %collective-permute-done.12.refs_9_.refs_8_), channel_id=1, source_target_pairs={{0,1},{1,0},{2,3},{3,2},{4,5},{5,4},{6,7},{7,6},{8,9},{9,8},{10,11... | collective-permute-start | bytes 442376 | tf_op jit(solution)/shard_map/ppermute | solution.py:507
  106.0 26.7 %collective-permute-start.19 = (bf16[4,48,2688]{2,1,0:T(8,128)(2,1)}, bf16[4,48,2688]{2,1,0:T(8,128)(2,1)}, u32[]{:S(2)}, u32[]{:S(2)}) collective-permute-start(bf16[4,48,2688]{2,1,0:T(8,128)(2,1)} %pad_maximum_fusion.1.refs_3_.refs_8_.refs_11_.refs_6_), channel_id=1, source_target_pairs={{0,1},{1,0},{2,3},{3,2},{4,5},{5,4},{6,7},{7,6},{8,9},{9,8},{10,11... | collective-permute-start | bytes 3096584 | tf_op jit(solution)/shard_map/ppermute | solution.py:507
  113.5 27.3 %collective-permute-start.21 = (bf16[4,48,2688]{2,1,0:T(8,128)(2,1)}, bf16[4,48,2688]{2,1,0:T(8,128)(2,1)}, u32[]{:S(2)}, u32[]{:S(2)}) collective-permute-start(bf16[4,48,2688]{2,1,0:T(8,128)(2,1)} %collective-permute-done.20.refs_5_.refs_10_.refs_13_.refs_8_), channel_id=1, source_target_pairs={{0,1},{1,0},{2,3},{3,2},{4,5},{5,4},{6,7},{7,6},{8,9},{9,8},{10,11... | collective-permute-start | bytes 3096584 | tf_op jit(solution)/shard_map/ppermute | solution.py:507
  127.8 24.7 %collective-permute-start.14 = (bf16[2,288,768]{2,1,0:T(8,128)(2,1)}, bf16[2,288,768]{2,1,0:T(8,128)(2,1)}, u32[]{:S(2)}, u32[]{:S(2)}) collective-permute-start(bf16[2,288,768]{2,1,0:T(8,128)(2,1)} %get-tuple-element.122.refs_3_), channel_id=1, source_target_pairs={{0,16},{16,0},{1,17},{17,1},{2,18},{18,2},{3,19},{19,3},{4,20},{20... | collective-permute-start | bytes 2654216 | tf_op jit(solution)/shard_map/ppermute | solution.py:504
  128.9 23.1 %collective-permute-start.27 = (bf16[2,240,768]{2,1,0:T(8,128)(2,1)S(1)}, bf16[2,240,768]{2,1,0:T(8,128)(2,1)}, u32[]{:S(2)}, u32[]{:S(2)}) collective-permute-start(bf16[2,240,768]{2,1,0:T(8,128)(2,1)S(1)} %maximum_select_fusion.refs_12_.refs_10_.refs_15_), channel_id=1, source_target_pairs={{0,2},{1,3},{2,0},{3,1},{4,6},{5,7},{6,4},{7,5},{8,10},{9,11},{10,... | collective-permute-start | bytes 2211848 | tf_op jit(solution)/shard_map/ppermute | solution.py:507
  130.1 32.6 %collective-permute-start.28 = (bf16[2,240,768]{2,1,0:T(8,128)(2,1)S(1)}, bf16[2,240,768]{2,1,0:T(8,128)(2,1)}, u32[]{:S(2)}, u32[]{:S(2)}) collective-permute-start(bf16[2,240,768]{2,1,0:T(8,128)(2,1)S(1)} %collective-permute-done.26.refs_13_.refs_11_.refs_16_), channel_id=1, source_target_pairs={{0,2},{1,3},{2,0},{3,1},{4,6},{5,7},{6,4},{7,5},{8,10},{9,11},{10,... | collective-permute-start | bytes 2211848 | tf_op jit(solution)/shard_map/ppermute | solution.py:507
  140.8 35.3 %collective-permute-start.33 = (bf16[48,1280]{1,0:T(8,128)(2,1)}, bf16[48,1280]{1,0:T(8,128)(2,1)S(1)}, u32[]{:S(2)}, u32[]{:S(2)}) collective-permute-start(bf16[48,1280]{1,0:T(8,128)(2,1)} %get-tuple-element.321), channel_id=1, source_target_pairs={{0,8},{4,12},{8,0},{12,4},{1,9},{5,13},{9,1},{13,5},{2,10},{6,14},... | collective-permute-start | bytes 368648 | tf_op jit(solution)/shard_map/ppermute | solution.py:554
  151.9 28.1 %collective-permute-start.34 = (bf16[48,1280]{1,0:T(8,128)(2,1)}, bf16[48,1280]{1,0:T(8,128)(2,1)S(1)}, u32[]{:S(2)}, u32[]{:S(2)}) collective-permute-start(bf16[48,1280]{1,0:T(8,128)(2,1)} %get-tuple-element.321), channel_id=1, source_target_pairs={{0,12},{4,8},{8,4},{12,0},{1,13},{5,9},{9,5},{13,1},{2,14},{6,10},... | collective-permute-start | bytes 368648 | tf_op jit(solution)/shard_map/ppermute | solution.py:554
  152.0 30.2 %collective-permute-start.52 = (bf16[48,2688]{1,0:T(8,128)(2,1)S(1)}, bf16[48,2688]{1,0:T(8,128)(2,1)S(1)}, u32[]{:S(2)}, u32[]{:S(2)}) collective-permute-start(bf16[48,2688]{1,0:T(8,128)(2,1)S(1)} %copy-done.65), channel_id=1, source_target_pairs={{0,4},{4,0},{8,12},{12,8},{1,5},{5,1},{9,13},{13,9},{2,6},{6,2},{1... | collective-permute-start | bytes 774152 | tf_op jit(solution)/shard_map/ppermute | solution.py:554
  152.5 30.7 %collective-permute-start.53 = (bf16[48,2688]{1,0:T(8,128)(2,1)S(1)}, bf16[48,2688]{1,0:T(8,128)(2,1)S(1)}, u32[]{:S(2)}, u32[]{:S(2)}) collective-permute-start(bf16[48,2688]{1,0:T(8,128)(2,1)S(1)} %copy-done.65), channel_id=1, source_target_pairs={{0,8},{4,12},{8,0},{12,4},{1,9},{5,13},{9,1},{13,5},{2,10},{6,14},... | collective-permute-start | bytes 774152 | tf_op jit(solution)/shard_map/ppermute | solution.py:554
  162.7 21.6 %collective-permute-start.54 = (bf16[48,2688]{1,0:T(8,128)(2,1)S(1)}, bf16[48,2688]{1,0:T(8,128)(2,1)S(1)}, u32[]{:S(2)}, u32[]{:S(2)}) collective-permute-start(bf16[48,2688]{1,0:T(8,128)(2,1)S(1)} %copy-done.65), channel_id=1, source_target_pairs={{0,12},{4,8},{8,4},{12,0},{1,13},{5,9},{9,5},{13,1},{2,14},{6,10},... | collective-permute-start | bytes 774152 | tf_op jit(solution)/shard_map/ppermute | solution.py:554
  189.8 51.2 %collective-permute-start.56 = (bf16[4,48,2688]{2,1,0:T(8,128)(2,1)S(1)}, bf16[4,48,2688]{2,1,0:T(8,128)(2,1)S(1)}, u32[]{:S(2)}, u32[]{:S(2)}) collective-permute-start(bf16[4,48,2688]{2,1,0:T(8,128)(2,1)S(1)} %pad_maximum_fusion.2.refs_6_.refs_8_.refs_11_), channel_id=1, source_target_pairs={{0,2},{1,3},{2,0},{3,1},{4,6},{5,7},{6,4},{7,5},{8,10},{9,11},{10,... | collective-permute-start | bytes 3096584 | tf_op jit(solution)/shard_map/ppermute | solution.py:507
  194.7 32.7 %collective-permute-start.36 = (bf16[4,48,1280]{2,1,0:T(8,128)(2,1)S(1)}, bf16[4,48,1280]{2,1,0:T(8,128)(2,1)S(1)}, u32[]{:S(2)}, u32[]{:S(2)}) collective-permute-start(bf16[4,48,1280]{2,1,0:T(8,128)(2,1)S(1)} %pad_maximum_fusion.5.refs_4_), channel_id=1, source_target_pairs={{0,2},{1,3},{2,0},{3,1},{4,6},{5,7},{6,4},{7,5},{8,10},{9,11},{10,... | collective-permute-start | bytes 1474568 | tf_op jit(solution)/shard_map/ppermute | solution.py:507
  197.0 41.4 %collective-permute-start.61 = (bf16[2,240,768]{2,1,0:T(8,128)(2,1)S(1)}, bf16[2,240,768]{2,1,0:T(8,128)(2,1)S(1)}, u32[]{:S(2)}, u32[]{:S(2)}) collective-permute-start(bf16[2,240,768]{2,1,0:T(8,128)(2,1)S(1)} %maximum_select_fusion.1.refs_12_.refs_10_.refs_15_), channel_id=1, source_target_pairs={{0,1},{1,0},{2,3},{3,2},{4,5},{5,4},{6,7},{7,6},{8,9},{9,8},{10,11... | collective-permute-start | bytes 2211848 | tf_op jit(solution)/shard_map/ppermute | solution.py:507
  197.9 39.1 %collective-permute-start.37 = (bf16[4,48,1280]{2,1,0:T(8,128)(2,1)S(1)}, bf16[4,48,1280]{2,1,0:T(8,128)(2,1)S(1)}, u32[]{:S(2)}, u32[]{:S(2)}) collective-permute-start(bf16[4,48,1280]{2,1,0:T(8,128)(2,1)S(1)} %collective-permute-done.35.refs_5_), channel_id=1, source_target_pairs={{0,2},{1,3},{2,0},{3,1},{4,6},{5,7},{6,4},{7,5},{8,10},{9,11},{10,... | collective-permute-start | bytes 1474568 | tf_op jit(solution)/shard_map/ppermute | solution.py:507
  219.1 72.9 %collective-permute-start.55 = (bf16[4,48,2688]{2,1,0:T(8,128)(2,1)S(1)}, bf16[4,48,2688]{2,1,0:T(8,128)(2,1)S(1)}, u32[]{:S(2)}, u32[]{:S(2)}) collective-permute-start(bf16[4,48,2688]{2,1,0:T(8,128)(2,1)S(1)} %pad_maximum_fusion.2.refs_6_.refs_8_.refs_11_), channel_id=1, source_target_pairs={{0,1},{1,0},{2,3},{3,2},{4,5},{5,4},{6,7},{7,6},{8,9},{9,8},{10,11... | collective-permute-start | bytes 3096584 | tf_op jit(solution)/shard_map/ppermute | solution.py:507
  253.3 21.8 %collective-permute-start.45 = (bf16[2,128,384]{2,1,0:T(8,128)(2,1)S(1)}, bf16[2,128,384]{2,1,0:T(8,128)(2,1)S(1)}, u32[]{:S(2)}, u32[]{:S(2)}) collective-permute-start(bf16[2,128,384]{2,1,0:T(8,128)(2,1)S(1)} %get-tuple-element.129.refs_2_), channel_id=1, source_target_pairs={{0,1},{1,0},{2,3},{3,2},{4,5},{5,4},{6,7},{7,6},{8,9},{9,8},{10,11... | collective-permute-start | bytes 589832 | tf_op jit(solution)/shard_map/ppermute | solution.py:507
  257.6 34.5 %collective-permute-start.57 = (bf16[4,48,2688]{2,1,0:T(8,128)(2,1)S(1)}, bf16[4,48,2688]{2,1,0:T(8,128)(2,1)}, u32[]{:S(2)}, u32[]{:S(2)}) collective-permute-start(bf16[4,48,2688]{2,1,0:T(8,128)(2,1)S(1)} %collective-permute-done.56.refs_8_.refs_10_.refs_13_), channel_id=1, source_target_pairs={{0,1},{1,0},{2,3},{3,2},{4,5},{5,4},{6,7},{7,6},{8,9},{9,8},{10,11... | collective-permute-start | bytes 3096584 | tf_op jit(solution)/shard_map/ppermute | solution.py:507
  257.8 26.7 %collective-permute-start.47 = (bf16[2,128,384]{2,1,0:T(8,128)(2,1)S(1)}, bf16[2,128,384]{2,1,0:T(8,128)(2,1)S(1)}, u32[]{:S(2)}, u32[]{:S(2)}) collective-permute-start(bf16[2,128,384]{2,1,0:T(8,128)(2,1)S(1)} %get-tuple-element.129.refs_2_), channel_id=1, source_target_pairs={{0,3},{1,2},{2,1},{3,0},{4,7},{5,6},{6,5},{7,4},{8,11},{9,10},{10,... | collective-permute-start | bytes 589832 | tf_op jit(solution)/shard_map/ppermute | solution.py:507
  275.1 38.1 %collective-permute-start.44 = (bf16[2,288,768]{2,1,0:T(8,128)(2,1)}, bf16[2,288,768]{2,1,0:T(8,128)(2,1)S(1)}, u32[]{:S(2)}, u32[]{:S(2)}) collective-permute-start(bf16[2,288,768]{2,1,0:T(8,128)(2,1)} %get-tuple-element.127.refs_3_), channel_id=1, source_target_pairs={{0,16},{16,0},{1,17},{17,1},{2,18},{18,2},{3,19},{19,3},{4,20},{20... | collective-permute-start | bytes 2654216 | tf_op jit(solution)/shard_map/ppermute | solution.py:504
  275.1 23.0 %collective-permute-start.62 = (bf16[2,240,768]{2,1,0:T(8,128)(2,1)S(1)}, bf16[2,240,768]{2,1,0:T(8,128)(2,1)S(1)}, u32[]{:S(2)}, u32[]{:S(2)}) collective-permute-start(bf16[2,240,768]{2,1,0:T(8,128)(2,1)S(1)} %maximum_select_fusion.1.refs_12_.refs_10_.refs_15_), channel_id=1, source_target_pairs={{0,2},{1,3},{2,0},{3,1},{4,6},{5,7},{6,4},{7,5},{8,10},{9,11},{10,... | collective-permute-start | bytes 2211848 | tf_op jit(solution)/shard_map/ppermute | solution.py:507
  284.5 28.6 %collective-permute-start.63 = (bf16[2,240,768]{2,1,0:T(8,128)(2,1)S(1)}, bf16[2,240,768]{2,1,0:T(8,128)(2,1)S(1)}, u32[]{:S(2)}, u32[]{:S(2)}) collective-permute-start(bf16[2,240,768]{2,1,0:T(8,128)(2,1)S(1)} %collective-permute-done.61.refs_13_.refs_11_.refs_16_), channel_id=1, source_target_pairs={{0,2},{1,3},{2,0},{3,1},{4,6},{5,7},{6,4},{7,5},{8,10},{9,11},{10,... | collective-permute-start | bytes 2211848 | tf_op jit(solution)/shard_map/ppermute | solution.py:507
  361.0 23.1 %collective-permute-start.70 = (bf16[2,288,768]{2,1,0:T(8,128)(2,1)}, bf16[2,288,768]{2,1,0:T(8,128)(2,1)}, u32[]{:S(2)}, u32[]{:S(2)}) collective-permute-start(bf16[2,288,768]{2,1,0:T(8,128)(2,1)} %get-tuple-element.140.refs_2_), channel_id=1, source_target_pairs={{0,16},{16,0},{1,17},{17,1},{2,18},{18,2},{3,19},{19,3},{4,20},{20... | collective-permute-start | bytes 2654216 | tf_op jit(solution)/shard_map/ppermute | solution.py:504
  379.8 60.5 %collective-permute-start.140 = (bf16[2,240,768]{2,1,0:T(8,128)(2,1)}, bf16[2,240,768]{2,1,0:T(8,128)(2,1)}, u32[]{:S(2)}, u32[]{:S(2)}) collective-permute-start(bf16[2,240,768]{2,1,0:T(8,128)(2,1)} %get-tuple-element.229), channel_id=1, source_target_pairs={{0,2},{1,3},{2,0},{3,1},{4,6},{5,7},{6,4},{7,5},{8,10},{9,11},{10,... | collective-permute-start | bytes 2211848 | tf_op jit(solution)/shard_map/ppermute | solution.py:507
  380.9 71.1 %collective-permute-start.127 = (bf16[4,48,2304]{2,1,0:T(8,128)(2,1)}, bf16[4,48,2304]{2,1,0:T(8,128)(2,1)}, u32[]{:S(2)}, u32[]{:S(2)}) collective-permute-start(bf16[4,48,2304]{2,1,0:T(8,128)(2,1)} %get-tuple-element.222), channel_id=1, source_target_pairs={{0,1},{1,0},{2,3},{3,2},{4,5},{5,4},{6,7},{7,6},{8,9},{9,8},{10,11... | collective-permute-start | bytes 2654216 | tf_op jit(solution)/shard_map/ppermute | solution.py:507
  438.3 27.9 %collective-permute-start.142 = (bf16[2,240,768]{2,1,0:T(8,128)(2,1)}, bf16[2,240,768]{2,1,0:T(8,128)(2,1)S(1)}, u32[]{:S(2)}, u32[]{:S(2)}) collective-permute-start(bf16[2,240,768]{2,1,0:T(8,128)(2,1)} %get-tuple-element.230), channel_id=1, source_target_pairs={{0,2},{1,3},{2,0},{3,1},{4,6},{5,7},{6,4},{7,5},{8,10},{9,11},{10,... | collective-permute-start | bytes 2211848 | tf_op jit(solution)/shard_map/ppermute | solution.py:507
  441.9 24.3 %collective-permute-start.141 = (bf16[2,240,768]{2,1,0:T(8,128)(2,1)S(1)}, bf16[2,240,768]{2,1,0:T(8,128)(2,1)S(1)}, u32[]{:S(2)}, u32[]{:S(2)}) collective-permute-start(bf16[2,240,768]{2,1,0:T(8,128)(2,1)S(1)} %add.434), channel_id=1, source_target_pairs={{0,1},{1,0},{2,3},{3,2},{4,5},{5,4},{6,7},{7,6},{8,9},{9,8},{10,11... | collective-permute-start | bytes 2211848 | tf_op jit(solution)/shard_map/ppermute | solution.py:507
  452.0 41.9 %collective-permute-start.126 = (bf16[4,48,2304]{2,1,0:T(8,128)(2,1)}, bf16[4,48,2304]{2,1,0:T(8,128)(2,1)S(1)}, u32[]{:S(2)}, u32[]{:S(2)}) collective-permute-start(bf16[4,48,2304]{2,1,0:T(8,128)(2,1)} %get-tuple-element.220), channel_id=1, source_target_pairs={{0,1},{1,0},{2,3},{3,2},{4,5},{5,4},{6,7},{7,6},{8,9},{9,8},{10,11... | collective-permute-start | bytes 2654216 | tf_op jit(solution)/shard_map/ppermute | solution.py:507
  455.1 40.2 %collective-permute-start.128 = (bf16[4,48,2304]{2,1,0:T(8,128)(2,1)S(1)}, bf16[4,48,2304]{2,1,0:T(8,128)(2,1)S(1)}, u32[]{:S(2)}, u32[]{:S(2)}) collective-permute-start(bf16[4,48,2304]{2,1,0:T(8,128)(2,1)S(1)} %add.423), channel_id=1, source_target_pairs={{0,2},{1,3},{2,0},{3,1},{4,6},{5,7},{6,4},{7,5},{8,10},{9,11},{10,... | collective-permute-start | bytes 2654216 | tf_op jit(solution)/shard_map/ppermute | solution.py:507
  465.5 22.3 %collective-permute-start.98 = (bf16[4,48,1536]{2,1,0:T(8,128)(2,1)S(1)}, bf16[4,48,1536]{2,1,0:T(8,128)(2,1)S(1)}, u32[]{:S(2)}, u32[]{:S(2)}) collective-permute-start(bf16[4,48,1536]{2,1,0:T(8,128)(2,1)S(1)} %copy-done.114), channel_id=1, source_target_pairs={{0,2},{1,3},{2,0},{3,1},{4,6},{5,7},{6,4},{7,5},{8,10},{9,11},{10,... | collective-permute-start | bytes 1769480 | tf_op jit(solution)/shard_map/ppermute | solution.py:507
  466.2 150.9 %collective-permute-start.85 = (bf16[2,128,768]{2,1,0:T(8,128)(2,1)S(1)}, bf16[2,128,768]{2,1,0:T(8,128)(2,1)S(1)}, u32[]{:S(2)}, u32[]{:S(2)}) collective-permute-start(bf16[2,128,768]{2,1,0:T(8,128)(2,1)S(1)} %copy-done.16), channel_id=1, source_target_pairs={{0,16},{16,0},{1,17},{17,1},{2,18},{18,2},{3,19},{19,3},{4,20},{20... | collective-permute-start | bytes 1179656 | tf_op jit(solution)/shard_map/ppermute | solution.py:504
  466.2 62.2 %collective-permute-start.73 = (bf16[2,288,768]{2,1,0:T(8,128)(2,1)S(1)}, bf16[2,288,768]{2,1,0:T(8,128)(2,1)S(1)}, u32[]{:S(2)}, u32[]{:S(2)}) collective-permute-start(bf16[2,288,768]{2,1,0:T(8,128)(2,1)S(1)} %copy-done.69), channel_id=1, source_target_pairs={{0,16},{16,0},{1,17},{17,1},{2,18},{18,2},{3,19},{19,3},{4,20},{20... | collective-permute-start | bytes 2654216 | tf_op jit(solution)/shard_map/ppermute | solution.py:504
  493.9 32.6 %collective-permute-start.145 = (bf16[240,768]{1,0:T(8,128)(2,1)S(1)}, bf16[240,768]{1,0:T(8,128)(2,1)S(1)}, u32[]{:S(2)}, u32[]{:S(2)}) collective-permute-start(bf16[240,768]{1,0:T(8,128)(2,1)S(1)} %get-tuple-element.294), channel_id=1, source_target_pairs={{12,0},{8,4},{20,24},{16,28},{13,1},{9,5},{21,25},{17,29},{14,2},{... | collective-permute-start | bytes 1105928 | tf_op jit(solution)/shard_map/ppermute | solution.py:818
  495.2 31.2 %collective-permute-start.144 = (bf16[240,768]{1,0:T(8,128)(2,1)S(1)}, bf16[240,768]{1,0:T(8,128)(2,1)S(1)}, u32[]{:S(2)}, u32[]{:S(2)}) collective-permute-start(bf16[240,768]{1,0:T(8,128)(2,1)S(1)} %get-tuple-element.293), channel_id=1, source_target_pairs={{8,0},{12,4},{16,24},{20,28},{9,1},{13,5},{17,25},{21,29},{10,2},{... | collective-permute-start | bytes 1105928 | tf_op jit(solution)/shard_map/ppermute | solution.py:818
  501.9 58.5 %collective-permute-start.129 = (bf16[48,2304]{1,0:T(8,128)(2,1)S(1)}, bf16[48,2304]{1,0:T(8,128)(2,1)S(1)}, u32[]{:S(2)}, u32[]{:S(2)}) collective-permute-start(bf16[48,2304]{1,0:T(8,128)(2,1)S(1)} %get-tuple-element.300), channel_id=1, source_target_pairs={{0,4},{4,0},{8,12},{12,8},{1,5},{5,1},{9,13},{13,9},{2,6},{6,2},{1... | collective-permute-start | bytes 663560 | tf_op jit(solution)/shard_map/ppermute | solution.py:793
  526.5 34.9 %collective-permute-start.130 = (bf16[48,2304]{1,0:T(8,128)(2,1)S(1)}, bf16[48,2304]{1,0:T(8,128)(2,1)S(1)}, u32[]{:S(2)}, u32[]{:S(2)}) collective-permute-start(bf16[48,2304]{1,0:T(8,128)(2,1)S(1)} %get-tuple-element.302), channel_id=1, source_target_pairs={{0,8},{4,12},{8,0},{12,4},{1,9},{5,13},{9,1},{13,5},{2,10},{6,14},... | collective-permute-start | bytes 663560 | tf_op jit(solution)/shard_map/ppermute | solution.py:793
  526.5 36.0 %collective-permute-start.131 = (bf16[48,2304]{1,0:T(8,128)(2,1)S(1)}, bf16[48,2304]{1,0:T(8,128)(2,1)S(1)}, u32[]{:S(2)}, u32[]{:S(2)}) collective-permute-start(bf16[48,2304]{1,0:T(8,128)(2,1)S(1)} %get-tuple-element.301), channel_id=1, source_target_pairs={{0,12},{4,8},{8,4},{12,0},{1,13},{5,9},{9,5},{13,1},{2,14},{6,10},... | collective-permute-start | bytes 663560 | tf_op jit(solution)/shard_map/ppermute | solution.py:793
  563.4 35.1 %collective-permute-start.100 = (bf16[4,48,1536]{2,1,0:T(8,128)(2,1)}, bf16[4,48,1536]{2,1,0:T(8,128)(2,1)S(1)}, u32[]{:S(2)}, u32[]{:S(2)}) collective-permute-start(bf16[4,48,1536]{2,1,0:T(8,128)(2,1)} %get-tuple-element.194), channel_id=1, source_target_pairs={{0,2},{1,3},{2,0},{3,1},{4,6},{5,7},{6,4},{7,5},{8,10},{9,11},{10,... | collective-permute-start | bytes 1769480 | tf_op jit(solution)/shard_map/ppermute | solution.py:507
  568.4 30.8 %collective-permute-start.99 = (bf16[4,48,1536]{2,1,0:T(8,128)(2,1)S(1)}, bf16[4,48,1536]{2,1,0:T(8,128)(2,1)S(1)}, u32[]{:S(2)}, u32[]{:S(2)}) collective-permute-start(bf16[4,48,1536]{2,1,0:T(8,128)(2,1)S(1)} %copy-done.82), channel_id=1, source_target_pairs={{0,1},{1,0},{2,3},{3,2},{4,5},{5,4},{6,7},{7,6},{8,9},{9,8},{10,11... | collective-permute-start | bytes 1769480 | tf_op jit(solution)/shard_map/ppermute | solution.py:507
  569.2 49.2 %collective-permute-start.134 = (bf16[2,240,768]{2,1,0:T(8,128)(2,1)}, bf16[2,240,768]{2,1,0:T(8,128)(2,1)S(1)}, u32[]{:S(2)}, u32[]{:S(2)}) collective-permute-start(bf16[2,240,768]{2,1,0:T(8,128)(2,1)} %get-tuple-element.225), channel_id=1, source_target_pairs={{0,2},{1,3},{2,0},{3,1},{4,6},{5,7},{6,4},{7,5},{8,10},{9,11},{10,... | collective-permute-start | bytes 2211848 | tf_op jit(solution)/shard_map/ppermute | solution.py:507
  572.0 35.2 %collective-permute-start.84 = (bf16[2,128,768]{2,1,0:T(8,128)(2,1)S(1)}, bf16[2,128,768]{2,1,0:T(8,128)(2,1)S(1)}, u32[]{:S(2)}, u32[]{:S(2)}) collective-permute-start(bf16[2,128,768]{2,1,0:T(8,128)(2,1)S(1)} %get-tuple-element.166.da_ref), channel_id=1, source_target_pairs={{0,16},{16,0},{1,17},{17,1},{2,18},{18,2},{3,19},{19,3},{4,20},{20... | collective-permute-start | bytes 1179656 | tf_op jit(solution)/shard_map/ppermute | solution.py:504
  607.2 22.7 %collective-permute-start.121 = (bf16[4,48,2304]{2,1,0:T(8,128)(2,1)}, bf16[4,48,2304]{2,1,0:T(8,128)(2,1)}, u32[]{:S(2)}, u32[]{:S(2)}) collective-permute-start(bf16[4,48,2304]{2,1,0:T(8,128)(2,1)} %get-tuple-element.212), channel_id=1, source_target_pairs={{0,1},{1,0},{2,3},{3,2},{4,5},{5,4},{6,7},{7,6},{8,9},{9,8},{10,11... | collective-permute-start | bytes 2654216 | tf_op jit(solution)/shard_map/ppermute | solution.py:507
  609.5 26.0 %collective-permute-start.92 = (bf16[4,48,1536]{2,1,0:T(8,128)(2,1)}, bf16[4,48,1536]{2,1,0:T(8,128)(2,1)}, u32[]{:S(2)}, u32[]{:S(2)}) collective-permute-start(bf16[4,48,1536]{2,1,0:T(8,128)(2,1)} %get-tuple-element.183), channel_id=1, source_target_pairs={{0,2},{1,3},{2,0},{3,1},{4,6},{5,7},{6,4},{7,5},{8,10},{9,11},{10,... | collective-permute-start | bytes 1769480 | tf_op jit(solution)/shard_map/ppermute | solution.py:507
  633.6 28.4 %collective-permute-start.120 = (bf16[4,48,2304]{2,1,0:T(8,128)(2,1)}, bf16[4,48,2304]{2,1,0:T(8,128)(2,1)}, u32[]{:S(2)}, u32[]{:S(2)}) collective-permute-start(bf16[4,48,2304]{2,1,0:T(8,128)(2,1)} %get-tuple-element.210), channel_id=1, source_target_pairs={{0,1},{1,0},{2,3},{3,2},{4,5},{5,4},{6,7},{7,6},{8,9},{9,8},{10,11... | collective-permute-start | bytes 2654216 | tf_op jit(solution)/shard_map/ppermute | solution.py:507
  634.3 28.7 %collective-permute-start.122 = (bf16[4,48,2304]{2,1,0:T(8,128)(2,1)S(1)}, bf16[4,48,2304]{2,1,0:T(8,128)(2,1)}, u32[]{:S(2)}, u32[]{:S(2)}) collective-permute-start(bf16[4,48,2304]{2,1,0:T(8,128)(2,1)S(1)} %add.417), channel_id=1, source_target_pairs={{0,2},{1,3},{2,0},{3,1},{4,6},{5,7},{6,4},{7,5},{8,10},{9,11},{10,... | collective-permute-start | bytes 2654216 | tf_op jit(solution)/shard_map/ppermute | solution.py:507
  640.1 32.6 %collective-permute-start.80 = (bf16[2,288,768]{2,1,0:T(8,128)(2,1)}, bf16[2,288,768]{2,1,0:T(8,128)(2,1)}, u32[]{:S(2)}, u32[]{:S(2)}) collective-permute-start(bf16[2,288,768]{2,1,0:T(8,128)(2,1)} %get-tuple-element.164), channel_id=1, source_target_pairs={{0,16},{16,0},{1,17},{17,1},{2,18},{18,2},{3,19},{19,3},{4,20},{20... | collective-permute-start | bytes 2654216 | tf_op jit(solution)/shard_map/ppermute | solution.py:504
  647.2 78.9 %collective-permute-start.149 = (f32[48,768]{1,0:T(8,128)}, f32[48,768]{1,0:T(8,128)S(1)}, u32[]{:S(2)}, u32[]{:S(2)}) collective-permute-start(f32[48,768]{1,0:T(8,128)} %slice.390), channel_id=1, source_target_pairs={{0,16},{1,17},{2,18},{3,19},{4,20},{5,21},{6,22},{7,23},{8,24},{9,... | collective-permute-start | bytes 442376 | tf_op jit(solution)/shard_map/ppermute | solution.py:987
  667.0 48.0 %collective-permute-start.132 = (f32[48,2304]{1,0:T(8,128)S(1)}, f32[48,2304]{1,0:T(8,128)S(1)}, u32[]{:S(2)}, u32[]{:S(2)}) collective-permute-start(f32[48,2304]{1,0:T(8,128)S(1)} %copy-done.62), channel_id=1, source_target_pairs={{0,16},{1,17},{2,18},{3,19},{4,20},{5,21},{6,22},{7,23},{8,24},{9,... | collective-permute-start | bytes 1327112 | tf_op jit(solution)/shard_map/ppermute | solution.py:987
  681.1 33.5 %collective-permute-start.139 = (bf16[240,768]{1,0:T(8,128)(2,1)S(1)}, bf16[240,768]{1,0:T(8,128)(2,1)S(1)}, u32[]{:S(2)}, u32[]{:S(2)}) collective-permute-start(bf16[240,768]{1,0:T(8,128)(2,1)S(1)} %copy-done.90), channel_id=1, source_target_pairs={{12,0},{8,4},{20,24},{16,28},{13,1},{9,5},{21,25},{17,29},{14,2},{... | collective-permute-start | bytes 1105928 | tf_op jit(solution)/shard_map/ppermute | solution.py:818
  682.4 32.1 %collective-permute-start.138 = (bf16[240,768]{1,0:T(8,128)(2,1)S(1)}, bf16[240,768]{1,0:T(8,128)(2,1)S(1)}, u32[]{:S(2)}, u32[]{:S(2)}) collective-permute-start(bf16[240,768]{1,0:T(8,128)(2,1)S(1)} %copy-done.91), channel_id=1, source_target_pairs={{8,0},{12,4},{16,24},{20,28},{9,1},{13,5},{17,25},{21,29},{10,2},{... | collective-permute-start | bytes 1105928 | tf_op jit(solution)/shard_map/ppermute | solution.py:818
  691.5 25.5 %collective-permute-start.123 = (bf16[48,2304]{1,0:T(8,128)(2,1)S(1)}, bf16[48,2304]{1,0:T(8,128)(2,1)S(1)}, u32[]{:S(2)}, u32[]{:S(2)}) collective-permute-start(bf16[48,2304]{1,0:T(8,128)(2,1)S(1)} %get-tuple-element.297), channel_id=1, source_target_pairs={{0,4},{4,0},{8,12},{12,8},{1,5},{5,1},{9,13},{13,9},{2,6},{6,2},{1... | collective-permute-start | bytes 663560 | tf_op jit(solution)/shard_map/ppermute | solution.py:793
  715.6 49.2 %collective-permute-start.147 = (f32[192,768]{1,0:T(8,128)S(1)}, f32[192,768]{1,0:T(8,128)S(1)}, u32[]{:S(2)}, u32[]{:S(2)}) collective-permute-start(f32[192,768]{1,0:T(8,128)S(1)} %copy-done.85), channel_id=1, source_target_pairs={{0,16},{1,17},{2,18},{3,19},{4,20},{5,21},{6,22},{7,23},{8,24},{9,... | collective-permute-start | bytes 1769480 | tf_op jit(solution)/shard_map/ppermute | solution.py:987
  726.8 31.8 %collective-permute-start.101 = (bf16[48,1536]{1,0:T(8,128)(2,1)S(1)}, bf16[48,1536]{1,0:T(8,128)(2,1)S(1)}, u32[]{:S(2)}, u32[]{:S(2)}) collective-permute-start(bf16[48,1536]{1,0:T(8,128)(2,1)S(1)} %copy-done.96), channel_id=1, source_target_pairs={{0,4},{4,0},{8,12},{12,8},{1,5},{5,1},{9,13},{13,9},{2,6},{6,2},{1... | collective-permute-start | bytes 442376 | tf_op jit(solution)/shard_map/ppermute | solution.py:793
  (203 other events, 2617.4 us)

commit v2 on v1

v2 whole, which is shorter than its diff:
```python
from functools import partial
import itertools
import math

import jax
import jax.numpy as jnp
from jax import lax
from jax.experimental import pallas as pl
from jax.experimental.pallas import tpu as pltpu
from jax.sharding import PartitionSpec as P

D = 768
HEADS = 12
HDIM = 64
WIN = 12
NQ = 128
CELLS = WIN * WIN
HALF = D // 2
HH = HEADS // 2
PAIRS = HH // 2
RIM = WIN // 2 * WIN
CQ_AT = 128 + 3 * HALF
OUT_AT = CQ_AT + HALF

epsilon = 1e-05
hidden_value = -1e30
scaling = 1.0 / math.sqrt(HDIM)
bf16 = jnp.bfloat16
f32 = jnp.float32
SWAP = [(0, 1), (1, 0)]
ANY = pl.BlockSpec(memory_space=pl.ANY)
SMEM = pl.BlockSpec(memory_space=pltpu.SMEM)


def whole(shape):
    return pl.BlockSpec(shape, lambda *_: (0,) * len(shape))


def per_batch(shape):
    return pl.BlockSpec((1,) + tuple(shape[1:]), lambda m: (m,) + (0,) * (len(shape) - 1))


def run(kernel, name, grid, ins, outs, scratch, micros):
    arrays = [a for a, _ in ins]
    return pl.pallas_call(
        kernel,
        grid=grid,
        in_specs=[s for _, s in ins],
        out_specs=[s for _, _, s in outs],
        out_shape=[jax.ShapeDtypeStruct(sh, dt) for sh, dt, _ in outs],
        scratch_shapes=scratch,
        compiler_params=pltpu.CompilerParams(vmem_limit_bytes=52 * 1024 * 1024),
        cost_estimate=pl.CostEstimate(flops=int(micros * 1.15e9 * 1), bytes_accessed=0, transcendentals=0),
        name=name,
    )(*arrays)


def slots_of(pieces):
    near = pieces[3].shape[0]
    spots = [(p, k, p, k) for p in range(3) for k in range(2 * near)]
    return spots + [(3 + h, k, 3, h * near + k) for h in range(2) for k in range(near)]


def segments(unit, layout, col0, cols):
    count, off_x, off_y, cut = layout
    slots = unit[0].shape[0]
    for p, off in enumerate((0, off_x, off_y)):
        for k in range(slots):
            yield p, col0 + off, 0, cols, p, k
    for piece, low, high in ((3, 0, cut), (4, cut, col0 + cols)):
        start, end = max(low, col0), min(high, col0 + cols)
        if start < end:
            for k in range(slots):
                yield piece, start - low, start - col0, end - start, 3, k


def fetch_columns(dst, unit, layout, order, col0, sem):
    cols = dst.shape[1]
    if len(unit) < 5:
        pltpu.make_async_copy(unit[0].at[:, pl.ds(col0, cols)], dst, sem).start()
        return
    slots, rows = unit[0].shape[:2]
    for piece, come, off, width, p, k in segments(unit, layout, col0, cols):
        to = pl.multiple_of(order[p * slots + k] * rows, 16)
        pltpu.make_async_copy(
            unit[piece].at[k, :, pl.ds(come, width)], dst.at[pl.ds(to, rows), pl.ds(off, width)], sem
        ).start()


def fetch_rows(dst, unit, layout, order, col0, row0, sem):
    if len(unit) < 5:
        if len(unit[0].shape) == 5:
            slots, spots, sides, rows, _ = unit[0].shape
            each = dst.shape[0] // (slots * spots)
            for k, p, side, b in itertools.product(
                range(slots), range(spots), range(sides), range(each // rows)
            ):
                to = pl.multiple_of(order[p * slots + k] * each + b * rows, 16)
                pltpu.make_async_copy(
                    unit[0].at[k, p, side, :, pl.ds(col0 + b * HALF, HALF)],
                    dst.at[pl.ds(to, rows), pl.ds(side * HALF, HALF)],
                    sem,
                ).start()
            return
        pltpu.make_async_copy(unit[-1].at[pl.ds(row0, dst.shape[0]), :], dst, sem).start()
        return
    slots, rows = unit[0].shape[:2]
    each = dst.shape[0] // (2 * slots)
    for b in range(each // rows):
        for piece, come, off, width, p, k in segments(unit, layout, col0 + b * HALF, HALF):
            base = order[p * (slots // 2) + k // 2] * each
            to = pl.multiple_of(base + b * rows, 16)
            pltpu.make_async_copy(
                unit[piece].at[k, :, pl.ds(come, width)],
                dst.at[pl.ds(to, rows), pl.ds((k % 2) * HALF + off, width)],
                sem,
            ).start()


def end_fetch(dst, sem):
    pltpu.make_async_copy(dst, dst, sem).wait()


def spread_columns(acc, unit, order, col0):
    cols = acc.shape[1]
    if len(unit) < 5:
        unit[0][:, col0 : col0 + cols] = acc[0:D].astype(bf16)
        return
    slots, rows = unit[0].shape[:2]
    for piece, at, p, k in slots_of(unit):
        come = pl.multiple_of(order[p * slots + k] * rows, 8)
        unit[piece][at, :, col0 : col0 + cols] = acc[pl.ds(come, rows), :].astype(bf16)


def spread_rows(acc, unit, order, height, side, col0, row0):
    if len(unit) < 5:
        unit[-1][row0 : row0 + height, side * HALF : side * HALF + HALF] = acc[0:height].astype(bf16)
        return
    slots, rows = unit[0].shape[:2]
    each = height // (2 * slots)
    for piece, at, p, k in slots_of(unit):
        if k % 2 != side:
            continue
        base = order[p * (slots // 2) + k // 2] * each
        for b in range(each // rows):
            come = pl.multiple_of(base + b * rows, 8)
            unit[piece][at, :, col0 + b * HALF : col0 + b * HALF + HALF] = acc[
                pl.ds(come, rows), :
            ].astype(bf16)


def nn(a, b):
    return jnp.dot(a, b, preferred_element_type=f32)


def nt(a, b):
    return lax.dot_general(a, b, (((1,), (1,)), ((), ())), preferred_element_type=f32)


def tn(a, b):
    return lax.dot_general(a, b, (((0,), (0,)), ((), ())), preferred_element_type=f32)


def norm_parts(values):
    center = values - jnp.mean(values, axis=-1, keepdims=True)
    inv = lax.rsqrt(jnp.mean(center * center, axis=-1, keepdims=True) + epsilon)
    return center * inv, inv


def norm_back(unit, inv, gain, grad):
    scaled = grad * gain
    return inv * (
        scaled
        - jnp.mean(scaled, axis=-1, keepdims=True)
        - unit * jnp.mean(scaled * unit, axis=-1, keepdims=True)
    )


def co_at(lower):
    if len(lower[0].shape) == 5:
        return lower[0].shape[4] - HALF, 0
    if len(lower) < 5:
        return 0, lower[-1].shape[0] - HALF
    return lower[0].shape[2] - HALF, 0


def lane_halves(rows):
    lane = lax.broadcasted_iota(jnp.int32, (rows, 128), 1)
    return lane < HDIM


def half_masks():
    lane = lax.broadcasted_iota(jnp.int32, (1, 128), 1)
    low = (lane < HDIM).astype(f32)
    return low.astype(bf16), (1.0 - low).astype(bf16)


def attn_forward(n, shifted, *refs):
    order_c, order_r, x_ref = refs[:3]
    refs = refs[3:]
    if shifted:
        mask_ref, refs = refs[0], refs[1:]
    unit, refs = refs[: n[0][0]], refs[n[0][0] :]
    h_ref, qkv_ref, p_ref, o_ref, part_ref, gain_ref, w_in, w_out, mixed, hidden, sem0, sem1 = refs
    tokens = x_ref.shape[1]
    own = o_ref.shape[1]
    lo = (tokens - own) // 2

    @pl.when(pl.program_id(0) == 0)
    def _():
        fetch_columns(w_in, unit, n[0], order_c, 0, sem0)
        fetch_rows(w_out, unit, n[0], order_r, OUT_AT, 0, sem1)
        end_fetch(w_in, sem0)
        end_fetch(w_out, sem1)
        gain_ref[...] = w_in[:, :128].astype(f32).T[0:8]

    direction, _ = norm_parts(x_ref[0].astype(f32))
    hidden[...] = direction * gain_ref[0:1]
    h_ref[0] = hidden[lo : lo + own].astype(bf16)
    qkv_ref[0] = nn(hidden[...].astype(bf16), w_in[:, 128:]).astype(bf16)
    first_half = lane_halves(CELLS)
    masks = half_masks()
    for block in range(tokens // CELLS):
        rows = slice(block * CELLS, (block + 1) * CELLS)
        for pair in range(PAIRS):
            q2 = qkv_ref[0, rows, pair * 128 : pair * 128 + 128]
            k2 = qkv_ref[0, rows, HALF + pair * 128 : HALF + pair * 128 + 128]
            v2 = qkv_ref[0, rows, 2 * HALF + pair * 128 : 2 * HALF + pair * 128 + 128]
            mixed_two = []
            for side in range(2):
                scores = nt(q2 * masks[side], k2) * scaling
                if shifted:
                    scores = scores + mask_ref[block]
                weights = jnp.exp(scores - jnp.max(scores, axis=-1, keepdims=True))
                probs = (weights / jnp.sum(weights, axis=-1, keepdims=True)).astype(bf16)
                p_ref[0, block * HH + pair * 2 + side] = probs
                mixed_two.append(nn(probs, v2))
            mixed[rows, pair * 128 : pair * 128 + 128] = jnp.where(
                first_half, mixed_two[0], mixed_two[1]
            )
    out = mixed[lo : lo + own].astype(bf16)
    o_ref[0] = out
    part_ref[0] = nn(out, w_out[...]).astype(bf16)


def mlp_forward(n, *refs):
    order_c, order_r, x_ref, pa_ref, pb_ref, gain_ref, cq_ref, valid_ref = refs[:8]
    refs = refs[8:]
    upper, lower, refs = refs[: n[1][0]], refs[n[1][0] : n[1][0] + n[2][0]], refs[n[1][0] + n[2][0] :]
    first_ref, h_ref, slope_ref, act_ref, part_ref, ckv_ref, e_ref, o_ref = refs[:8]
    w_up, w_down, sem0, sem1 = refs[8:]
    hid = slope_ref.shape[2]
    tokens = x_ref.shape[1]

    @pl.when(pl.program_id(0) == 0)
    def _():
        fetch_columns(w_up, upper, n[1], order_c, 0, sem0)
        fetch_rows(w_down, lower, n[2], order_r, 0, 0, sem1)
        end_fetch(w_up, sem0)
        end_fetch(w_down, sem1)

    first = x_ref[0].astype(f32) + (pa_ref[0].astype(f32) + pb_ref[0].astype(f32))
    first_ref[0] = first
    unit, _ = norm_parts(first)
    hidden = (unit * gain_ref[1:2]).astype(bf16)
    h_ref[0] = hidden
    ckv_ref[0] = nn(hidden, w_up[:, hid:]).astype(bf16)
    step = 512
    for at in range(0, hid, step):
        lifted = nn(hidden, w_up[:, at : at + step])
        cdf = 0.5 + 0.5 * lax.erf(lifted * math.sqrt(0.5))
        act_ref[0, :, at : at + step] = (lifted * cdf).astype(bf16)
        pdf = jnp.exp(lifted * lifted * -0.5) * (1.0 / math.sqrt(2.0 * math.pi))
        slope_ref[0, :, at : at + step] = (cdf + lifted * pdf).astype(bf16)
    part_ref[0] = nn(act_ref[0], w_down[...]).astype(bf16)

    valid = jnp.broadcast_to(valid_ref[0], (NQ, tokens)) > 0.5
    first_half = lane_halves(NQ)
    masks = half_masks()
    lane = lax.broadcasted_iota(jnp.int32, (NQ, 128), 1)
    stats = jnp.zeros((NQ, 128), f32)
    for pair in range(PAIRS):
        q2 = cq_ref[0, :, pair * 128 : pair * 128 + 128]
        k2 = ckv_ref[0, :, pair * 128 : pair * 128 + 128]
        v2 = ckv_ref[0, :, HALF + pair * 128 : HALF + pair * 128 + 128]
        mixed_two = []
        for side in range(2):
            head = pair * 2 + side
            scores = jnp.where(valid, nt(q2 * masks[side], k2) * scaling, hidden_value)
            peak = jnp.max(scores, axis=-1, keepdims=True)
            weights = jnp.where(valid, jnp.exp(scores - peak), 0.0)
            total = jnp.sum(weights, axis=-1, keepdims=True)
            for at, value in ((0, peak), (16, total)):
                high = value.astype(bf16).astype(f32)
                stats = jnp.where(lane == at + head, high, stats)
                stats = jnp.where(lane == at + 8 + head, value - high, stats)
            low = weights.astype(bf16)
            e_ref[0, head] = low
            mixed_two.append(nn(low, v2))
        o_ref[0, :, pair * 128 : pair * 128 + 128] = jnp.where(
            first_half, mixed_two[0], mixed_two[1]
        ).astype(bf16)
    o_ref[0, :, HALF:] = stats.astype(bf16)


def query_in(n, has_parts, *refs):
    order_c, q_ref, gain_ref = refs[:3]
    refs = refs[3:]
    if has_parts:
        pa_ref, pb_ref, live_ref, refs = refs[0], refs[1], refs[2], refs[3:]
    unit, refs = refs[: n[0][0]], refs[n[0][0] :]
    if has_parts:
        new_ref, refs = refs[0], refs[1:]
    h_ref, cq_ref, w_q, sem = refs
    fetch_columns(w_q, unit, n[0], order_c, CQ_AT, sem)
    end_fetch(w_q, sem)
    for m in range(q_ref.shape[0]):
        query = q_ref[m].astype(f32)
        if has_parts:
            query = query + live_ref[m] * (pa_ref[m].astype(f32) + pb_ref[m].astype(f32))
            low = query.astype(bf16)
            new_ref[m] = low
            query = low.astype(f32)
        direction, _ = norm_parts(query)
        hidden = (direction * gain_ref[2:3]).astype(bf16)
        h_ref[m] = hidden
        cq_ref[m] = nn(hidden, w_q[...]).astype(bf16)


def query_out(n, ns, *refs):
    order_r, order_s = refs[:2]
    refs = refs[2:]
    os, refs = refs[:ns], refs[ns:]
    lower, refs = refs[: n[2][0]], refs[n[2][0] :]
    att_ref, low_ref, coef_ref, part_ref, w_co, o_all, sem = refs
    fetch_rows(w_co, lower, n[2], order_r, *co_at(lower), sem)
    for p in range(ns):
        o_all[order_s[p]] = os[p][...]
    first_half = lane_halves(NQ)
    end_fetch(w_co, sem)

    def stat(block, at):
        wide = block.astype(f32)
        return wide[:, at : at + 8] + wide[:, at + 8 : at + 16]

    for m in range(att_ref.shape[0]):
        stats = [o_all[s, m, :, HALF:] for s in range(ns)]
        peaks = [stat(block, 0) for block in stats]
        peak = peaks[0]
        for other in peaks[1:]:
            peak = jnp.maximum(peak, other)
        scales = [jnp.exp(p - peak) for p in peaks]
        total = scales[0] * stat(stats[0], 16)
        for scale, block in zip(scales[1:], stats[1:]):
            total = total + scale * stat(block, 16)
        inverse = 1.0 / jnp.where(total > 0.0, total, 1.0)
        coef_ref[m, :, 0:8] = jnp.exp(stat(os[0][m, :, HALF:], 0) - peak) * inverse
        factors = [scale * inverse for scale in scales]
        for pair in range(PAIRS):
            mixed = jnp.zeros((NQ, 128), f32)
            for s in range(ns):
                at = pair * 2
                factor = jnp.where(
                    first_half, factors[s][:, at : at + 1], factors[s][:, at + 1 : at + 2]
                )
                mixed = mixed + factor * o_all[s, m, :, pair * 128 : pair * 128 + 128].astype(f32)
            att_ref[m, :, pair * 128 : pair * 128 + 128] = mixed
        low = att_ref[m].astype(bf16)
        low_ref[m] = low
        part_ref[m] = nn(low, w_co[...]).astype(bf16)


def mlp_backward(n, *refs):
    order_c, order_r, ds_ref, slope_ref, e_ref, coef_ref, dq_ref, live_ref, att_ref, cq_ref, ckv_ref = refs[:11]
    refs = refs[11:]
    upper, lower, refs = refs[: n[1][0]], refs[n[1][0] : n[1][0] + n[2][0]], refs[n[1][0] + n[2][0] :]
    du_ref, dckv_ref, dcq_ref, part_ref, dc_ref, w_up, w_down, w_co, sem0, sem1, sem2 = refs
    hid = slope_ref.shape[2]
    tokens = ds_ref.shape[1]

    @pl.when(pl.program_id(0) == 0)
    def _():
        fetch_rows(w_down, lower, n[2], order_r, 0, 0, sem1)
        fetch_rows(w_co, lower, n[2], order_r, *co_at(lower), sem2)
        fetch_columns(w_up, upper, n[1], order_c, 0, sem0)
        end_fetch(w_down, sem1)
        end_fetch(w_co, sem2)
        end_fetch(w_up, sem0)

    grad_second = ds_ref[0]
    step = 512
    for at in range(0, hid, step):
        grad_act = nt(grad_second, w_down[at : at + step, :])
        du_ref[0, :, at : at + step] = (
            grad_act * slope_ref[0, :, at : at + step].astype(f32)
        ).astype(bf16)

    grad_cross = (live_ref[0] * dq_ref[0].astype(f32)).astype(bf16)
    dc_ref[0] = grad_cross
    grad_att = nt(grad_cross, w_co[...]).astype(bf16)
    first_q = lane_halves(NQ)
    first_k = lane_halves(tokens)
    masks = half_masks()
    for pair in range(PAIRS):
        lanes = slice(pair * 128, pair * 128 + 128)
        upper = slice(HALF + pair * 128, HALF + pair * 128 + 128)
        a2 = grad_att[:, lanes]
        q2 = cq_ref[0, :, lanes]
        k2 = ckv_ref[0, :, lanes]
        v2 = ckv_ref[0, :, upper]
        inner = a2.astype(f32) * att_ref[0, :, lanes]
        dq_two, dk_two, dv_two = [], [], []
        for side in range(2):
            head = pair * 2 + side
            keep = first_q if side == 0 else jnp.logical_not(first_q)
            delta = jnp.sum(jnp.where(keep, inner, 0.0), axis=-1, keepdims=True)
            probs = e_ref[0, head].astype(f32) * coef_ref[0, :, head : head + 1]
            grad_probs = nt(a2 * masks[side], v2)
            grad_scores = (probs * (grad_probs - delta)).astype(bf16)
            dq_two.append(nn(grad_scores, k2))
            dk_two.append(tn(grad_scores, q2))
            dv_two.append(tn(probs.astype(bf16), a2))
        dcq_ref[0, :, lanes] = (jnp.where(first_q, dq_two[0], dq_two[1]) * scaling).astype(bf16)
        dckv_ref[0, :, lanes] = (jnp.where(first_k, dk_two[0], dk_two[1]) * scaling).astype(bf16)
        dckv_ref[0, :, upper] = jnp.where(first_k, dv_two[0], dv_two[1]).astype(bf16)
    part_ref[0] = (
        nt(du_ref[0], w_up[:, :hid]) + nt(dckv_ref[0], w_up[:, hid:])
    ).astype(bf16)


def first_backward(n, *refs):
    order_r, ds_ref, da_ref, db_ref, first_ref, gain_ref = refs[:6]
    source, refs = refs[6 : 6 + n[0][0]], refs[6 + n[0][0] :]
    df_ref, low_ref, do_ref, dg_ref, w_out, sem = refs

    @pl.when(pl.program_id(0) == 0)
    def _():
        fetch_rows(w_out, source, n[0], order_r, OUT_AT, 0, sem)
        dg_ref[...] = jnp.zeros_like(dg_ref)
        end_fetch(w_out, sem)

    grad = da_ref[0].astype(f32) + db_ref[0].astype(f32)
    unit, inv = norm_parts(first_ref[0])
    dg_ref[0:1] += jnp.sum(grad * unit, axis=0, keepdims=True)
    grad_first = ds_ref[0].astype(f32) + norm_back(unit, inv, gain_ref[1:2], grad)
    df_ref[0] = grad_first
    low = grad_first.astype(bf16)
    low_ref[0] = low
    do_ref[0] = nt(low, w_out[...]).astype(bf16)


def attn_backward(n, *refs):
    order_c, do_ref, qkv_ref, p_ref = refs[:4]
    unit, refs = refs[4 : 4 + n[0][0]], refs[4 + n[0][0] :]
    dqkv_ref, part_ref, w_in, wide, sem = refs
    tokens = do_ref.shape[1]
    own = dqkv_ref.shape[1]
    lo = (tokens - own) // 2

    @pl.when(pl.program_id(0) == 0)
    def _():
        fetch_columns(w_in, unit, n[0], order_c, 128, sem)
        end_fetch(w_in, sem)

    first_half = lane_halves(CELLS)
    masks = half_masks()
    for block in range(tokens // CELLS):
        rows = slice(block * CELLS, (block + 1) * CELLS)
        for pair in range(PAIRS):
            lanes = slice(pair * 128, pair * 128 + 128)
            q2 = qkv_ref[0, rows, lanes]
            k2 = qkv_ref[0, rows, HALF + pair * 128 : HALF + pair * 128 + 128]
            v2 = qkv_ref[0, rows, 2 * HALF + pair * 128 : 2 * HALF + pair * 128 + 128]
            g2 = do_ref[0, rows, lanes]
            dq_two, dk_two, dv_two = [], [], []
            for side in range(2):
                probs = p_ref[0, block * HH + pair * 2 + side]
                wide_probs = probs.astype(f32)
                grad_probs = nt(g2 * masks[side], v2)
                delta = jnp.sum(wide_probs * grad_probs, axis=-1, keepdims=True)
                grad_scores = (wide_probs * (grad_probs - delta)).astype(bf16)
                dq_two.append(nn(grad_scores, k2))
                dk_two.append(tn(grad_scores, q2))
                dv_two.append(tn(probs, g2))
            wide[rows, lanes] = jnp.where(first_half, dq_two[0], dq_two[1]) * scaling
            wide[rows, HALF + pair * 128 : HALF + pair * 128 + 128] = (
                jnp.where(first_half, dk_two[0], dk_two[1]) * scaling
            )
            wide[rows, 2 * HALF + pair * 128 : 2 * HALF + pair * 128 + 128] = jnp.where(
                first_half, dv_two[0], dv_two[1]
            )
    low = wide[lo : lo + own].astype(bf16)
    dqkv_ref[0] = low
    part_ref[0] = nt(low, w_in[...]).astype(bf16)


def input_backward(x_ref, df_ref, da_ref, db_ref, gain_ref, dx_ref, dg_ref):
    @pl.when(pl.program_id(0) == 0)
    def _():
        dg_ref[...] = jnp.zeros_like(dg_ref)

    grad = da_ref[0].astype(f32) + db_ref[0].astype(f32)
    unit, inv = norm_parts(x_ref[0].astype(f32))
    dg_ref[0:1] += jnp.sum(grad * unit, axis=0, keepdims=True)
    dx_ref[0] = (df_ref[0] + norm_back(unit, inv, gain_ref[0:1], grad)).astype(bf16)


def query_back_one(n, *refs):
    order_c, one_ref, two_ref = refs[:3]
    unit, refs = refs[3 : 3 + n[0][0]], refs[3 + n[0][0] :]
    dcq_ref, part_ref, w_q, sem = refs
    fetch_columns(w_q, unit, n[0], order_c, CQ_AT, sem)
    end_fetch(w_q, sem)
    for m in range(dcq_ref.shape[0]):
        low = (one_ref[m].astype(f32) + two_ref[m].astype(f32)).astype(bf16)
        dcq_ref[m] = low
        part_ref[m] = nt(low, w_q[...]).astype(bf16)


def query_back_two(q_ref, dq_ref, da_ref, db_ref, gain_ref, out_ref, dg_ref):
    total = jnp.zeros((1, D), f32)
    for m in range(q_ref.shape[0]):
        grad = da_ref[m].astype(f32) + db_ref[m].astype(f32)
        unit, inv = norm_parts(q_ref[m].astype(f32))
        total = total + jnp.sum(grad * unit, axis=0, keepdims=True)
        out_ref[m] = (dq_ref[m].astype(f32) + norm_back(unit, inv, gain_ref[2:3], grad)).astype(bf16)
    dg_ref[...] = jnp.broadcast_to(total, dg_ref.shape)


def weight_grads(n, plan, *refs):
    order_c, order_r = refs[:2]
    count = 1 + max(max(item[0], item[1]) for item in plan)
    sides, refs = refs[2 : 2 + count], refs[2 + count :]
    outs = []
    for k in n:
        outs.append(refs[:k])
        refs = refs[k:]
    acc = refs[0]
    for left, right, unit, by_rows, col0, row0 in plan:
        height, width = sides[left].shape[1], sides[right].shape[1]
        if left == right:
            turned = jnp.concatenate([sides[left][...], jnp.zeros((120, height), f32)], axis=0).T
            acc[0:height, 0:128] = turned
            spread_columns(acc.at[:, 0:128], outs[unit], order_c, col0)
            continue
        for at in range(0, width, HALF):
            acc[0:height] = tn(sides[left][...], sides[right][:, at : at + HALF])
            if by_rows:
                spread_rows(acc, outs[unit], order_r, height, at // HALF, col0, row0)
            else:
                spread_columns(acc, outs[unit], order_c, col0 + at)


def per_device(
    patches,
    queries,
    page_rows,
    window_mask,
    query_lengths,
    plan,
    norm_attn,
    norm_mlp,
    norm_query,
    attn_input,
    attn_output,
    mlp_up,
    mlp_down,
    cross_query,
    cross_pair,
    cross_output,
    patch_cotangent,
    query_cotangent,
):
    core = lax.axis_index("section")
    zi = lax.axis_index("dp")
    qi = lax.axis_index("seq")
    nz, ns = lax.axis_size("dp"), lax.axis_size("seq")
    rows = attn_input.shape[1]
    hid = mlp_up.shape[2] // 2
    manual = rows % 16 == 0 and ns == 4 and nz & (nz - 1) == 0
    near = nz // 2
    batches, row_count, col_count = patches.shape[:3]
    tokens = row_count * col_count
    core_zero = core == 0

    def swap(x):
        return lax.ppermute(x, "section", SWAP)

    def across(x, r):
        return lax.ppermute(x, "seq", [(j, j ^ r) for j in range(ns)])

    def tied(x, after):
        return x if after is None else lax.optimization_barrier((x, after))[0]

    far = (zi // near) ^ core
    if manual:
        order_c = [((zi ^ r) * ns + (qi ^ p)) for p in range(ns) for r in range(nz)]
        order_r = [
            ((zi ^ (far * near + k)) - core * near) * ns + (qi ^ p)
            for p in range(ns)
            for k in range(near)
        ]
    else:
        order_c = order_r = [zi]
    order_s = [qi ^ p for p in range(ns)]
    order_c, order_r, order_s = (
        jnp.stack(o).astype(jnp.int32) for o in (order_c, order_r, order_s)
    )

    gain_block = jnp.stack([norm_attn[0], norm_mlp[0], norm_query[0]], axis=1)
    gain_block = jnp.pad(gain_block, ((0, 0), (0, 125)))
    win, up, cq, cp = attn_input[0], mlp_up[0], cross_query[0], cross_pair[0]

    def half_columns(side):
        def half(a, w):
            return a[:, side * w : (side + 1) * w]

        first = [half(win[:, k * D : (k + 1) * D], HALF) for k in range(3)]
        return [
            jnp.concatenate([gain_block] + first + [half(cq, HALF)], axis=1),
            jnp.concatenate([half(up, hid), half(cp[:, :D], HALF), half(cp[:, D:], HALF)], axis=1),
        ]

    halves = [half_columns(side) for side in range(2)]

    def fold(w):
        return jnp.stack(
            [
                jnp.concatenate(
                    [
                        w[b * rows : (b + 1) * rows, side * HALF : (side + 1) * HALF]
                        for b in range(w.shape[0] // rows)
                    ],
                    axis=1,
                )
                for side in range(2)
            ]
        )

    down_co = jnp.concatenate([mlp_down[0], cross_output[0]], axis=0)

    def z_pairs(bit):
        return [
            (c * nz + j, c * nz + (j ^ bit))
            for c in range(2)
            for j in range(c * near, (c + 1) * near)
        ]

    def z_step(parts, bit, after):
        out = []
        for stack, by_rows in parts:
            stack = tied(stack, after)
            if not by_rows:
                got = lax.ppermute(stack, "dp", [(j, j ^ bit) for j in range(nz)])
                out.append((jnp.concatenate([stack, got]), False, got))
                continue
            got = lax.ppermute(stack, ("section", "dp"), z_pairs(bit))
            if bit < near:
                stack = jnp.concatenate([stack, got])
            else:
                stack = jnp.where(far == 0, stack, got)
                stack = stack.reshape((nz,) + stack.shape[2:])
            out.append((stack, True, got))
        return [o[:2] for o in out], tuple(o[2] for o in out)

    units = [[None] * 3 for _ in range(2)]
    counts = [[None] * 3 for _ in range(2)]
    if manual:
        col_send = [jnp.where(core_zero, b, a) for a, b in zip(*halves)]
        col_mine = [jnp.where(core_zero, a, b) for a, b in zip(*halves)]
        row_mine = [fold(attn_output[0]), fold(down_co)]
        col_recv = [swap(col_send[0])]
        row_recv = [swap(row_mine[0])]
        col_recv.append(swap(tied(col_send[1], (col_recv[0], row_recv[0]))))
        row_recv.append(swap(tied(row_mine[1], (col_recv[0], row_recv[0]))))

        queue = []
        for layer in range(2):
            own_layer = core == layer
            cols = [jnp.where(own_layer, a, b)[None] for a, b in zip(col_mine, col_recv)]
            folded = [jnp.where(own_layer, a, b)[None] for a, b in zip(row_mine, row_recv)]
            queue += [[(cols[0], False), (folded[0], True)], [(cols[1], False)], [(folded[1], True)]]
        bits = []
        while 2 ** len(bits) < nz:
            bits.append(2 ** len(bits))
        last_rows = queue.pop()[0][0][0]
        count = len(queue)

        def early_steps(k, after):
            tokens_of = ()
            for bit in bits[:-1]:
                queue[k], after = z_step(queue[k], bit, after)
                tokens_of += after
            return tokens_of

        lead = early_steps(0, None)
        queue[0], _ = z_step(queue[0], bits[-1], lead)
        ahead = early_steps(1, lead)
        token = ()
        messages = []
        from_x = from_y = jnp.zeros((nz, rows, 0), bf16)
        cut = 0
        before = None
        for k in range(count + 1):
            low, high = from_x[..., :cut], from_y[..., cut:]
            x_parts, y_parts = [high], [low]
            own = None
            if k < count:
                parts = [stack for stack, _ in queue[k]]
                own = parts[0] if len(parts) == 1 else jnp.concatenate(parts, axis=2)
                own = tied(own, token)
                x_parts.append(own)
                y_parts.append(own)
            sent_x, sent_y = jnp.concatenate(x_parts, axis=2), jnp.concatenate(y_parts, axis=2)
            messages.append((sent_x, sent_y))
            got_x, got_y = across(sent_x, 1), across(sent_y, 2)
            if k + 1 < count:
                queue[k + 1], got = z_step(queue[k + 1], bits[-1], (token, ahead))
                ahead = early_steps(k + 2, got) if k + 2 < count else got
            if before is not None:
                b = k - 1
                units[b // 3][b % 3] = before[0] + [got_y, got_x]
                counts[b // 3][b % 3] = (5,) + before[1] + (cut,)
            if own is None:
                break
            before = ([own, got_x, got_y], (high.shape[2], low.shape[2]))
            from_x, from_y = got_x[..., high.shape[2] :], got_y[..., low.shape[2] :]
            cut = own.shape[2] // 256 * 128
            token = (got_x, got_y)
        stack = jnp.stack([last_rows] + [across(last_rows, r) for r in range(1, ns)])[None]
        stack = tied(stack, ahead)
        for bit in bits:
            got = lax.ppermute(stack, ("section", "dp"), z_pairs(bit))
            stack = jnp.concatenate([stack, got]) if bit < near else jnp.where(far == 0, stack, got)
        units[1][2] = [stack]
        counts[1][2] = (1, 0, 0, 0)
        counts = tuple(tuple(c) for c in counts)
    else:

        def gather_all(x):
            return lax.all_gather(
                lax.all_gather(x, ("dp", "seq"), axis=0, tiled=True), "section", axis=0
            )

        whole_cols = [[gather_all(h[k]) for h in halves] for k in range(2)]
        whole_rows = [gather_all(x) for x in (attn_output[0], mlp_down[0], cross_output[0])]
        for layer in range(2):
            cols = [jnp.where(core_zero, a[layer], b[layer]) for a, b in whole_cols]
            mine = [
                lax.dynamic_slice_in_dim(w[layer], core * (w.shape[1] // 2), w.shape[1] // 2, 0)
                for w in whole_rows
            ]
            units[layer] = [[cols[0], mine[0]], [cols[1]], [jnp.concatenate(mine[1:], axis=0)]]
        counts = (((2, 0, 0, 0), (1, 0, 0, 0), (1, 0, 0, 0)),) * 2
        messages = [()] * 7

    order = jnp.arange(batches)
    inverse = jnp.sum(jnp.where(plan[0][None, :] == order[:, None], order[None, :], 0), axis=1)
    query_start = jnp.take(queries, inverse, axis=0)
    query_given = jnp.take(query_cotangent, inverse, axis=0)
    lengths = jnp.take(query_lengths, inverse)
    live = (jnp.arange(NQ)[None, :] < lengths[:, None]).astype(f32)[:, :, None]
    window_rows = qi * (row_count // WIN) + jnp.arange(row_count // WIN)
    marks = (window_rows[None, :, None] < page_rows[:, None, None]) & (window_mask == 1)
    valid = jnp.repeat(jnp.repeat(marks, WIN, axis=1), WIN, axis=2)
    valid = valid.reshape(batches, 1, tokens).astype(f32)
    blocks_wide = (row_count + WIN) // WIN
    cell = jnp.arange(CELLS)
    frame_row = qi * row_count - WIN // 2 + jnp.arange(blocks_wide)[:, None] * WIN + cell // WIN
    inside = (frame_row >= 0) & (frame_row < row_count * ns)
    side_of = (cell % WIN) < WIN // 2
    same = side_of[:, None] == side_of[None, :]
    mask = jnp.where(inside[:, None, :] & same[None], 0.0, hidden_value).astype(f32)

    pages = patches.reshape(batches, tokens, D)
    given = patch_cotangent.reshape(batches, tokens, D)

    def widened(edge_source):
        top = lax.ppermute(
            edge_source[:, tokens - RIM :], "seq", [(j, j + 1) for j in range(ns - 1)]
        )
        bottom = lax.ppermute(edge_source[:, :RIM], "seq", [(j + 1, j) for j in range(ns - 1)])
        return jnp.concatenate([top, edge_source, bottom], axis=1)

    def pieces(unit):
        return [(piece, ANY) for piece in unit]

    def shaped(shape, dtype, batched=True):
        return (shape, dtype, per_batch(shape) if batched else whole(shape))

    def batched(a):
        return (a, per_batch(a.shape))

    def full(a):
        return (a, whole(a.shape))

    dma = pltpu.SemaphoreType.DMA

    def forward(layer, x, query, query_parts):
        u, n = units[layer], counts[layer]
        shifted = layer == 1
        wide_x = wide_x1 if shifted else x
        wide = wide_x.shape[1]
        blocks = wide // CELLS
        wide_x = tied(wide_x, messages[2 + 3 * layer])
        ins = [(order_c, SMEM), (order_r, SMEM), batched(wide_x)]
        if shifted:
            ins.append(full(mask))
        h1, qkv, probs, mixed, part, gains = run(
            partial(attn_forward, n, shifted),
            "attn_forward",
            (batches,),
            ins + pieces(u[0]),
            [
                shaped((batches, tokens, D), bf16),
                shaped((batches, wide, 3 * HALF), bf16),
                shaped((batches, blocks * HH, CELLS, CELLS), bf16),
                shaped((batches, tokens, HALF), bf16),
                shaped((batches, tokens, D), bf16),
                shaped((8, D), f32, False),
            ],
            [
                pltpu.VMEM((D, 128 + 3 * HALF), bf16),
                pltpu.VMEM((HALF, D), bf16),
                pltpu.VMEM((wide, HALF), f32),
                pltpu.VMEM((wide, D), f32),
                dma,
                dma,
            ],
            10,
        )
        other = swap(part)
        q_ins = [(order_c, SMEM), full(query), full(gains)]
        q_outs = [
            shaped((batches, NQ, D), bf16, False),
            shaped((batches, NQ, HALF), bf16, False),
        ]
        if query_parts is not None:
            q_ins += [full(query_parts[0]), full(query_parts[1]), full(live)]
            q_outs = [shaped((batches, NQ, D), bf16, False)] + q_outs
        got = run(
            partial(query_in, n, query_parts is not None),
            "query_in",
            (),
            q_ins + pieces(u[0]),
            q_outs,
            [pltpu.VMEM((D, HALF), bf16), dma],
            2.5,
        )
        if query_parts is not None:
            query, got = got[0], got[1:]
        hq, cq_now = got
        first, h2, slope, act, second_part, ckv, e, o = run(
            partial(mlp_forward, n),
            "mlp_forward",
            (batches,),
            [
                (order_c, SMEM),
                (order_r, SMEM),
                batched(tied(x, messages[min(4 + 2 * layer, len(messages) - 1)])),
                batched(part),
                batched(other),
                full(gains),
                batched(cq_now),
                batched(valid),
            ]
            + pieces(u[1])
            + pieces(u[2]),
            [
                shaped((batches, tokens, D), f32),
                shaped((batches, tokens, D), bf16),
                shaped((batches, tokens, hid), bf16),
                shaped((batches, tokens, hid), bf16),
                shaped((batches, tokens, D), bf16),
                shaped((batches, tokens, D), bf16),
                shaped((batches, HH, NQ, tokens), bf16),
                shaped((batches, NQ, HALF + 128), bf16),
            ],
            [pltpu.VMEM((D, hid + D), bf16), pltpu.VMEM((hid, D), bf16), dma, dma],
            14,
        )
        second_other = swap(second_part)
        os = [o] + [across(o, r) for r in range(1, ns)]
        att, att_low, coef, q_part = run(
            partial(query_out, n, ns),
            "query_out",
            (),
            [(order_r, SMEM), (order_s, SMEM)]
            + [full(a) for a in os]
            + pieces(u[2]),
            [
                shaped((batches, NQ, HALF), f32, False),
                shaped((batches, NQ, HALF), bf16, False),
                shaped((batches, NQ, 128), f32, False),
                shaped((batches, NQ, D), bf16, False),
            ],
            [
                pltpu.VMEM((HALF, D), bf16),
                pltpu.VMEM((ns, batches, NQ, HALF + 128), bf16),
                dma,
            ],
            4.5,
        )
        q_other = swap(q_part)
        x_next = (first + (second_part.astype(f32) + second_other.astype(f32))).astype(bf16)
        kept = dict(
            x=x, query=query, h1=h1, qkv=qkv, probs=probs, mixed=mixed, gains=gains, hq=hq,
            cq=cq_now, first=first, h2=h2, slope=slope, act=act, ckv=ckv, e=e, att=att,
            att_low=att_low, coef=coef,
        )
        return x_next, (q_part, q_other), kept

    def sums(kernel_plan, sides, shapes, height, name, after=None):
        flat = run(
            partial(weight_grads, tuple(len(unit) for unit in shapes), kernel_plan),
            name,
            (),
            [(order_c, SMEM), (order_r, SMEM)] + [full(s) for s in sides],
            [shaped(shape, bf16, False) for unit in shapes for shape in unit],
            [pltpu.VMEM((height, HALF), f32)],
            12 if height > D else 6,
        )
        out = []
        for unit in shapes:
            out.append(flat[: len(unit)])
            flat = flat[len(unit) :]
        return out

    def unit_shapes(cols, row_height):
        if not manual:
            shapes = [(D, cols)] if cols else []
            return shapes + ([(row_height, D)] if row_height else [])
        width = cols + row_height // (rows * nz * ns // 2) * HALF
        return [(nz, rows, width)] * 3 + [(near, rows, width)] * 2

    def reduce_one(unit, after):
        own, one, two, low, high = unit
        low, high = tied((low, high), after)
        low, high = across(low, 2), across(high, 1)
        return (own, one, two, low, high), (low, high)

    def reduce_two(unit, after):
        own, one, two, low, high = tied(unit, after)
        one = jnp.concatenate([one[:near] + low, one[near:]])
        two = jnp.concatenate([two[:near], two[near:] + high])
        one, two = across(one, 1), across(two, 2)
        return (own, one, two), (one, two)

    def reduce_three(unit, cols, after):
        own, one, two = tied(unit, after)
        total = own.astype(f32) + one.astype(f32) + two.astype(f32)
        col, row = total[..., :cols], total[..., cols:]
        sent = col[near:].astype(bf16)
        got_col = lax.ppermute(sent, "dp", [(j, j ^ near) for j in range(nz)])
        sent = row.astype(bf16)
        got_row = lax.ppermute(sent, ("section", "dp"), [(b, a) for a, b in z_pairs(near)])
        return [(col[:near], got_col), (row, got_row)], (got_col, got_row)

    def reduce_four(parts, after):
        out = []
        token = ()
        for by_rows, (total, got) in enumerate(tied(parts, after)):
            total = total + got.astype(f32)
            if by_rows:
                total = total.reshape((near, 2) + total.shape[1:])
            bit = near // 2
            while bit:
                sent = total[bit:].astype(bf16)
                pairs = [(b, a) for a, b in z_pairs(bit)] if by_rows else [
                    (j, j ^ bit) for j in range(nz)
                ]
                got = lax.ppermute(sent, ("section", "dp") if by_rows else "dp", pairs)
                token += (got,)
                total = total[:bit] + got.astype(f32)
                bit //= 2
            out.append(total[0])
        return out, token

    def unfold(row):
        blocks = row.shape[2] // HALF
        return jnp.concatenate(
            [
                jnp.concatenate([row[side, :, b * HALF : (b + 1) * HALF] for side in range(2)], axis=1)
                for b in range(blocks)
            ],
            axis=0,
        )

    def reduce_plain(unit, cols, heights):
        out = []
        if cols:
            out.append(lax.psum_scatter(unit[0], ("dp", "seq"), scatter_dimension=0, tiled=True))
        if len(unit) > 1 or not cols:
            cut = heights[0] * nz * ns // 2
            pieces_of = [unit[-1][:cut], unit[-1][cut:]]
            out += [
                lax.psum_scatter(
                    lax.all_gather(piece, "section", axis=0, tiled=True),
                    ("dp", "seq"),
                    scatter_dimension=0,
                    tiled=True,
                )
                for piece in pieces_of
            ]
        return [o.astype(f32) for o in out]

    share = 1.0 / ns

    def backward(layer, grad_patch, grad_query, kept, emit):
        u, n = units[layer], counts[layer]
        shifted = layer == 1
        gains = kept["gains"]
        du, dckv, dcq_part, part, dcross = run(
            partial(mlp_backward, n),
            "mlp_backward",
            (batches,),
            [(order_c, SMEM), (order_r, SMEM)]
            + [
                batched(a)
                for a in (
                    grad_patch, kept["slope"], kept["e"], kept["coef"], grad_query, live,
                    kept["att"], kept["cq"], kept["ckv"],
                )
            ]
            + pieces(u[1])
            + pieces(u[2]),
            [
                shaped((batches, tokens, hid), bf16),
                shaped((batches, tokens, D), bf16),
                shaped((batches, NQ, HALF), bf16),
                shaped((batches, tokens, D), bf16),
                shaped((batches, NQ, D), bf16),
            ],
            [
                pltpu.VMEM((D, hid + D), bf16),
                pltpu.VMEM((hid, D), bf16),
                pltpu.VMEM((HALF, D), bf16),
                dma,
                dma,
                dma,
            ],
            14,
        )
        emit("mlp", part)
        other = swap(part)
        dcq_got = across(dcq_part, 1)

        def flat(a):
            return a.reshape(-1, a.shape[-1])

        row_at = hid + D if manual else 0
        row_base = hid // (nz * ns // 2) // rows * HALF if manual else 0
        early = sums(
            (
                (0, 1, 0, False, 0, 0),
                (0, 2, 0, False, hid, 0),
                (3, 4, 0, True, row_at, 0),
                (5, 6, 0, True, row_at + row_base, hid),
            ),
            [
                flat(kept["h2"]), flat(du), flat(dckv), flat(kept["act"]), flat(grad_patch),
                flat(kept["att_low"]), flat(dcross * jnp.asarray(share, bf16)),
            ],
            [unit_shapes(hid + D, hid + HALF)],
            hid,
            "early_grads",
        )
        part = tied(part, early[0][0])
        dcq_got = tied(dcq_got, early[0][0])
        bit = 2
        while bit < ns:
            dcq_part = (dcq_part.astype(f32) + dcq_got.astype(f32)).astype(bf16)
            dcq_got = across(dcq_part, bit)
            bit *= 2
        emit("early", (early[0], dcq_part))
        grad_first, first_low, grad_mixed, dg_mlp = run(
            partial(first_backward, n),
            "first_backward",
            (batches,),
            [(order_r, SMEM)]
            + [batched(a) for a in (grad_patch, part, other, kept["first"])]
            + [full(gains)]
            + pieces(u[0]),
            [
                shaped((batches, tokens, D), f32),
                shaped((batches, tokens, D), bf16),
                shaped((batches, tokens, HALF), bf16),
                shaped((8, D), f32, False),
            ],
            [pltpu.VMEM((HALF, D), bf16), dma],
            5.6,
        )
        wide_grad = widened(grad_mixed) if shifted else grad_mixed
        emit("first", grad_mixed)
        wide = wide_grad.shape[1]
        dqkv, part = run(
            partial(attn_backward, n),
            "attn_backward",
            (batches,),
            [(order_c, SMEM)]
            + [batched(a) for a in (wide_grad, kept["qkv"], kept["probs"])]
            + pieces(u[0]),
            [shaped((batches, tokens, 3 * HALF), bf16), shaped((batches, tokens, D), bf16)],
            [pltpu.VMEM((D, 3 * HALF), bf16), pltpu.VMEM((wide, 3 * HALF), f32), dma],
            15,
        )
        emit("attn", part)
        other = swap(part)
        dcq_got = tied(dcq_got, dqkv)
        dcq, q_part = run(
            partial(query_back_one, n),
            "query_back_one",
            (),
            [(order_c, SMEM), full(dcq_part), full(dcq_got)] + pieces(u[0]),
            [shaped((batches, NQ, HALF), bf16, False), shaped((batches, NQ, D), bf16, False)],
            [pltpu.VMEM((D, HALF), bf16), dma],
            2.5,
        )
        q_other = swap(q_part)
        last_x = kept["x"]
        dx, dg_attn = run(
            input_backward,
            "input_backward",
            (batches,),
            [batched(a) for a in (last_x, grad_first, part, other)] + [full(gains)],
            [shaped((batches, tokens, D), bf16), shaped((8, D), f32, False)],
            [],
            3,
        )
        dq, dg_query = run(
            query_back_two,
            "query_back_two",
            (),
            [full(a) for a in (kept["query"], grad_query, q_part, q_other, gains)],
            [shaped((batches, NQ, D), bf16, False), shaped((8, D), f32, False)],
            [],
            1,
        )
        dgains = jnp.concatenate([dg_attn[0:1], dg_mlp[0:1], dg_query[0:1] * share], axis=0)
        emit(
            "late",
            ([
                flat(kept["h1"]), flat(dqkv), flat(kept["hq"]), flat(dcq * jnp.asarray(share, bf16)),
                flat(kept["mixed"]), flat(first_low),
            ], dgains),
        )
        return dx, dq

    x1, q_parts, kept0 = forward(0, pages, query_start, None)
    wide_x1 = widened(x1)
    x2, q_parts_two, kept1 = forward(1, x1, query_start, q_parts)
    query_last = (
        kept1["query"].astype(f32)
        + live * (q_parts_two[0].astype(f32) + q_parts_two[1].astype(f32))
    ).astype(bf16)

    widths = (hid + D, hid + D, 8 * HALF + 128)
    out_rows = attn_output.shape[1]
    heights = [(mlp_down.shape[1], cross_output.shape[1])] * 2 + [(out_rows, out_rows)]
    state = [None] * 3
    late_sides = []

    rounds = [()]

    def one_round(*items, after=()):
        for unit, step in items:
            now = state[unit]
            if not manual:
                if step == 4:
                    now = reduce_plain(now, widths[unit], heights[unit])
            elif step == 1:
                now, got = reduce_one(now, after)
            elif step == 2:
                now, got = reduce_two(now, after)
            elif step == 3:
                now, got = reduce_three(now, widths[unit], after)
            else:
                now, got = reduce_four(now, after)
                rows_of = unfold(now[1])
                cut = heights[unit][0]
                now = [now[0], rows_of[:cut], rows_of[cut:]]
            state[unit] = now
            rounds[unit, step] = got if manual else ()

    rounds = {}

    def emit_late_layer(what, value):
        if what == "early":
            state[1] = value[0]
            one_round((1, 1), after=value[1])
        elif what == "attn":
            one_round((1, 2), after=value)
        elif what == "late":
            late_sides.extend(value)

    def emit_first_layer(what, value):
        if what == "early":
            state[0] = value[0]
            one_round((0, 1), after=value[1])
            one_round((1, 3), after=value[1])
        elif what == "first":
            one_round((0, 2), after=value)
        elif what == "late":
            sides = tied(late_sides[0] + value[0], rounds[1, 3])
            gain_sums = jnp.concatenate(
                [value[1], late_sides[1], jnp.zeros((2, D), f32)], axis=0
            )
            row_at = 8 * HALF + 128
            (state[2],) = sums(
                [
                    item
                    for k in range(2)
                    for item in (
                        (6 * k, 6 * k + 1, 0, False, 4 * HALF * k, 0),
                        (6 * k + 2, 6 * k + 3, 0, False, 4 * HALF * k + 3 * HALF, 0),
                        (6 * k + 4, 6 * k + 5, 0, True, row_at + HALF * k, HALF * k),
                    )
                ]
                + [(12, 12, 0, False, 8 * HALF, 0)],
                sides + [gain_sums],
                [unit_shapes(8 * HALF + 128, 2 * HALF)],
                D,
                "late_grads",
            )
            one_round((2, 1))

    given = tied(given, x2)
    kept1["h2"] = tied(kept1["h2"], query_last)
    dx1, dq1 = backward(1, given, query_given, kept1, emit_late_layer)
    dx0, dq0 = backward(0, dx1, dq1, kept0, emit_first_layer)
    one_round((1, 4), after=state[2][0])
    one_round((0, 3), after=state[2][0])
    one_round((2, 2), after=(rounds[0, 2], state[2][0]))
    one_round((2, 3), after=rounds[0, 3])
    one_round((0, 4), after=rounds[2, 2])

    def handed(low, high):
        return [swap(jnp.where(core_zero, b, a)) for a, b in zip(low, high)]

    got_early = handed(
        [state[0][0], jnp.concatenate(state[0][1:], axis=0)],
        [state[1][0], jnp.concatenate(state[1][1:], axis=0)],
    )
    one_round((2, 4), after=(rounds[0, 4], got_early))
    cols, rows_of = state[2][0], state[2][1:]
    low_cols, high_cols = cols[:, : 4 * HALF], cols[:, 4 * HALF : 8 * HALF]
    got_late = handed([high_cols, rows_of[1]], [low_cols, rows_of[0]])
    own_early = [jnp.where(core_zero, a, b) for a, b in zip(state[0], state[1])]
    own_late = [jnp.where(core_zero, high_cols, low_cols)]
    own_late.append(jnp.where(core_zero, rows_of[1], rows_of[0]))
    cut = heights[0][0]
    mine = own_early + own_late
    theirs = [got_early[0], got_early[1][:cut], got_early[1][cut:]] + got_late

    def col_halves(k):
        low = jnp.where(core_zero, mine[k], theirs[k])
        high = jnp.where(core_zero, theirs[k], mine[k])
        return low, high

    holder = zi // near if manual else core

    def row_block(k):
        return jnp.where(holder == core, mine[k], theirs[k])

    low, high = col_halves(0)
    grad_up = jnp.concatenate([low[:, :hid], high[:, :hid]], axis=1)
    grad_pair = jnp.concatenate(
        [
            low[:, hid : hid + HALF], high[:, hid : hid + HALF],
            low[:, hid + HALF :], high[:, hid + HALF :],
        ],
        axis=1,
    )
    low, high = col_halves(3)
    grad_in = jnp.concatenate(
        [side[:, k * HALF : (k + 1) * HALF] for k in range(3) for side in (low, high)], axis=1
    )
    grad_cq = jnp.concatenate([low[:, 3 * HALF :], high[:, 3 * HALF :]], axis=1)
    grad_down, grad_co, grad_out = row_block(1), row_block(2), row_block(4)

    gain_rows = jnp.where(core_zero, cols[:, 8 * HALF : 8 * HALF + 3], cols[:, 8 * HALF + 3 : 8 * HALF + 6])
    own_gains = gain_rows.T

    patch_ends = jnp.where(core_zero, dx0, x2).reshape(1, batches, row_count, col_count, D)
    query_ends = jnp.take(jnp.where(core_zero, dq0, query_last), plan[0], axis=0)[None]
    return (
        patch_ends,
        query_ends,
        own_gains[0:1],
        own_gains[1:2],
        own_gains[2:3],
        grad_in[None],
        grad_out[None],
        grad_up[None],
        grad_down[None],
        grad_cq[None],
        grad_pair[None],
        grad_co[None],
    )


def solution(mesh):
    return jax.shard_map(
        per_device,
        mesh=mesh,
        in_specs=(
            P("dp", "seq", None, None),
            P("dp", None, None),
            P("dp"),
            P("dp", "seq", None),
            P("dp"),
            P("dp", None),
            P("section", ("dp", "seq")),
            P("section", ("dp", "seq")),
            P("section", ("dp", "seq")),
            P("section", ("dp", "seq"), None),
            P("section", ("dp", "seq"), None),
            P("section", ("dp", "seq"), None),
            P("section", ("dp", "seq"), None),
            P("section", ("dp", "seq"), None),
            P("section", ("dp", "seq"), None),
            P("section", ("dp", "seq"), None),
            P("dp", "seq", None, None),
            P("dp", None, None),
        ),
        out_specs=(
            P("section", "dp", "seq", None, None),
            P("section", "dp", None, None),
            P("section", ("dp", "seq")),
            P("section", ("dp", "seq")),
            P("section", ("dp", "seq")),
            P("section", ("dp", "seq"), None),
            P("section", ("dp", "seq"), None),
            P("section", ("dp", "seq"), None),
            P("section", ("dp", "seq"), None),
            P("section", ("dp", "seq"), None),
            P("section", ("dp", "seq"), None),
            P("section", ("dp", "seq"), None),
        ),
        check_vma=False,
    )
```

time: 776 us -> 631 us (0.81)
  waiting for transfers between devices: 306 us -> 214 us
  starting transfers between devices: 209 us -> 137 us
  other arithmetic: 38.9 us -> 48.5 us
    ppermute x66 -> x37, waiting for transfers between devices: 169 us -> 76.8 us  [across(): return lax.ppermute(x, 'seq', [(j, j ^ r) for j in range(ns)])]
    ppermute x64 -> x28, starting transfers between devices: 121 us -> 80.3 us  [the longest x6 22.7 us: z_step(): got = lax.ppermute(stack, ('section', 'dp'), z_pairs(bit))]
    ppermute x66 -> x37, starting transfers between devices: 77.8 us -> 46.2 us  [across(): return lax.ppermute(x, 'seq', [(j, j ^ r) for j in range(ns)])]
    ppermute x2, waiting for transfers between devices: 12.2 us -> 0.01 us  [widened(): lax.ppermute(edge_source[:, tokens - RIM:], 'seq', [(j, j + 1) for j in r...]
    ppermute x64 -> x28, waiting for transfers between devices: 117 us -> 128 us  [the longest x8 43.6 us: z_step(): got = lax.ppermute(stack, 'dp', [(j, j ^ bit) for j in range(nz)])]
    concatenate x1 -> x24, other arithmetic: 0.03 us -> 9.84 us  [the longest x4 3.71 us: per_device(): jnp.concatenate(y_parts, axis=2)]
    pallas_call x24 -> x23, Pallas kernels: 176 us -> 178 us  [run(): pl.pallas_call(kernel, grid=grid, in_specs=[s for _, s in ins], out_specs...]
    unnamed x242 -> x169, local copies, waits for them, and re-layouts: 20.1 us -> 21.8 us
  transfers between devices with their start and end apart: 150 -> 89, of which waited for: 48 -> 32; matrix products, arithmetic and copies ran while one was open for 7% -> 12% of each run, Pallas kernels for 19% -> 23%
where the time goes in v2:
time: 631 us; the launch traced here: 621 us
  waiting for transfers between devices  214 us (34%)
  Pallas kernels  178 us (28%)
  starting transfers between devices  137 us (22%)
  other arithmetic  48.5 us (8%)
  local copies, waits for them, and re-layouts  40.9 us (6%)
    pallas_call x23, Pallas kernels, run(): pl.pallas_call(kernel, grid=grid, in_specs=[s for _, s in ins], out_specs...  178 us
    ppermute x37, waiting for transfers between devices, across(): return lax.ppermute(x, 'seq', [(j, j ^ r) for j in range(ns)])  76.8 us
    ppermute x37, starting transfers between devices, across(): return lax.ppermute(x, 'seq', [(j, j ^ r) for j in range(ns)])  46.2 us
    ppermute x8, waiting for transfers between devices, z_step(): got = lax.ppermute(stack, 'dp', [(j, j ^ bit) for j in range(nz)])  43.6 us
    ppermute x3, waiting for transfers between devices, reduce_three(): got_col = lax.ppermute(sent, 'dp', [(j, j ^ near) for j in range(nz)])  37.1 us
    ppermute x6, starting transfers between devices, z_step(): got = lax.ppermute(stack, ('section', 'dp'), z_pairs(bit))  22.7 us
    ppermute x3, waiting for transfers between devices, reduce_three(): lax.ppermute(sent, ('section', 'dp'), [(b, a) for a, b in z_pairs(near)])  22.4 us
    unnamed x169, local copies, waits for them, and re-layouts  21.8 us
  transfers between devices with their start and end apart: 89, of which 32 were waited for; matrix products, arithmetic and copies ran while one was open for 12% of the time, Pallas kernels for 23%

profile of v2, /device:TPU:0, one launch (start us, length us, event | category | flops | bytes accessed | tf_op | source)
XLA Modules:
  0.0 621.4 jit_solution(14131640630964452420)
XLA Ops:
  10.2 4.9 collective-permute-start.3
  18.6 2.5 collective-permute-done.1
  21.1 2.4 collective-permute-start.5
  24.4 2.5 collective-permute-start.8
  27.8 9.7 %collective-permute-done.8 = bf16[1,48,2304]{2,1,0:T(8,128)(2,1)S(1)} collective-permute-done((bf16[1,48,2304]{2,1,0:T(8,128)(2,1)S(1)}, bf16[1,48,2304]{2,1,0:T(8,128)(2,1)S(1)}, u32[]{:S(2)}, u32[]{:S(2)}) %collective-permute-start.8) | collective-permute-done | bytes 221216 | tf_op jit(solution)/shard_map/ppermute | solution.py:654
  37.5 2.2 collective-permute-start.9
  44.5 15.9 %collective-permute-done.9 = bf16[2,48,2304]{2,1,0:T(8,128)(2,1)S(1)} collective-permute-done((bf16[2,48,2304]{2,1,0:T(8,128)(2,1)S(1)}, bf16[2,48,2304]{2,1,0:T(8,128)(2,1)S(1)}, u32[]{:S(2)}, u32[]{:S(2)}) %collective-permute-start.9) | collective-permute-done | bytes 442400 | tf_op jit(solution)/shard_map/ppermute | solution.py:654
  60.4 3.1 collective-permute-start.13
  63.6 6.1 collective-permute-done.13
  77.9 3.0 copy.73
  84.0 8.6 %collective-permute-start.18 = (bf16[1,2,48,384]{3,2,1,0:T(8,128)(2,1)S(1)}, bf16[1,2,48,384]{3,2,1,0:T(8,128)(2,1)S(1)}, u32[]{:S(2)}, u32[]{:S(2)}) collective-permute-start(bf16[1,2,48,384]{3,2,1,0:T(8,128)(2,1)S(1)} %get-tuple-element.199), channel_id=1, source_target_pairs={{0,4},{4,0},{24,28},{28,24},{1,5},{5,1},{25,29},{29,25},{2,6},{6,2... | collective-permute-start | bytes 221192 | tf_op jit(solution)/shard_map/ppermute | solution.py:657
  95.0 3.1 collective-permute-start.41
  98.2 9.2 %collective-permute-done.11.refs_6_.refs_10_.refs_13_.refs_9_.refs_7_ = bf16[4,48,3328]{2,1,0:T(8,128)(2,1)} collective-permute-done((bf16[4,48,3328]{2,1,0:T(8,128)(2,1)}, bf16[4,48,3328]{2,1,0:T(8,128)(2,1)}, u32[]{:S(2)}, u32[]{:S(2)}) %collective-permute-start.11) | collective-permute-done | bytes 1277984 | tf_op jit(solution)/shard_map/ppermute | solution.py:590
  107.3 4.9 collective-permute-start.17
  120.2 3.1 collective-permute-done.41
  124.6 6.9 %collective-permute-done.19 = bf16[2,48,1664]{2,1,0:T(8,128)(2,1)S(1)} collective-permute-done((bf16[2,48,1664]{2,1,0:T(8,128)(2,1)S(1)}, bf16[2,48,1664]{2,1,0:T(8,128)(2,1)S(1)}, u32[]{:S(2)}, u32[]{:S(2)}) %collective-permute-start.19) | collective-permute-done | bytes 319520 | tf_op jit(solution)/shard_map/ppermute | solution.py:654
  132.4 5.1 collective-permute-done.23
  139.9 4.7 collective-permute-start.22
  144.8 9.4 %attn_forward.2 = (bf16[2,288,768]{2,1,0:T(8,128)(2,1)}, bf16[2,288,1152]{2,1,0:T(8,128)(2,1)}, bf16[2,12,144,144]{3,2,1,0:T(8,128)(2,1)}, bf16[2,288,384]{2,1,0...) custom-call(s32[16]{0:T(128)S(1)} %stack.151.refs_0_, s32[8]{0:T(128)S(1)} %stack.134.refs_1_.refs_0_, ...), custom_call_target="tpu_custom_call" | custom-call | flops 11500000256 | tf_op jit(solution)/shard_map/attn_forward/pallas_call | solution.py:45
  156.6 9.3 %collective-permute-start.42 = (bf16[1,4,2,48,1920]{4,3,2,1,0:T(8,128)(2,1)S(1)}, bf16[1,4,2,48,1920]{4,3,2,1,0:T(8,128)(2,1)S(1)}, u32[]{:S(2)}, u32[]{:S(2)}) collective-permute-start(bf16[1,4,2,48,1920]{4,3,2,1,0:T(8,128)(2,1)S(1)} %maximum_bitcast_fusion), channel_id=1, source_target_pairs={{0,4},{4,0},{24,28},{28,24},{1,5},{5,1},{25,29},{29,25},{2,6},{6,2... | collective-permute-start | bytes 4423688 | tf_op jit(solution)/shard_map/ppermute | solution.py:733
  171.1 13.0 %mlp_forward.2 = (f32[2,288,768]{2,1,0:T(8,128)}, bf16[2,288,768]{2,1,0:T(8,128)(2,1)}, bf16[2,288,1536]{2,1,0:T(8,128)(2,1)}, bf16[2,288,1536]{2,1,0:T(8,128)(2...) custom-call(s32[16]{0:T(128)S(1)} %stack.151.refs_0_, ...), custom_call_target="tpu_custom_call" | custom-call | flops 16099999744 | tf_op jit(solution)/shard_map/mlp_forward/pallas_call | solution.py:45
  186.7 4.2 collective-permute-start.43
  196.6 6.0 collective-permute-done.33.refs_3_
  206.4 27.8 %collective-permute-done.34.refs_4_ = bf16[2,128,512]{2,1,0:T(8,128)(2,1)S(1)} collective-permute-done((bf16[2,128,512]{2,1,0:T(8,128)(2,1)S(1)}, bf16[2,128,512]{2,1,0:T(8,128)(2,1)S(1)}, u32[]{:S(2)}, u32[]{:S(2)}) %collective-permute-start.34) | collective-permute-done | bytes 262176 | tf_op jit(solution)/shard_map/ppermute | solution.py:590
  236.8 4.2 query_out.2
  241.1 5.2 collective-permute-done.31
  250.2 12.4 %attn_forward.3 = (bf16[2,288,768]{2,1,0:T(8,128)(2,1)}, bf16[2,432,1152]{2,1,0:T(8,128)(2,1)}, bf16[2,18,144,144]{3,2,1,0:T(8,128)(2,1)}, bf16[2,288,384]{2,1,0...) custom-call(s32[16]{0:T(128)S(1)} %stack.151.refs_0_, s32[8]{0:T(128)S(1)} %stack.134.refs_1_.refs_0_, ...), custom_call_target="tpu_custom_call" | custom-call | flops 11500000256 | tf_op jit(solution)/shard_map/attn_forward/pallas_call | solution.py:45
  263.5 2.9 query_in.3
  266.4 3.9 broadcast_select_fusion.refs_13_.refs_6_.refs_16_
  271.2 13.3 %mlp_forward.3 = (f32[2,288,768]{2,1,0:T(8,128)}, bf16[2,288,768]{2,1,0:T(8,128)(2,1)}, bf16[2,288,1536]{2,1,0:T(8,128)(2,1)}, bf16[2,288,1536]{2,1,0:T(8,128)(2...) custom-call(s32[16]{0:T(128)S(1)} %stack.151.refs_0_, ...), custom_call_target="tpu_custom_call" | custom-call | flops 16099999744 | tf_op jit(solution)/shard_map/mlp_forward/pallas_call | solution.py:45
  288.7 5.0 collective-permute-done.45.refs_3_
  293.7 5.3 collective-permute-done.46.refs_4_
  300.4 4.2 query_out.3
  310.8 14.2 %mlp_backward.2 = (bf16[2,288,1536]{2,1,0:T(8,128)(2,1)}, bf16[2,288,768]{2,1,0:T(8,128)(2,1)}, bf16[2,128,384]{2,1,0:T(8,128)(2,1)S(1)}, bf16[2,288,768]{2,1,0:T(8,128)(2,1)}, bf16[2,128,768]{2,1,0:T(8,128)(2,1)S(1)}) custom-call(s32[16]{0:T(128)S(1)} %stack.151.refs_0_, s32[8]{0:T(128)S(1)} %stack.134.refs_1_.refs_0_, ...), custom_call_target="tpu_custom_call" | custom-call | flops 16099999744 | tf_op jit(solution)/shard_map/mlp_backward/pallas_call | solution.py:45
  325.9 11.5 %early_grads.2 = (bf16[4,48,4224]{2,1,0:T(8,128)(2,1)}, bf16[4,48,4224]{2,1,0:T(8,128)(2,1)}, bf16[4,48,4224]{2,1,0:T(8,128)(2,1)}, bf16[2,48,4224]{2,1,0:T(8,128)(2,1)S(1)}, bf16[2,48,4224]{2,1,0:T(8,128)(2,1)}) custom-call(s32[16]{0:T(128)S(1)} %stack.151.refs_0_, s32[8]{0:T(128)S(1)} %stack.134.refs_1_.refs_0_, bf16[576,768]{1,0:T(8,128)(2,1)} %bitcast.272, ...), custom_call_target="tpu_custom_call" | custom-call | flops 13799999488 | tf_op jit(solution)/shard_map/early_grads/pallas_call | solution.py:45
  338.4 5.7 first_backward.2
  344.1 3.0 collective-permute-start.50
  348.5 3.9 collective-permute-start.54
  354.8 17.8 %attn_backward.2 = (bf16[2,288,1152]{2,1,0:T(8,128)(2,1)}, bf16[2,288,768]{2,1,0:T(8,128)(2,1)}) custom-call(s32[16]{0:T(128)S(1)} %stack.151.refs_0_, bf16[2,432,384]{2,1,0:T(8,128)(2,1)S(1)} %pad_maximum_fusion.20.refs_1_, bf16[2,432,1152]{2,1,0:T(8,128)(2,1)} %get-tuple-element.244.refs_2_, bf16[2,18,144,144]{3,2,1,0:T(8,128)(2,1)} %get-tuple-element.245.refs_3_, ...), custom_call_target="tpu_custom_call" | custom-call | flops 17250000896 | tf_op jit(solution)/shard_map/attn_backward/pallas_call | solution.py:45
  376.2 2.4 slice_add_fusion.3
  383.8 2.9 input_backward.2
  387.7 14.4 %mlp_backward.3 = (bf16[2,288,1536]{2,1,0:T(8,128)(2,1)}, bf16[2,288,768]{2,1,0:T(8,128)(2,1)}, bf16[2,128,384]{2,1,0:T(8,128)(2,1)S(1)}, bf16[2,288,768]{2,1,0:T(8,128)(2,1)}, bf16[2,128,768]{2,1,0:T(8,128)(2,1)S(1)}) custom-call(s32[16]{0:T(128)S(1)} %stack.151.refs_0_, s32[8]{0:T(128)S(1)} %stack.134.refs_1_.refs_0_, bf16[2,288,768]{2,1,0:T(8,128)(2,1)} %copy-done.14, ...), custom_call_target="tpu_custom_call" | custom-call | flops 16099999744 | tf_op jit(solution)/shard_map/mlp_backward/pallas_call | solution.py:45
  402.6 11.6 %early_grads.3 = (bf16[4,48,4224]{2,1,0:T(8,128)(2,1)}, bf16[4,48,4224]{2,1,0:T(8,128)(2,1)}, bf16[4,48,4224]{2,1,0:T(8,128)(2,1)}, bf16[2,48,4224]{2,1,0:T(8,128)(2,1)S(1)}, bf16[2,48,4224]{2,1,0:T(8,128)(2,1)}) custom-call(s32[16]{0:T(128)S(1)} %stack.151.refs_0_, s32[8]{0:T(128)S(1)} %stack.134.refs_1_.refs_0_, bf16[576,768]{1,0:T(8,128)(2,1)} %bitcast.269, ...), custom_call_target="tpu_custom_call" | custom-call | flops 13799999488 | tf_op jit(solution)/shard_map/early_grads/pallas_call | solution.py:45
  414.8 8.3 %collective-permute-done.58 = bf16[2,128,384]{2,1,0:T(8,128)(2,1)S(1)} collective-permute-done((bf16[2,128,384]{2,1,0:T(8,128)(2,1)S(1)}, bf16[2,128,384]{2,1,0:T(8,128)(2,1)S(1)}, u32[]{:S(2)}, u32[]{:S(2)}) %collective-permute-start.58) | collective-permute-done | bytes 196640 | tf_op jit(solution)/shard_map/ppermute | solution.py:590
  427.0 2.9 convert_add_fusion.1
  434.4 4.4 collective-permute-start.65
  438.8 5.6 first_backward.3
  444.4 13.2 %attn_backward.3 = (bf16[2,288,1152]{2,1,0:T(8,128)(2,1)}, bf16[2,288,768]{2,1,0:T(8,128)(2,1)}) custom-call(s32[16]{0:T(128)S(1)} %stack.151.refs_0_, bf16[2,288,384]{2,1,0:T(8,128)(2,1)S(1)} %get-tuple-element.269.refs_1_, bf16[2,288,1152]{2,1,0:T(8,128)(2,1)} %get-tuple-element.270.refs_2_, bf16[2,12,144,144]{3,2,1,0:T(8,128)(2,1)} %get-tuple-element.271.refs_3_, ...), custom_call_target="tpu_custom_call" | custom-call | flops 17250000896 | tf_op jit(solution)/shard_map/attn_backward/pallas_call | solution.py:45
  460.5 2.3 slice_add_fusion.1
  469.8 2.4 collective-permute-done.65
  472.2 3.1 input_backward.3
  476.4 11.0 %late_grads.1 = (bf16[4,48,3968]{2,1,0:T(8,128)(2,1)}, bf16[4,48,3968]{2,1,0:T(8,128)(2,1)}, bf16[4,48,3968]{2,1,0:T(8,128)(2,1)}, bf16[2,48,3968]{2,1,0:T(8,128)(2,1)}, bf16[2,48,3968]{2,1,0:T(8,128)(2,1)}) custom-call(s32[16]{0:T(128)S(1)} %stack.151.refs_0_, s32[8]{0:T(128)S(1)} %stack.134.refs_1_.refs_0_, bf16[576,768]{1,0:T(8,128)(2,1)} %bitcast.268, ...), custom_call_target="tpu_custom_call" | custom-call | flops 6899999744 | tf_op jit(solution)/shard_map/late_grads/pallas_call | solution.py:45
  490.8 10.2 %collective-permute-start.83 = (bf16[1,2,48,1920]{3,2,1,0:T(8,128)(2,1)S(1)}, bf16[1,2,48,1920]{3,2,1,0:T(8,128)(2,1)S(1)}, u32[]{:S(2)}, u32[]{:S(2)}) collective-permute-start(bf16[1,2,48,1920]{3,2,1,0:T(8,128)(2,1)S(1)} %fusion.7), channel_id=1, source_target_pairs={{4,0},{0,4},{28,24},{24,28},{5,1},{1,5},{29,25},{25,29},{6,2},{2,6... | collective-permute-start | bytes 1105928 | tf_op jit(solution)/shard_map/ppermute | solution.py:972
  504.3 4.6 collective-permute-done.83
  511.0 7.1 %collective-permute-done.67 = bf16[2,48,3968]{2,1,0:T(8,128)(2,1)S(1)} collective-permute-done((bf16[2,48,3968]{2,1,0:T(8,128)(2,1)}, bf16[2,48,3968]{2,1,0:T(8,128)(2,1)S(1)}, u32[]{:S(2)}, u32[]{:S(2)}) %collective-permute-start.67) | collective-permute-done | bytes 761888 | tf_op jit(solution)/shard_map/ppermute | solution.py:590
  518.0 2.8 collective-permute-done.68
  523.9 2.4 convert_add_fusion
  527.9 3.6 collective-permute-start.75
  531.7 34.7 %collective-permute-done.75 = bf16[2,48,2304]{2,1,0:T(8,128)(2,1)S(1)} collective-permute-done((bf16[2,48,2304]{2,1,0:T(8,128)(2,1)S(1)}, bf16[2,48,2304]{2,1,0:T(8,128)(2,1)S(1)}, u32[]{:S(2)}, u32[]{:S(2)}) %collective-permute-start.75) | collective-permute-done | bytes 442400 | tf_op jit(solution)/shard_map/ppermute | solution.py:954
  570.1 2.9 collective-permute-start.80
  574.9 7.0 %collective-permute-done.80 = bf16[1,2,48,1920]{3,2,1,0:T(8,128)(2,1)S(1)} collective-permute-done((bf16[1,2,48,1920]{3,2,1,0:T(8,128)(2,1)S(1)}, bf16[1,2,48,1920]{3,2,1,0:T(8,128)(2,1)S(1)}, u32[]{:S(2)}, u32[]{:S(2)}) %collective-permute-start.80) | collective-permute-done | bytes 368672 | tf_op jit(solution)/shard_map/ppermute | solution.py:972
  584.2 22.4 %collective-permute-done.78 = bf16[4,48,768]{2,1,0:T(8,128)(2,1)S(1)} collective-permute-done((bf16[4,48,768]{2,1,0:T(8,128)(2,1)S(1)}, bf16[4,48,768]{2,1,0:T(8,128)(2,1)S(1)}, u32[]{:S(2)}, u32[]{:S(2)}) %collective-permute-start.78) | collective-permute-done | bytes 294944 | tf_op jit(solution)/shard_map/ppermute | solution.py:956
  607.0 3.9 collective-permute-start.87
  611.8 3.9 collective-permute-done.87
  (490 shorter events, 148.1 us)
Async XLA Ops:
  18.0 21.8 %collective-permute-start.12 = (bf16[2,48,1920]{2,1,0:T(8,128)(2,1)S(1)}, bf16[2,48,1920]{2,1,0:T(8,128)(2,1)S(1)}, u32[]{:S(2)}, u32[]{:S(2)}) collective-permute-start(bf16[2,48,1920]{2,1,0:T(8,128)(2,1)S(1)} %pad_maximum_fusion.23), channel_id=1, source_target_pairs={{0,16},{16,0},{1,17},{17,1},{2,18},{18,2},{3,19},{19,3},{4,20},{20... | collective-permute-start | bytes 1105928 | tf_op jit(solution)/shard_map/ppermute | solution.py:587
  23.6 17.8 %collective-permute-start.4 = (bf16[2,48,1664]{2,1,0:T(8,128)(2,1)S(1)}, bf16[2,48,1664]{2,1,0:T(8,128)(2,1)S(1)}, u32[]{:S(2)}, u32[]{:S(2)}) collective-permute-start(bf16[2,48,1664]{2,1,0:T(8,128)(2,1)S(1)} %pad_maximum_fusion.24), channel_id=1, source_target_pairs={{0,8},{4,12},{8,0},{12,4},{1,9},{5,13},{9,1},{13,5},{2,10},{6,14},... | collective-permute-start | bytes 958472 | tf_op jit(solution)/shard_map/ppermute | solution.py:654
  24.4 13.0 %collective-permute-start.8 = (bf16[1,48,2304]{2,1,0:T(8,128)(2,1)S(1)}, bf16[1,48,2304]{2,1,0:T(8,128)(2,1)S(1)}, u32[]{:S(2)}, u32[]{:S(2)}) collective-permute-start(bf16[1,48,2304]{2,1,0:T(8,128)(2,1)S(1)} %get-tuple-element.191), channel_id=1, source_target_pairs={{0,4},{4,0},{8,12},{12,8},{1,5},{5,1},{9,13},{13,9},{2,6},{6,2},{1... | collective-permute-start | bytes 663560 | tf_op jit(solution)/shard_map/ppermute | solution.py:654
  37.5 22.8 %collective-permute-start.9 = (bf16[2,48,2304]{2,1,0:T(8,128)(2,1)S(1)}, bf16[2,48,2304]{2,1,0:T(8,128)(2,1)S(1)}, u32[]{:S(2)}, u32[]{:S(2)}) collective-permute-start(bf16[2,48,2304]{2,1,0:T(8,128)(2,1)S(1)} %pad_maximum_fusion.21), channel_id=1, source_target_pairs={{0,8},{4,12},{8,0},{12,4},{1,9},{5,13},{9,1},{13,5},{2,10},{6,14},... | collective-permute-start | bytes 1327112 | tf_op jit(solution)/shard_map/ppermute | solution.py:654
  41.4 29.4 %collective-permute-start.10 = (bf16[4,48,2048]{2,1,0:T(8,128)(2,1)S(1)}, bf16[4,48,2048]{2,1,0:T(8,128)(2,1)S(1)}, u32[]{:S(2)}, u32[]{:S(2)}) collective-permute-start(bf16[4,48,2048]{2,1,0:T(8,128)(2,1)S(1)} %pad_maximum_fusion.17.refs_3_.refs_6_.refs_4_), channel_id=1, source_target_pairs={{0,2},{1,3},{2,0},{3,1},{4,6},{5,7},{6,4},{7,5},{8,10},{9,11},{10,... | collective-permute-start | bytes 2359304 | tf_op jit(solution)/shard_map/ppermute | solution.py:590
  43.0 27.8 %collective-permute-start.6 = (bf16[4,48,2048]{2,1,0:T(8,128)(2,1)S(1)}, bf16[4,48,2048]{2,1,0:T(8,128)(2,1)S(1)}, u32[]{:S(2)}, u32[]{:S(2)}) collective-permute-start(bf16[4,48,2048]{2,1,0:T(8,128)(2,1)S(1)} %pad_maximum_fusion.17.refs_3_.refs_6_.refs_4_), channel_id=1, source_target_pairs={{0,1},{1,0},{2,3},{3,2},{4,5},{5,4},{6,7},{7,6},{8,9},{9,8},{10,11... | collective-permute-start | bytes 2359304 | tf_op jit(solution)/shard_map/ppermute | solution.py:590
  70.8 13.2 %collective-permute-start.14 = (bf16[2,2,48,1920]{3,2,1,0:T(8,128)(2,1)}, bf16[2,2,48,1920]{3,2,1,0:T(8,128)(2,1)}, u32[]{:S(2)}, u32[]{:S(2)}) collective-permute-start(bf16[2,2,48,1920]{3,2,1,0:T(8,128)(2,1)} %pad_maximum_fusion.19), channel_id=1, source_target_pairs={{0,8},{4,12},{24,16},{28,20},{1,9},{5,13},{25,17},{29,21},{2,10},{... | collective-permute-start | bytes 2211848 | tf_op jit(solution)/shard_map/ppermute | solution.py:657
  74.8 32.5 %collective-permute-start.11 = (bf16[4,48,3328]{2,1,0:T(8,128)(2,1)}, bf16[4,48,3328]{2,1,0:T(8,128)(2,1)}, u32[]{:S(2)}, u32[]{:S(2)}) collective-permute-start(bf16[4,48,3328]{2,1,0:T(8,128)(2,1)} %get-tuple-element.433), channel_id=1, source_target_pairs={{0,2},{1,3},{2,0},{3,1},{4,6},{5,7},{6,4},{7,5},{8,10},{9,11},{10,... | collective-permute-start | bytes 3833864 | tf_op jit(solution)/shard_map/ppermute | solution.py:590
  76.4 35.9 %collective-permute-start.15 = (bf16[4,48,3328]{2,1,0:T(8,128)(2,1)}, bf16[4,48,3328]{2,1,0:T(8,128)(2,1)}, u32[]{:S(2)}, u32[]{:S(2)}) collective-permute-start(bf16[4,48,3328]{2,1,0:T(8,128)(2,1)} %get-tuple-element.434), channel_id=1, source_target_pairs={{0,1},{1,0},{2,3},{3,2},{4,5},{5,4},{6,7},{7,6},{8,9},{9,8},{10,11... | collective-permute-start | bytes 3833864 | tf_op jit(solution)/shard_map/ppermute | solution.py:590
  82.9 35.8 %collective-permute-start.39 = (bf16[2,48,1920]{2,1,0:T(8,128)(2,1)S(1)}, bf16[2,48,1920]{2,1,0:T(8,128)(2,1)S(1)}, u32[]{:S(2)}, u32[]{:S(2)}) collective-permute-start(bf16[2,48,1920]{2,1,0:T(8,128)(2,1)S(1)} %get-tuple-element.455), channel_id=1, source_target_pairs={{0,1},{1,0},{2,3},{3,2},{4,5},{5,4},{6,7},{7,6},{8,9},{9,8},{10,11... | collective-permute-start | bytes 1105928 | tf_op jit(solution)/shard_map/ppermute | solution.py:590
  83.5 36.6 %collective-permute-start.40 = (bf16[2,48,1920]{2,1,0:T(8,128)(2,1)S(1)}, bf16[2,48,1920]{2,1,0:T(8,128)(2,1)S(1)}, u32[]{:S(2)}, u32[]{:S(2)}) collective-permute-start(bf16[2,48,1920]{2,1,0:T(8,128)(2,1)S(1)} %get-tuple-element.455), channel_id=1, source_target_pairs={{0,2},{1,3},{2,0},{3,1},{4,6},{5,7},{6,4},{7,5},{8,10},{9,11},{10,... | collective-permute-start | bytes 1105928 | tf_op jit(solution)/shard_map/ppermute | solution.py:590
  84.0 11.0 %collective-permute-start.18 = (bf16[1,2,48,384]{3,2,1,0:T(8,128)(2,1)S(1)}, bf16[1,2,48,384]{3,2,1,0:T(8,128)(2,1)S(1)}, u32[]{:S(2)}, u32[]{:S(2)}) collective-permute-start(bf16[1,2,48,384]{3,2,1,0:T(8,128)(2,1)S(1)} %get-tuple-element.199), channel_id=1, source_target_pairs={{0,4},{4,0},{24,28},{28,24},{1,5},{5,1},{25,29},{29,25},{2,6},{6,2... | collective-permute-start | bytes 221192 | tf_op jit(solution)/shard_map/ppermute | solution.py:657
  95.0 28.3 %collective-permute-start.41 = (bf16[2,48,1920]{2,1,0:T(8,128)(2,1)S(1)}, bf16[2,48,1920]{2,1,0:T(8,128)(2,1)S(1)}, u32[]{:S(2)}, u32[]{:S(2)}) collective-permute-start(bf16[2,48,1920]{2,1,0:T(8,128)(2,1)S(1)} %get-tuple-element.455), channel_id=1, source_target_pairs={{0,3},{1,2},{2,1},{3,0},{4,7},{5,6},{6,5},{7,4},{8,11},{9,10},{10,... | collective-permute-start | bytes 1105928 | tf_op jit(solution)/shard_map/ppermute | solution.py:590
  107.3 11.3 %collective-permute-start.17 = (bf16[1,48,1664]{2,1,0:T(8,128)(2,1)S(1)}, bf16[1,48,1664]{2,1,0:T(8,128)(2,1)S(1)}, u32[]{:S(2)}, u32[]{:S(2)}) collective-permute-start(bf16[1,48,1664]{2,1,0:T(8,128)(2,1)S(1)} %copy-done.44), channel_id=1, source_target_pairs={{0,4},{4,0},{8,12},{12,8},{1,5},{5,1},{9,13},{13,9},{2,6},{6,2},{1... | collective-permute-start | bytes 479240 | tf_op jit(solution)/shard_map/ppermute | solution.py:654
  114.7 23.8 %collective-permute-start.16 = (bf16[4,48,3072]{2,1,0:T(8,128)(2,1)S(1)}, bf16[4,48,3072]{2,1,0:T(8,128)(2,1)S(1)}, u32[]{:S(2)}, u32[]{:S(2)}) collective-permute-start(bf16[4,48,3072]{2,1,0:T(8,128)(2,1)S(1)} %get-tuple-element.458), channel_id=1, source_target_pairs={{0,1},{1,0},{2,3},{3,2},{4,5},{5,4},{6,7},{7,6},{8,9},{9,8},{10,11... | collective-permute-start | bytes 3538952 | tf_op jit(solution)/shard_map/ppermute | solution.py:590
  118.6 19.8 %collective-permute-start.21 = (bf16[4,48,3072]{2,1,0:T(8,128)(2,1)S(1)}, bf16[4,48,3072]{2,1,0:T(8,128)(2,1)S(1)}, u32[]{:S(2)}, u32[]{:S(2)}) collective-permute-start(bf16[4,48,3072]{2,1,0:T(8,128)(2,1)S(1)} %get-tuple-element.457), channel_id=1, source_target_pairs={{0,2},{1,3},{2,0},{3,1},{4,6},{5,7},{6,4},{7,5},{8,10},{9,11},{10,... | collective-permute-start | bytes 3538952 | tf_op jit(solution)/shard_map/ppermute | solution.py:590
  120.2 11.4 %collective-permute-start.19 = (bf16[2,48,1664]{2,1,0:T(8,128)(2,1)S(1)}, bf16[2,48,1664]{2,1,0:T(8,128)(2,1)S(1)}, u32[]{:S(2)}, u32[]{:S(2)}) collective-permute-start(bf16[2,48,1664]{2,1,0:T(8,128)(2,1)S(1)} %pad_maximum_fusion.25), channel_id=1, source_target_pairs={{0,8},{4,12},{8,0},{12,4},{1,9},{5,13},{9,1},{13,5},{2,10},{6,14},... | collective-permute-start | bytes 958472 | tf_op jit(solution)/shard_map/ppermute | solution.py:654
  138.5 18.1 %collective-permute-start.24 = (bf16[2,48,2304]{2,1,0:T(8,128)(2,1)S(1)}, bf16[2,48,2304]{2,1,0:T(8,128)(2,1)S(1)}, u32[]{:S(2)}, u32[]{:S(2)}) collective-permute-start(bf16[2,48,2304]{2,1,0:T(8,128)(2,1)S(1)} %pad_maximum_fusion.22), channel_id=1, source_target_pairs={{0,8},{4,12},{8,0},{12,4},{1,9},{5,13},{9,1},{13,5},{2,10},{6,14},... | collective-permute-start | bytes 1327112 | tf_op jit(solution)/shard_map/ppermute | solution.py:654
  139.9 26.1 %collective-permute-start.22 = (bf16[4,48,2944]{2,1,0:T(8,128)(2,1)S(1)}, bf16[4,48,2944]{2,1,0:T(8,128)(2,1)}, u32[]{:S(2)}, u32[]{:S(2)}) collective-permute-start(bf16[4,48,2944]{2,1,0:T(8,128)(2,1)S(1)} %pad_maximum_fusion.14), channel_id=1, source_target_pairs={{0,2},{1,3},{2,0},{3,1},{4,6},{5,7},{6,4},{7,5},{8,10},{9,11},{10,... | collective-permute-start | bytes 3391496 | tf_op jit(solution)/shard_map/ppermute | solution.py:590
  144.7 22.6 %collective-permute-start.25 = (bf16[4,48,3072]{2,1,0:T(8,128)(2,1)S(1)}, bf16[4,48,3072]{2,1,0:T(8,128)(2,1)}, u32[]{:S(2)}, u32[]{:S(2)}) collective-permute-start(bf16[4,48,3072]{2,1,0:T(8,128)(2,1)S(1)} %pad_maximum_fusion.13), channel_id=1, source_target_pairs={{0,1},{1,0},{2,3},{3,2},{4,5},{5,4},{6,7},{7,6},{8,9},{9,8},{10,11... | collective-permute-start | bytes 3538952 | tf_op jit(solution)/shard_map/ppermute | solution.py:590
  154.3 16.8 %collective-permute-start.26 = (bf16[2,288,768]{2,1,0:T(8,128)(2,1)}, bf16[2,288,768]{2,1,0:T(8,128)(2,1)}, u32[]{:S(2)}, u32[]{:S(2)}) collective-permute-start(bf16[2,288,768]{2,1,0:T(8,128)(2,1)} %get-tuple-element.208.refs_3_), channel_id=1, source_target_pairs={{0,16},{16,0},{1,17},{17,1},{2,18},{18,2},{3,19},{19,3},{4,20},{20... | collective-permute-start | bytes 2654216 | tf_op jit(solution)/shard_map/ppermute | solution.py:587
  156.6 28.9 %collective-permute-start.42 = (bf16[1,4,2,48,1920]{4,3,2,1,0:T(8,128)(2,1)S(1)}, bf16[1,4,2,48,1920]{4,3,2,1,0:T(8,128)(2,1)S(1)}, u32[]{:S(2)}, u32[]{:S(2)}) collective-permute-start(bf16[1,4,2,48,1920]{4,3,2,1,0:T(8,128)(2,1)S(1)} %maximum_bitcast_fusion), channel_id=1, source_target_pairs={{0,4},{4,0},{24,28},{28,24},{1,5},{5,1},{25,29},{29,25},{2,6},{6,2... | collective-permute-start | bytes 4423688 | tf_op jit(solution)/shard_map/ppermute | solution.py:733
  184.1 19.5 %collective-permute-start.27 = (bf16[2,288,768]{2,1,0:T(8,128)(2,1)}, bf16[2,288,768]{2,1,0:T(8,128)(2,1)}, u32[]{:S(2)}, u32[]{:S(2)}) collective-permute-start(bf16[2,288,768]{2,1,0:T(8,128)(2,1)} %get-tuple-element.212), channel_id=1, source_target_pairs={{0,16},{16,0},{1,17},{17,1},{2,18},{18,2},{3,19},{19,3},{4,20},{20... | collective-permute-start | bytes 2654216 | tf_op jit(solution)/shard_map/ppermute | solution.py:587
  186.7 79.7 %collective-permute-start.43 = (bf16[2,4,2,48,1920]{4,3,2,1,0:T(8,128)(2,1)}, bf16[2,4,2,48,1920]{4,3,2,1,0:T(8,128)(2,1)}, u32[]{:S(2)}, u32[]{:S(2)}) collective-permute-start(bf16[2,4,2,48,1920]{4,3,2,1,0:T(8,128)(2,1)} %constant_dynamic-update-slice_fusion.20), channel_id=1, source_target_pairs={{0,8},{4,12},{24,16},{28,20},{1,9},{5,13},{25,17},{29,21},{2,10},{... | collective-permute-start | bytes 8847368 | tf_op jit(solution)/shard_map/ppermute | solution.py:733
  194.0 55.0 %collective-permute-start.28 = (bf16[4,48,3328]{2,1,0:T(8,128)(2,1)}, bf16[4,48,3328]{2,1,0:T(8,128)(2,1)S(1)}, u32[]{:S(2)}, u32[]{:S(2)}) collective-permute-start(bf16[4,48,3328]{2,1,0:T(8,128)(2,1)} %get-tuple-element.431), channel_id=1, source_target_pairs={{0,2},{1,3},{2,0},{3,1},{4,6},{5,7},{6,4},{7,5},{8,10},{9,11},{10,... | collective-permute-start | bytes 3833864 | tf_op jit(solution)/shard_map/ppermute | solution.py:590
  195.0 52.4 %collective-permute-start.29 = (bf16[4,48,3328]{2,1,0:T(8,128)(2,1)}, bf16[4,48,3328]{2,1,0:T(8,128)(2,1)S(1)}, u32[]{:S(2)}, u32[]{:S(2)}) collective-permute-start(bf16[4,48,3328]{2,1,0:T(8,128)(2,1)} %get-tuple-element.432), channel_id=1, source_target_pairs={{0,1},{1,0},{2,3},{3,2},{4,5},{5,4},{6,7},{7,6},{8,9},{9,8},{10,11... | collective-permute-start | bytes 3833864 | tf_op jit(solution)/shard_map/ppermute | solution.py:590
  202.6 31.6 %collective-permute-start.34 = (bf16[2,128,512]{2,1,0:T(8,128)(2,1)S(1)}, bf16[2,128,512]{2,1,0:T(8,128)(2,1)S(1)}, u32[]{:S(2)}, u32[]{:S(2)}) collective-permute-start(bf16[2,128,512]{2,1,0:T(8,128)(2,1)S(1)} %get-tuple-element.217.refs_2_), channel_id=1, source_target_pairs={{0,2},{1,3},{2,0},{3,1},{4,6},{5,7},{6,4},{7,5},{8,10},{9,11},{10,... | collective-permute-start | bytes 786440 | tf_op jit(solution)/shard_map/ppermute | solution.py:590
  203.6 31.9 %collective-permute-start.35 = (bf16[2,128,512]{2,1,0:T(8,128)(2,1)S(1)}, bf16[2,128,512]{2,1,0:T(8,128)(2,1)S(1)}, u32[]{:S(2)}, u32[]{:S(2)}) collective-permute-start(bf16[2,128,512]{2,1,0:T(8,128)(2,1)S(1)} %get-tuple-element.217.refs_2_), channel_id=1, source_target_pairs={{0,3},{1,2},{2,1},{3,0},{4,7},{5,6},{6,5},{7,4},{8,11},{9,10},{10,... | collective-permute-start | bytes 786440 | tf_op jit(solution)/shard_map/ppermute | solution.py:590
  241.0 21.7 %collective-permute-start.36 = (bf16[2,128,768]{2,1,0:T(8,128)(2,1)}, bf16[2,128,768]{2,1,0:T(8,128)(2,1)S(1)}, u32[]{:S(2)}, u32[]{:S(2)}) collective-permute-start(bf16[2,128,768]{2,1,0:T(8,128)(2,1)} %get-tuple-element.218.refs_3_), channel_id=1, source_target_pairs={{0,16},{16,0},{1,17},{17,1},{2,18},{18,2},{3,19},{19,3},{4,20},{20... | collective-permute-start | bytes 1179656 | tf_op jit(solution)/shard_map/ppermute | solution.py:587
  247.5 22.8 %collective-permute-start.37 = (bf16[4,48,1152]{2,1,0:T(8,128)(2,1)S(1)}, bf16[4,48,1152]{2,1,0:T(8,128)(2,1)S(1)}, u32[]{:S(2)}, u32[]{:S(2)}) collective-permute-start(bf16[4,48,1152]{2,1,0:T(8,128)(2,1)S(1)} %slice.616), channel_id=1, source_target_pairs={{0,2},{1,3},{2,0},{3,1},{4,6},{5,7},{6,4},{7,5},{8,10},{9,11},{10,... | collective-permute-start | bytes 1327112 | tf_op jit(solution)/shard_map/ppermute | solution.py:590
  249.0 21.2 %collective-permute-start.38 = (bf16[4,48,1152]{2,1,0:T(8,128)(2,1)S(1)}, bf16[4,48,1152]{2,1,0:T(8,128)(2,1)S(1)}, u32[]{:S(2)}, u32[]{:S(2)}) collective-permute-start(bf16[4,48,1152]{2,1,0:T(8,128)(2,1)S(1)} %slice.615), channel_id=1, source_target_pairs={{0,1},{1,0},{2,3},{3,2},{4,5},{5,4},{6,7},{7,6},{8,9},{9,8},{10,11... | collective-permute-start | bytes 1327112 | tf_op jit(solution)/shard_map/ppermute | solution.py:590
  285.8 13.3 %collective-permute-start.46 = (bf16[2,128,512]{2,1,0:T(8,128)(2,1)S(1)}, bf16[2,128,512]{2,1,0:T(8,128)(2,1)S(1)}, u32[]{:S(2)}, u32[]{:S(2)}) collective-permute-start(bf16[2,128,512]{2,1,0:T(8,128)(2,1)S(1)} %get-tuple-element.226.refs_2_), channel_id=1, source_target_pairs={{0,2},{1,3},{2,0},{3,1},{4,6},{5,7},{6,4},{7,5},{8,10},{9,11},{10,... | collective-permute-start | bytes 786440 | tf_op jit(solution)/shard_map/ppermute | solution.py:590
  287.5 12.9 %collective-permute-start.47 = (bf16[2,128,512]{2,1,0:T(8,128)(2,1)S(1)}, bf16[2,128,512]{2,1,0:T(8,128)(2,1)S(1)}, u32[]{:S(2)}, u32[]{:S(2)}) collective-permute-start(bf16[2,128,512]{2,1,0:T(8,128)(2,1)S(1)} %get-tuple-element.226.refs_2_), channel_id=1, source_target_pairs={{0,3},{1,2},{2,1},{3,0},{4,7},{5,6},{6,5},{7,4},{8,11},{9,10},{10,... | collective-permute-start | bytes 786440 | tf_op jit(solution)/shard_map/ppermute | solution.py:590
  288.7 19.8 %collective-permute-start.44 = (bf16[2,288,768]{2,1,0:T(8,128)(2,1)}, bf16[2,288,768]{2,1,0:T(8,128)(2,1)S(1)}, u32[]{:S(2)}, u32[]{:S(2)}) collective-permute-start(bf16[2,288,768]{2,1,0:T(8,128)(2,1)} %get-tuple-element.222), channel_id=1, source_target_pairs={{0,16},{16,0},{1,17},{17,1},{2,18},{18,2},{3,19},{19,3},{4,20},{20... | collective-permute-start | bytes 2654216 | tf_op jit(solution)/shard_map/ppermute | solution.py:587
  325.0 12.5 %collective-permute-start.53 = (bf16[2,128,384]{2,1,0:T(8,128)(2,1)S(1)}, bf16[2,128,384]{2,1,0:T(8,128)(2,1)S(1)}, u32[]{:S(2)}, u32[]{:S(2)}) collective-permute-start(bf16[2,128,384]{2,1,0:T(8,128)(2,1)S(1)} %get-tuple-element.251), channel_id=1, source_target_pairs={{0,1},{1,0},{2,3},{3,2},{4,5},{5,4},{6,7},{7,6},{8,9},{9,8},{10,11... | collective-permute-start | bytes 589832 | tf_op jit(solution)/shard_map/ppermute | solution.py:590
  325.9 11.6 %collective-permute-start.49 = (bf16[2,288,768]{2,1,0:T(8,128)(2,1)}, bf16[2,288,768]{2,1,0:T(8,128)(2,1)S(1)}, u32[]{:S(2)}, u32[]{:S(2)}) collective-permute-start(bf16[2,288,768]{2,1,0:T(8,128)(2,1)} %get-tuple-element.241.refs_2_), channel_id=1, source_target_pairs={{0,16},{16,0},{1,17},{17,1},{2,18},{18,2},{3,19},{19,3},{4,20},{20... | collective-permute-start | bytes 2654216 | tf_op jit(solution)/shard_map/ppermute | solution.py:587
  348.5 24.0 %collective-permute-start.54 = (bf16[2,128,384]{2,1,0:T(8,128)(2,1)S(1)}, bf16[2,128,384]{2,1,0:T(8,128)(2,1)S(1)}, u32[]{:S(2)}, u32[]{:S(2)}) collective-permute-start(bf16[2,128,384]{2,1,0:T(8,128)(2,1)S(1)} %add_convert_fusion.4.refs_1_), channel_id=1, source_target_pairs={{0,2},{1,3},{2,0},{3,1},{4,6},{5,7},{6,4},{7,5},{8,10},{9,11},{10,... | collective-permute-start | bytes 589832 | tf_op jit(solution)/shard_map/ppermute | solution.py:590
  352.4 22.9 %collective-permute-start.61 = (bf16[2,48,4224]{2,1,0:T(8,128)(2,1)S(1)}, bf16[2,48,4224]{2,1,0:T(8,128)(2,1)S(1)}, u32[]{:S(2)}, u32[]{:S(2)}) collective-permute-start(bf16[2,48,4224]{2,1,0:T(8,128)(2,1)S(1)} %get-tuple-element.294), channel_id=1, source_target_pairs={{0,2},{1,3},{2,0},{3,1},{4,6},{5,7},{6,4},{7,5},{8,10},{9,11},{10,... | collective-permute-start | bytes 2433032 | tf_op jit(solution)/shard_map/ppermute | solution.py:590
  352.5 22.8 %collective-permute-start.62 = (bf16[2,48,4224]{2,1,0:T(8,128)(2,1)S(1)}, bf16[2,48,4224]{2,1,0:T(8,128)(2,1)S(1)}, u32[]{:S(2)}, u32[]{:S(2)}) collective-permute-start(bf16[2,48,4224]{2,1,0:T(8,128)(2,1)S(1)} %copy-done.70), channel_id=1, source_target_pairs={{0,1},{1,0},{2,3},{3,2},{4,5},{5,4},{6,7},{7,6},{8,9},{9,8},{10,11... | collective-permute-start | bytes 2433032 | tf_op jit(solution)/shard_map/ppermute | solution.py:590
  379.9 45.3 %collective-permute-start.64 = (bf16[4,48,4224]{2,1,0:T(8,128)(2,1)}, bf16[4,48,4224]{2,1,0:T(8,128)(2,1)}, u32[]{:S(2)}, u32[]{:S(2)}) collective-permute-start(bf16[4,48,4224]{2,1,0:T(8,128)(2,1)} %pad_maximum_fusion.1), channel_id=1, source_target_pairs={{0,2},{1,3},{2,0},{3,1},{4,6},{5,7},{6,4},{7,5},{8,10},{9,11},{10,... | collective-permute-start | bytes 4866056 | tf_op jit(solution)/shard_map/ppermute | solution.py:590
  381.4 45.6 %collective-permute-start.63 = (bf16[4,48,4224]{2,1,0:T(8,128)(2,1)S(1)}, bf16[4,48,4224]{2,1,0:T(8,128)(2,1)}, u32[]{:S(2)}, u32[]{:S(2)}) collective-permute-start(bf16[4,48,4224]{2,1,0:T(8,128)(2,1)S(1)} %pad_maximum_fusion), channel_id=1, source_target_pairs={{0,1},{1,0},{2,3},{3,2},{4,5},{5,4},{6,7},{7,6},{8,9},{9,8},{10,11... | collective-permute-start | bytes 4866056 | tf_op jit(solution)/shard_map/ppermute | solution.py:590
  402.2 20.9 %collective-permute-start.58 = (bf16[2,128,384]{2,1,0:T(8,128)(2,1)S(1)}, bf16[2,128,384]{2,1,0:T(8,128)(2,1)S(1)}, u32[]{:S(2)}, u32[]{:S(2)}) collective-permute-start(bf16[2,128,384]{2,1,0:T(8,128)(2,1)S(1)} %get-tuple-element.274), channel_id=1, source_target_pairs={{0,1},{1,0},{2,3},{3,2},{4,5},{5,4},{6,7},{7,6},{8,9},{9,8},{10,11... | collective-permute-start | bytes 589832 | tf_op jit(solution)/shard_map/ppermute | solution.py:590
  402.6 31.8 %collective-permute-start.56 = (bf16[2,288,768]{2,1,0:T(8,128)(2,1)}, bf16[2,288,768]{2,1,0:T(8,128)(2,1)S(1)}, u32[]{:S(2)}, u32[]{:S(2)}) collective-permute-start(bf16[2,288,768]{2,1,0:T(8,128)(2,1)} %get-tuple-element.267.refs_2_), channel_id=1, source_target_pairs={{0,16},{16,0},{1,17},{17,1},{2,18},{18,2},{3,19},{19,3},{4,20},{20... | collective-permute-start | bytes 2654216 | tf_op jit(solution)/shard_map/ppermute | solution.py:587
  423.1 34.6 %collective-permute-start.59 = (bf16[2,128,384]{2,1,0:T(8,128)(2,1)S(1)}, bf16[2,128,384]{2,1,0:T(8,128)(2,1)S(1)}, u32[]{:S(2)}, u32[]{:S(2)}) collective-permute-start(bf16[2,128,384]{2,1,0:T(8,128)(2,1)S(1)} %add_convert_fusion.3.refs_1_), channel_id=1, source_target_pairs={{0,2},{1,3},{2,0},{3,1},{4,6},{5,7},{6,4},{7,5},{8,10},{9,11},{10,... | collective-permute-start | bytes 589832 | tf_op jit(solution)/shard_map/ppermute | solution.py:590
  424.9 35.0 %collective-permute-start.69 = (bf16[2,48,4224]{2,1,0:T(8,128)(2,1)S(1)}, bf16[2,48,4224]{2,1,0:T(8,128)(2,1)}, u32[]{:S(2)}, u32[]{:S(2)}) collective-permute-start(bf16[2,48,4224]{2,1,0:T(8,128)(2,1)S(1)} %get-tuple-element.333), channel_id=1, source_target_pairs={{0,2},{1,3},{2,0},{3,1},{4,6},{5,7},{6,4},{7,5},{8,10},{9,11},{10,... | collective-permute-start | bytes 2433032 | tf_op jit(solution)/shard_map/ppermute | solution.py:590
  425.2 35.3 %collective-permute-start.70 = (bf16[2,48,4224]{2,1,0:T(8,128)(2,1)}, bf16[2,48,4224]{2,1,0:T(8,128)(2,1)}, u32[]{:S(2)}, u32[]{:S(2)}) collective-permute-start(bf16[2,48,4224]{2,1,0:T(8,128)(2,1)} %get-tuple-element.334), channel_id=1, source_target_pairs={{0,1},{1,0},{2,3},{3,2},{4,5},{5,4},{6,7},{7,6},{8,9},{9,8},{10,11... | collective-permute-start | bytes 2433032 | tf_op jit(solution)/shard_map/ppermute | solution.py:590
  432.9 39.3 %collective-permute-start.66 = (bf16[4,48,1920]{2,1,0:T(8,128)(2,1)}, bf16[4,48,1920]{2,1,0:T(8,128)(2,1)}, u32[]{:S(2)}, u32[]{:S(2)}) collective-permute-start(bf16[4,48,1920]{2,1,0:T(8,128)(2,1)} %slice.821), channel_id=1, source_target_pairs={{8,0},{12,4},{16,24},{20,28},{9,1},{13,5},{17,25},{21,29},{10,2},{... | collective-permute-start | bytes 2211848 | tf_op jit(solution)/shard_map/ppermute | solution.py:956
  434.4 37.8 %collective-permute-start.65 = (bf16[2,48,2304]{2,1,0:T(8,128)(2,1)}, bf16[2,48,2304]{2,1,0:T(8,128)(2,1)}, u32[]{:S(2)}, u32[]{:S(2)}) collective-permute-start(bf16[2,48,2304]{2,1,0:T(8,128)(2,1)} %slice.815), channel_id=1, source_target_pairs={{0,8},{4,12},{8,0},{12,4},{1,9},{5,13},{9,1},{13,5},{2,10},{6,14},... | collective-permute-start | bytes 1327112 | tf_op jit(solution)/shard_map/ppermute | solution.py:954
  459.9 12.3 %collective-permute-start.57 = (bf16[2,288,768]{2,1,0:T(8,128)(2,1)}, bf16[2,288,768]{2,1,0:T(8,128)(2,1)}, u32[]{:S(2)}, u32[]{:S(2)}) collective-permute-start(bf16[2,288,768]{2,1,0:T(8,128)(2,1)} %get-tuple-element.272.da_ref), channel_id=1, source_target_pairs={{0,16},{16,0},{1,17},{17,1},{2,18},{18,2},{3,19},{19,3},{4,20},{20... | collective-permute-start | bytes 2654216 | tf_op jit(solution)/shard_map/ppermute | solution.py:587
  464.1 46.8 %collective-permute-start.72 = (bf16[4,48,4224]{2,1,0:T(8,128)(2,1)}, bf16[4,48,4224]{2,1,0:T(8,128)(2,1)}, u32[]{:S(2)}, u32[]{:S(2)}) collective-permute-start(bf16[4,48,4224]{2,1,0:T(8,128)(2,1)} %pad_maximum_fusion.3), channel_id=1, source_target_pairs={{0,2},{1,3},{2,0},{3,1},{4,6},{5,7},{6,4},{7,5},{8,10},{9,11},{10,... | collective-permute-start | bytes 4866056 | tf_op jit(solution)/shard_map/ppermute | solution.py:590
  467.2 43.8 %collective-permute-start.71 = (bf16[4,48,4224]{2,1,0:T(8,128)(2,1)}, bf16[4,48,4224]{2,1,0:T(8,128)(2,1)}, u32[]{:S(2)}, u32[]{:S(2)}) collective-permute-start(bf16[4,48,4224]{2,1,0:T(8,128)(2,1)} %pad_maximum_fusion.2), channel_id=1, source_target_pairs={{0,1},{1,0},{2,3},{3,2},{4,5},{5,4},{6,7},{7,6},{8,9},{9,8},{10,11... | collective-permute-start | bytes 4866056 | tf_op jit(solution)/shard_map/ppermute | solution.py:590
  487.4 30.6 %collective-permute-start.67 = (bf16[2,48,3968]{2,1,0:T(8,128)(2,1)}, bf16[2,48,3968]{2,1,0:T(8,128)(2,1)S(1)}, u32[]{:S(2)}, u32[]{:S(2)}) collective-permute-start(bf16[2,48,3968]{2,1,0:T(8,128)(2,1)} %get-tuple-element.327), channel_id=1, source_target_pairs={{0,2},{1,3},{2,0},{3,1},{4,6},{5,7},{6,4},{7,5},{8,10},{9,11},{10,... | collective-permute-start | bytes 2285576 | tf_op jit(solution)/shard_map/ppermute | solution.py:590
  488.8 32.0 %collective-permute-start.68 = (bf16[2,48,3968]{2,1,0:T(8,128)(2,1)}, bf16[2,48,3968]{2,1,0:T(8,128)(2,1)S(1)}, u32[]{:S(2)}, u32[]{:S(2)}) collective-permute-start(bf16[2,48,3968]{2,1,0:T(8,128)(2,1)} %get-tuple-element.328), channel_id=1, source_target_pairs={{0,1},{1,0},{2,3},{3,2},{4,5},{5,4},{6,7},{7,6},{8,9},{9,8},{10,11... | collective-permute-start | bytes 2285576 | tf_op jit(solution)/shard_map/ppermute | solution.py:590
  490.8 18.0 %collective-permute-start.83 = (bf16[1,2,48,1920]{3,2,1,0:T(8,128)(2,1)S(1)}, bf16[1,2,48,1920]{3,2,1,0:T(8,128)(2,1)S(1)}, u32[]{:S(2)}, u32[]{:S(2)}) collective-permute-start(bf16[1,2,48,1920]{3,2,1,0:T(8,128)(2,1)S(1)} %fusion.7), channel_id=1, source_target_pairs={{4,0},{0,4},{28,24},{24,28},{5,1},{1,5},{29,25},{25,29},{6,2},{2,6... | collective-permute-start | bytes 1105928 | tf_op jit(solution)/shard_map/ppermute | solution.py:972
  508.9 65.5 %collective-permute-start.81 = (bf16[1,48,2304]{2,1,0:T(8,128)(2,1)S(1)}, bf16[1,48,2304]{2,1,0:T(8,128)(2,1)S(1)}, u32[]{:S(2)}, u32[]{:S(2)}) collective-permute-start(bf16[1,48,2304]{2,1,0:T(8,128)(2,1)S(1)} %slice.817), channel_id=1, source_target_pairs={{0,4},{4,0},{8,12},{12,8},{1,5},{5,1},{9,13},{13,9},{2,6},{6,2},{1... | collective-permute-start | bytes 663560 | tf_op jit(solution)/shard_map/ppermute | solution.py:972
  521.2 45.3 %collective-permute-start.74 = (bf16[4,48,3968]{2,1,0:T(8,128)(2,1)S(1)}, bf16[4,48,3968]{2,1,0:T(8,128)(2,1)S(1)}, u32[]{:S(2)}, u32[]{:S(2)}) collective-permute-start(bf16[4,48,3968]{2,1,0:T(8,128)(2,1)S(1)} %pad_maximum_fusion.5), channel_id=1, source_target_pairs={{0,2},{1,3},{2,0},{3,1},{4,6},{5,7},{6,4},{7,5},{8,10},{9,11},{10,... | collective-permute-start | bytes 4571144 | tf_op jit(solution)/shard_map/ppermute | solution.py:590
  522.7 43.7 %collective-permute-start.73 = (bf16[4,48,3968]{2,1,0:T(8,128)(2,1)S(1)}, bf16[4,48,3968]{2,1,0:T(8,128)(2,1)S(1)}, u32[]{:S(2)}, u32[]{:S(2)}) collective-permute-start(bf16[4,48,3968]{2,1,0:T(8,128)(2,1)S(1)} %pad_maximum_fusion.4), channel_id=1, source_target_pairs={{0,1},{1,0},{2,3},{3,2},{4,5},{5,4},{6,7},{7,6},{8,9},{9,8},{10,11... | collective-permute-start | bytes 4571144 | tf_op jit(solution)/shard_map/ppermute | solution.py:590
  526.5 40.0 %collective-permute-start.76 = (bf16[4,48,1920]{2,1,0:T(8,128)(2,1)S(1)}, bf16[4,48,1920]{2,1,0:T(8,128)(2,1)S(1)}, u32[]{:S(2)}, u32[]{:S(2)}) collective-permute-start(bf16[4,48,1920]{2,1,0:T(8,128)(2,1)S(1)} %slice.820), channel_id=1, source_target_pairs={{8,0},{12,4},{16,24},{20,28},{9,1},{13,5},{17,25},{21,29},{10,2},{... | collective-permute-start | bytes 2211848 | tf_op jit(solution)/shard_map/ppermute | solution.py:956
  527.9 38.5 %collective-permute-start.75 = (bf16[2,48,2304]{2,1,0:T(8,128)(2,1)S(1)}, bf16[2,48,2304]{2,1,0:T(8,128)(2,1)S(1)}, u32[]{:S(2)}, u32[]{:S(2)}) collective-permute-start(bf16[2,48,2304]{2,1,0:T(8,128)(2,1)S(1)} %slice.814), channel_id=1, source_target_pairs={{0,8},{4,12},{8,0},{12,4},{1,9},{5,13},{9,1},{13,5},{2,10},{6,14},... | collective-permute-start | bytes 1327112 | tf_op jit(solution)/shard_map/ppermute | solution.py:954
  570.1 11.8 %collective-permute-start.80 = (bf16[1,2,48,1920]{3,2,1,0:T(8,128)(2,1)S(1)}, bf16[1,2,48,1920]{3,2,1,0:T(8,128)(2,1)S(1)}, u32[]{:S(2)}, u32[]{:S(2)}) collective-permute-start(bf16[1,2,48,1920]{3,2,1,0:T(8,128)(2,1)S(1)} %fusion.6), channel_id=1, source_target_pairs={{4,0},{0,4},{28,24},{24,28},{5,1},{1,5},{29,25},{25,29},{6,2},{2,6... | collective-permute-start | bytes 1105928 | tf_op jit(solution)/shard_map/ppermute | solution.py:972
  573.0 33.6 %collective-permute-start.77 = (bf16[2,48,3200]{2,1,0:T(8,128)(2,1)S(1)}, bf16[2,48,3200]{2,1,0:T(8,128)(2,1)S(1)}, u32[]{:S(2)}, u32[]{:S(2)}) collective-permute-start(bf16[2,48,3200]{2,1,0:T(8,128)(2,1)S(1)} %slice.813), channel_id=1, source_target_pairs={{0,8},{4,12},{8,0},{12,4},{1,9},{5,13},{9,1},{13,5},{2,10},{6,14},... | collective-permute-start | bytes 1843208 | tf_op jit(solution)/shard_map/ppermute | solution.py:954
  573.1 33.6 %collective-permute-start.78 = (bf16[4,48,768]{2,1,0:T(8,128)(2,1)S(1)}, bf16[4,48,768]{2,1,0:T(8,128)(2,1)S(1)}, u32[]{:S(2)}, u32[]{:S(2)}) collective-permute-start(bf16[4,48,768]{2,1,0:T(8,128)(2,1)S(1)} %slice.819), channel_id=1, source_target_pairs={{8,0},{12,4},{16,24},{20,28},{9,1},{13,5},{17,25},{21,29},{10,2},{... | collective-permute-start | bytes 884744 | tf_op jit(solution)/shard_map/ppermute | solution.py:956
  582.3 24.4 %collective-permute-start.84 = (f32[240,768]{1,0:T(8,128)S(1)}, f32[240,768]{1,0:T(8,128)S(1)}, u32[]{:S(2)}, u32[]{:S(2)}) collective-permute-start(f32[240,768]{1,0:T(8,128)S(1)} %broadcast_select_fusion.6), channel_id=1, source_target_pairs={{0,16},{16,0},{1,17},{17,1},{2,18},{18,2},{3,19},{19,3},{4,20},{20... | collective-permute-start | bytes 2211848 | tf_op jit(solution)/shard_map/ppermute | solution.py:587
  606.8 11.2 %collective-permute-start.85 = (bf16[1,48,3200]{2,1,0:T(8,128)(2,1)S(1)}, bf16[1,48,3200]{2,1,0:T(8,128)(2,1)S(1)}, u32[]{:S(2)}, u32[]{:S(2)}) collective-permute-start(bf16[1,48,3200]{2,1,0:T(8,128)(2,1)S(1)} %slice.816), channel_id=1, source_target_pairs={{0,4},{4,0},{8,12},{12,8},{1,5},{5,1},{9,13},{13,9},{2,6},{6,2},{1... | collective-permute-start | bytes 921608 | tf_op jit(solution)/shard_map/ppermute | solution.py:972
  (102 other events, 1143.5 us)
